TPU v7x, 128 devices: a whole 4x4x4 slice. The times are simulated.
128 devices in a mesh: dp: 64 (over y, x, z), mp: 2 (over core).
Axes of the slice: x: 4, y: 4, z: 4, core: 2. Of those that a mesh axis runs over, the one named last changes fastest.
Arguments:
- tokens: bfloat16 [1792, 64, 1024], P('dp', None, 'mp'), may hold values from -10.2 to 10.2, as said below
- doc_ids: int32 [1792, 64], P('dp'), may hold values from 0 to 3, never falling along the last dimension, each value on 1 to 32 neighbouring positions
- dest: int32 [1792], P('dp'), may hold values from 0 to 1791, as said below
- owner: int32 [1792, 4], P('dp'), may hold values from 0 to 63, as said below
- w_qkv: bfloat16 [1024, 3, 1024], P(None, None, 'mp'), may hold values from -0.1875 to 0.1875
- w_out: bfloat16 [1024, 1024], P('mp'), may hold values from -0.1875 to 0.1875
- gain_attn: float32 [1024], replicated, may hold values from 0.1 to 1.9
- w_up: bfloat16 [1024, 4096], P(None, 'mp'), may hold values from -0.1875 to 0.1875
- w_down: bfloat16 [4096, 1024], P('mp'), may hold values from -0.09375 to 0.09375
- gain_ffn: float32 [1024], replicated, may hold values from 0.1 to 1.9
Outputs:
- encoded: bfloat16 [1792, 64, 1024], P('dp', None, 'mp')
- index_rows: float32 [64, 192, 1024], P('dp', None, 'mp')
Inputs may be any that keep to these rules, and one draw needn't show every extreme that they name: `tokens`: values of a standard normal scale. `dest`: A permutation of the rows; slot j of an index of dp goes to slot j; at most 1 row of one index of dp go to the same index of dp, and that many do in every draw. At most 3 documents of one index of dp have the same owner, and some owner receives exactly 3 from every index.
All inputs are finite; a program needn't handle non-finite values.
Results may differ from a plain program's by a relative error of at most 0.0078.
Values may be sent and summed in bfloat16 or wider, within the bound.
No kernel may reach another device: no remote copies, remote signals or barrier semaphores. Data moves between devices by JAX's collectives and lax.ppermute only.
A program may use at most 128 MiB of HBM per device.

v0:
```python
import math

import jax
import jax.numpy as jnp
from jax import lax
from jax.sharding import PartitionSpec as P

HD = 64


def attend(flat_rows, segment_ids, qkv_weight, out_weight):
    row_count, seq_len = segment_ids.shape
    model_width = qkv_weight.shape[0]
    width = qkv_weight.shape[2]
    head_local = width // HD
    qkv = jnp.dot(
        flat_rows, qkv_weight.reshape(model_width, 3 * width), preferred_element_type=jnp.float32
    ).astype(jnp.bfloat16)
    qkv = qkv.reshape(row_count, seq_len, 3, head_local, HD)
    scores = jnp.einsum(
        "rqhd,rkhd->rhqk", qkv[:, :, 0], qkv[:, :, 1], preferred_element_type=jnp.float32
    ) / math.sqrt(HD)
    same_doc = segment_ids[:, :, None] == segment_ids[:, None, :]
    scores = jnp.where(same_doc[:, None], scores, jnp.float32(-1e30))
    row_top = jnp.max(scores, -1, keepdims=True)
    weights_exp = jnp.exp(scores - row_top)
    probs = (weights_exp / jnp.sum(weights_exp, -1, keepdims=True)).astype(jnp.bfloat16)
    context = jnp.einsum(
        "rhqk,rkhd->rqhd", probs, qkv[:, :, 2], preferred_element_type=jnp.float32
    ).astype(jnp.bfloat16)
    return jnp.dot(context.reshape(-1, width), out_weight, preferred_element_type=jnp.float32)


def pool_docs(encoded, segment_ids, doc_slots):
    onehot = (segment_ids[..., None] == jnp.arange(doc_slots, dtype=jnp.int32)).astype(jnp.float32)
    doc_sums = jnp.einsum(
        "rsk,rsf->rkf", onehot, encoded.astype(jnp.float32), precision=lax.Precision.HIGHEST
    )
    doc_counts = jnp.sum(onehot, 1)[..., None]
    return doc_sums / doc_counts


def reduce_norm(partial_sum, base_half, gain, need_full):
    own_width = base_half.shape[-1]
    offset = lax.axis_index("mp") * own_width
    gain_half = lax.dynamic_slice_in_dim(gain, offset, own_width)
    shared = lax.psum_scatter(partial_sum, "mp", scatter_dimension=1, tiled=True)
    pre_norm = base_half.astype(jnp.float32) + shared
    row_mean = lax.psum(jnp.sum(pre_norm, -1), "mp")[:, None] / gain.shape[0]
    centred = pre_norm - row_mean
    row_var = lax.psum(jnp.sum(centred * centred, -1), "mp")[:, None] / gain.shape[0]
    own_half = (centred * lax.rsqrt(row_var + 1e-05) * gain_half).astype(jnp.bfloat16)
    full_rows = lax.all_gather(own_half, "mp", axis=1, tiled=True) if need_full else None
    return (own_half, full_rows)


def shards(tokens, doc_ids, dest, owner, w_qkv, w_out, gain_attn, w_up, w_down, gain_ffn):
    device_count = lax.axis_size("dp")
    row_count, seq_len, own_width = tokens.shape
    model_width = w_qkv.shape[0]
    doc_slots = owner.shape[1]
    peer_rows = (row_count + device_count - 1) // device_count
    row_position = jnp.arange(row_count, dtype=jnp.int32)
    before = row_position[None, :] < row_position[:, None]
    target_dev = dest // row_count
    send_rank = jnp.sum(
        ((target_dev[:, None] == target_dev[None, :]) & before).astype(jnp.int32), -1
    )
    send_slot = target_dev * peer_rows + send_rank
    pick_rows = send_slot[None, :] == jnp.arange(device_count * peer_rows, dtype=jnp.int32)[:, None]
    outgoing = jnp.einsum(
        "pr,rsf->psf", pick_rows.astype(jnp.bfloat16), tokens, preferred_element_type=jnp.bfloat16
    )
    pick_int = pick_rows.astype(jnp.int32)
    outgoing_ids = jnp.einsum("pr,rs->ps", pick_int, doc_ids)
    outgoing_dest = jnp.sum(pick_int * (dest + 1)[None, :], -1) - 1
    received = lax.all_to_all(outgoing, "dp", split_axis=0, concat_axis=0, tiled=True)
    received_ids, received_dest = (
        lax.all_to_all(outgoing_ids, "dp", split_axis=0, concat_axis=0, tiled=True),
        lax.all_to_all(outgoing_dest, "dp", split_axis=0, concat_axis=0, tiled=True),
    )
    local_target = received_dest - lax.axis_index("dp") * row_count
    placing_rows = local_target[None, :] == row_position[:, None]
    moved = jnp.einsum(
        "rp,psf->rsf",
        placing_rows.astype(jnp.bfloat16),
        received,
        preferred_element_type=jnp.bfloat16,
    )
    segment_ids = jnp.einsum("rp,ps->rs", placing_rows.astype(jnp.int32), received_ids)
    doc_total = row_count * doc_slots
    full_input = lax.all_gather(moved, "mp", axis=2, tiled=True)
    flat_rows = full_input.reshape(-1, model_width)
    mixed_heads = attend(flat_rows, segment_ids, w_qkv, w_out)
    normed_half, normed_full = reduce_norm(
        mixed_heads, moved.reshape(-1, own_width), gain_attn, True
    )
    hidden = jax.nn.gelu(
        jnp.dot(normed_full, w_up, preferred_element_type=jnp.float32), approximate=False
    ).astype(jnp.bfloat16)
    ffn_out = jnp.dot(hidden, w_down, preferred_element_type=jnp.float32)
    encoded_half, encoded_full = reduce_norm(ffn_out, normed_half, gain_ffn, False)
    encoded = encoded_half.reshape(row_count, seq_len, own_width)
    pooled = pool_docs(encoded, segment_ids, doc_slots)
    squares = lax.psum(jnp.sum(pooled * pooled, -1), "mp")
    embedded = pooled * lax.rsqrt(squares[..., None] / model_width + 1e-06)
    capacity = (doc_total + device_count - 1) // device_count + 1
    owners = owner.reshape(-1)
    position = jnp.arange(doc_total, dtype=jnp.int32)
    earlier = (owners[:, None] == owners[None, :]) & (position[None, :] < position[:, None])
    slot_rank = jnp.sum(earlier.astype(jnp.int32), -1)
    target_slot = owners * capacity + slot_rank
    placing = (
        target_slot[None, :] == jnp.arange(device_count * capacity, dtype=jnp.int32)[:, None]
    ).astype(jnp.float32)
    sending = jnp.dot(
        placing,
        embedded.reshape(doc_total, own_width),
        precision=lax.Precision.HIGHEST,
        preferred_element_type=jnp.float32,
    )
    index_part = lax.all_to_all(sending, "dp", split_axis=0, concat_axis=0, tiled=True)
    return (encoded, index_part[None])


def solution(mesh):
    return jax.shard_map(
        shards,
        mesh=mesh,
        in_specs=(
            P("dp", None, "mp"),
            P("dp", None),
            P("dp"),
            P("dp", None),
            P(None, None, "mp"),
            P("mp", None),
            P(),
            P(None, "mp"),
            P("mp", None),
            P(),
        ),
        out_specs=(P("dp", None, "mp"), P("dp", None, "mp")),
        check_vma=False,
    )
```

profile of v0, /device:TPU:0, one launch (start us, length us, event | category | flops | bytes accessed | tf_op | source)
XLA Modules:
  0.0 371.9 jit_solution(17141482767576491087)
XLA Ops:
  7.2 0.8 broadcast_add_fusion
  8.3 0.7 copy.57
  9.0 11.5 %all-to-all-start = ((s32[64,1,1]{2,1,0:T(1,128)}), s32[64,1,1]{2,1,0:T(1,128)S(1)}, u32[]{:S(2)}, u32[]{:S(2)}) async-start(s32[64,1,1]{2,1,0:T(1,128)} %copy.57), calls=%async_computation | async-start | bytes 65536 | tf_op jit(solution)/shard_map/all_to_all | solution.py:80
  20.5 1.5 fusion.25
  22.0 4.4 %copy.59 = bf16[64,64,512]{2,1,0:T(8,128)(2,1)} copy(bf16[64,64,512]{2,0,1:T(8,128)(2,1)S(1)} %fusion.25) | data formatting | bytes 8388608 | tf_op jit(solution)/shard_map/pr,rsf->psf/dot_general | solution.py:71
  26.4 3.6 all-to-all-done
  30.0 7.1 %all-to-all-start.1 = ((bf16[64,64,512]{2,1,0:T(8,128)(2,1)}), bf16[64,64,512]{2,1,0:T(8,128)(2,1)}, u32[]{:S(2)}, u32[]{:S(2)}) async-start(bf16[64,64,512]{2,1,0:T(8,128)(2,1)} %copy.59), calls=%async_computation.1 | async-start | bytes 8388608 | tf_op jit(solution)/shard_map/all_to_all | solution.py:77
  37.2 1.2 subtract_reduce_fusion
  38.4 50.7 %all-to-all-done.1 = bf16[64,64,512]{2,1,0:T(8,128)(2,1)} async-done(((bf16[64,64,512]{2,1,0:T(8,128)(2,1)}), bf16[64,64,512]{2,1,0:T(8,128)(2,1)}, u32[]{:S(2)}, u32[]{:S(2)}) %all-to-all-start.1) | async-done | bytes 4194336 | tf_op jit(solution)/shard_map/all_to_all | solution.py:77
  89.1 8.6 %fusion.14 = bf16[28,64,512]{2,0,1:T(8,128)(2,1)} fusion(bf16[64,64,512]{2,1,0:T(8,128)(2,1)} %all-to-all-done.1, s32[64]{0:T(128)S(1)} %subtract_reduce_fusion), kind=kOutput, calls=%fused_computation.26 | convolution fusion | flops 117442304 | bytes 6029568 | tf_op jit(solution)/shard_map/rp,psf->rsf/dot_general | solution.py:84
  97.7 0.9 fusion.36
  98.6 11.8 %all-to-all-start.2 = ((s32[64,1,64]{2,1,0:T(1,128)}), s32[64,1,64]{2,1,0:T(1,128)S(1)}, u32[]{:S(2)}, u32[]{:S(2)}) async-start(s32[64,1,64]{2,1,0:T(1,128)} %bitcast.8), calls=%async_computation.2 | async-start | bytes 65536 | tf_op jit(solution)/shard_map/all_to_all | solution.py:79
  110.5 4.9 %copy.63 = bf16[1024,3,512]{0,2,1:T(8,128)(2,1)} copy(bf16[1024,3,512]{2,0,1:T(8,128)(2,1)} %param.14) | data formatting | bytes 6291456 | tf_op args[4]
  115.4 4.5 %all-to-all-done.2 = s32[64,1,64]{2,1,0:T(1,128)S(1)} async-done(((s32[64,1,64]{2,1,0:T(1,128)}), s32[64,1,64]{2,1,0:T(1,128)S(1)}, u32[]{:S(2)}, u32[]{:S(2)}) %all-to-all-start.2) | async-done | bytes 16416 | tf_op jit(solution)/shard_map/all_to_all | solution.py:79
  120.5 4.4 %copy.62 = bf16[28,64,1024]{2,1,0:T(8,128)(2,1)S(1)} copy(bf16[28,64,1024]{2,0,1:T(8,128)(2,1)} %all-gather.3.cloned.1.call-done) | data formatting | bytes 7340032 | tf_op jit(solution)/shard_map/all_gather | solution.py:92
  124.8 8.0 %convolution_convert_fusion = bf16[1792,1536]{1,0:T(8,128)(2,1)} fusion(bf16[1792,1024]{1,0:T(8,128)(2,1)S(1)} %bitcast.57, bf16[1024,1536]{0,1:T(8,128)(2,1)S(1)} %bitcast.58), kind=kOutput, calls=%fused_computation.20 | convolution fusion | flops 5639897088 | bytes 12320768 | tf_op jit(solution)/shard_map/dot_general | solution.py:16
  132.8 14.5 %reshape.109 = bf16[28,64,3,8,64]{4,3,2,1,0:T(8,128)(2,1)} reshape(bf16[1792,1536]{1,0:T(8,128)(2,1)} %convolution_convert_fusion) | data formatting | bytes 11010048 | tf_op jit(solution)/shard_map/reshape | solution.py:19
  147.3 7.8 %fusion.78 = (bf16[28,64,1,8,64]{4,3,2,1,0:T(8,128)(2,1)}, bf16[28,64,1,8,64]{4,3,2,1,0:T(8,128)(2,1)}, bf16[28,64,1,8,64]{4,3,2,1,0:T(8,128)(2,1)}) fusion(bf16[28,64,3,8,64]{4,3,2,1,0:T(8,128)(2,1)} %reshape.109), kind=kLoop, calls=%fused_computation.119 | loop fusion | bytes 11010048 | tf_op jit(solution)/shard_map/slice | solution.py:29
  155.1 6.2 %copy.73 = bf16[28,64,1,8,64]{1,4,3,0,2:T(8,128)(2,1)} copy(bf16[28,64,1,8,64]{4,3,2,1,0:T(8,128)(2,1)} %get-tuple-element.2) | data formatting | bytes 3670016
  161.3 5.2 %fusion.17 = f32[28,8,64,64]{2,3,1,0:T(8,128)S(1)} fusion(bf16[28,64,1,8,64]{4,3,2,1,0:T(8,128)(2,1)} %get-tuple-element.3, bf16[28,64,1,8,64]{4,3,2,1,0:T(8,128)(2,1)} %get-tuple-element.4), kind=kOutput, calls=%fused_computation.30 | convolution fusion | flops 117440512 | bytes 7340032 | tf_op jit(solution)/shard_map/rqhd,rkhd->rhqk/dot_general | solution.py:20
  166.5 3.1 fusion.79
  169.6 2.9 convert_bitcast_fusion
  172.6 6.3 %copy.69 = bf16[28,64,8,64]{3,2,1,0:T(8,128)(2,1)} copy(bf16[28,64,8,64]{1,3,2,0:T(8,128)(2,1)} %convert_bitcast_fusion) | data formatting | bytes 3670016 | tf_op jit(solution)/shard_map/convert_element_type | solution.py:30
  178.9 15.2 %reshape.110 = bf16[1792,512]{1,0:T(8,128)(2,1)S(1)} reshape(bf16[28,64,8,64]{3,2,1,0:T(8,128)(2,1)} %copy.69) | data formatting | bytes 3670016 | tf_op jit(solution)/shard_map/reshape | solution.py:31
  194.1 5.1 %fusion.82 = f32[1792,1024]{1,0:T(8,128)} fusion(bf16[1792,512]{1,0:T(8,128)(2,1)S(1)} %reshape.110, bf16[512,1024]{1,0:T(8,128)(2,1)S(1)} %copy-done.12), kind=kOutput, calls=%fused_computation.122 | convolution fusion | flops 1879048192 | bytes 10223616 | tf_op jit(solution)/shard_map/dot_general | solution.py:31
  199.3 4.6 %copy.61 = f32[28,64,512]{2,1,0:T(8,128)} copy(bf16[28,64,512]{2,0,1:T(8,128)(2,1)} %fusion.14) | data formatting | bytes 5505024 | tf_op jit(solution)/shard_map/convert_element_type | solution.py:48
  203.9 11.5 %reduce-scatter.3.cloned.1.call-done = f32[1792,512]{1,0:T(8,128)} async-done(((f32[1792,1024]{1,0:T(8,128)}), f32[1792,512]{1,0:T(8,128)}) %reduce-scatter.3.cloned.1.call-update) | async-done | bytes 3670032 | tf_op jit(solution)/shard_map/reduce_scatter | solution.py:47
  215.4 3.5 fusion.77
  219.0 2.6 psum.35
  221.6 4.0 %multiply_reduce_fusion.1 = f32[1792]{0:T(1024)S(1)} fusion(f32[1792]{0:T(1024)S(1)} %broadcast_multiply_fusion.2, f32[1792,512]{1,0:T(8,128)} %reduce-scatter.3.cloned.1.call-done, f32[28,64,512]{2,1,0:T(8,128)} %copy.61), kind=kLoop, calls=%fused_computation.38 | loop fusion | flops 3668224 | bytes 7354368 | tf_op jit(solution)/shard_map/reduce_sum | solution.py:51
  225.6 2.5 psum.36
  228.1 4.6 %multiply_convert_fusion.1 = bf16[1792,512]{1,0:T(8,128)(2,1)} fusion(f32[512]{0:T(512)S(1)} %dynamic_slice.6, f32[1792]{0:T(1024)S(1)} %add_rsqrt_fusion.2, f32[1792]{0:T(1024)S(1)} %broadcast_multiply_fusion.2, f32[1792,512]{1,0:T(8,128)} %reduce-scatter.3.cloned.1.call-done, f32[28,64,512]{2,1,0:T(8,128)} %copy.61), kind=kLoop, calls=%fused_computation.37 | loop fusion | flops 4587520 | bytes 9191424 | tf_op jit(solution)/shard_map/convert_element_type | solution.py:52
  232.9 17.1 %all-gather.5.cloned.1.call-done = bf16[1792,1024]{1,0:T(8,128)(2,1)} async-done(((bf16[1792,512]{1,0:T(8,128)(2,1)}), bf16[1792,1024]{1,0:T(8,128)(2,1)}) %all-gather.5.cloned.1.call-update) | async-done | bytes 3670032 | tf_op jit(solution)/shard_map/all_gather | solution.py:53
  249.9 40.1 %fusion.103 = bf16[1792,2048]{1,0:T(8,128)(2,1)S(1)} fusion(bf16[1792,1024]{1,0:T(8,128)(2,1)} %all-gather.5.cloned.1.call-done, bf16[1024,2048]{1,0:T(8,128)(2,1)} %param.17), kind=kOutput, calls=%fused_computation.4.clone.clone.1 | convolution fusion | flops 7754743808 | bytes 15204352 | tf_op jit(solution)/shard_map/dot_general | solution.py:99
  290.0 10.0 %fusion.11 = f32[1792,1024]{1,0:T(8,128)} fusion(bf16[2048,1024]{1,0:T(8,128)(2,1)S(1)} %copy-done.11, bf16[1792,2048]{1,0:T(8,128)(2,1)S(1)} %fusion.103), kind=kOutput, calls=%fused_computation.24 | convolution fusion | flops 7516192768 | bytes 18874368 | tf_op jit(solution)/shard_map/dot_general | solution.py:101
  300.1 0.7 copy-done.10
  301.3 18.7 %reduce-scatter.5.cloned.1.call-done = f32[1792,512]{1,0:T(8,128)} async-done(((f32[1792,1024]{1,0:T(8,128)}), f32[1792,512]{1,0:T(8,128)}) %reduce-scatter.5.cloned.1.call-update) | async-done | bytes 3670032 | tf_op jit(solution)/shard_map/reduce_scatter | solution.py:47
  320.0 2.5 fusion.27
  322.5 2.6 psum.37
  325.1 3.5 multiply_reduce_fusion
  328.6 2.5 psum.38
  331.2 3.1 multiply_convert_fusion
  334.3 1.2 copy-done.5
  335.5 0.4 multiply_reduce_fusion.2
  336.0 3.5 psum.39
  339.7 0.4 fusion.28
  340.4 23.8 %all_to_all.29 = f32[64,3,512]{2,1,0:T(4,128)S(1)} all-to-all(f32[64,3,512]{2,1,0:T(4,128)S(1)} %copy.71), channel_id=1, replica_groups=mesh['dp'=64,'mp'=2] {'dp'}, dimensions={0} | all-to-all | bytes 786432 | tf_op jit(solution)/shard_map/all_to_all | solution.py:122
  364.2 0.9 broadcast_in_dim.12
  (57 shorter events, 2.2 us)
Async XLA Ops:
  7.2 13.3 %copy-start = (bf16[28,64,512]{2,1,0:T(8,128)(2,1)S(1)}, bf16[28,64,512]{2,1,0:T(8,128)(2,1)}, u32[]{:S(2)}) copy-start(bf16[28,64,512]{2,1,0:T(8,128)(2,1)} %param.10) | copy-start | bytes 5505028
  9.0 21.0 %all-to-all-start = ((s32[64,1,1]{2,1,0:T(1,128)}), s32[64,1,1]{2,1,0:T(1,128)S(1)}, u32[]{:S(2)}, u32[]{:S(2)}) async-start(s32[64,1,1]{2,1,0:T(1,128)} %copy.57), calls=%async_computation | async-start | bytes 65536 | tf_op jit(solution)/shard_map/all_to_all | solution.py:80
  26.4 71.3 %copy-start.13 = (s32[28,64]{1,0:T(8,128)S(1)}, s32[28,64]{1,0:T(8,128)}, u32[]{:S(2)}) copy-start(s32[28,64]{1,0:T(8,128)} %param.11) | copy-start | bytes 21508
  30.0 59.1 %all-to-all-start.1 = ((bf16[64,64,512]{2,1,0:T(8,128)(2,1)}), bf16[64,64,512]{2,1,0:T(8,128)(2,1)}, u32[]{:S(2)}, u32[]{:S(2)}) async-start(bf16[64,64,512]{2,1,0:T(8,128)(2,1)} %copy.59), calls=%async_computation.1 | async-start | bytes 8388608 | tf_op jit(solution)/shard_map/all_to_all | solution.py:77
  37.1 83.3 %all-gather.3.cloned.1.call-start = ((), (), s32[]{:S(2)}) async-start(), calls=%async_computation.6 | async-start | bytes 6291456 | tf_op jit(solution)/shard_map/all_gather | solution.py:92
  98.6 21.3 %all-to-all-start.2 = ((s32[64,1,64]{2,1,0:T(1,128)}), s32[64,1,64]{2,1,0:T(1,128)S(1)}, u32[]{:S(2)}, u32[]{:S(2)}) async-start(s32[64,1,64]{2,1,0:T(1,128)} %bitcast.8), calls=%async_computation.2 | async-start | bytes 65536 | tf_op jit(solution)/shard_map/all_to_all | solution.py:79
  110.5 104.9 %reduce-scatter.3.cloned.1.call-start = ((), (), s32[]{:S(2)}) async-start(), calls=%async_computation.7 | async-start | bytes 11010048 | tf_op jit(solution)/shard_map/reduce_scatter | solution.py:47
  120.1 12.7 %copy-start.6 = (s32[28,64]{1,0:T(8,128)}, s32[28,64]{1,0:T(8,128)S(1)}, u32[]{:S(2)}) copy-start(s32[28,64]{1,0:T(8,128)S(1)} %fusion.34) | copy-start | bytes 21508
  120.5 4.4 %copy-start.4 = (bf16[1024,3,512]{0,2,1:T(8,128)(2,1)S(1)}, bf16[1024,3,512]{0,2,1:T(8,128)(2,1)}, u32[]{:S(2)}) copy-start(bf16[1024,3,512]{0,2,1:T(8,128)(2,1)} %copy.63) | copy-start | bytes 9437188
  166.5 3.1 copy-start.3
  172.6 21.6 %copy-start.12 = (bf16[512,1024]{1,0:T(8,128)(2,1)S(1)}, bf16[512,1024]{1,0:T(8,128)(2,1)}, u32[]{:S(2)}) copy-start(bf16[512,1024]{1,0:T(8,128)(2,1)} %param.15) | copy-start | bytes 3145732
  194.1 5.1 %copy-start.9 = (f32[1024]{0:T(1024)S(1)}, f32[1024]{0:T(1024)}, u32[]{:S(2)}) copy-start(f32[1024]{0:T(1024)} %param.16) | copy-start | bytes 12292
  199.2 50.7 %all-gather.5.cloned.1.call-start = ((), (), s32[]{:S(2)}) async-start(), calls=%async_computation.8 | async-start | bytes 5505024 | tf_op jit(solution)/shard_map/all_gather | solution.py:53
  232.8 87.2 %reduce-scatter.5.cloned.1.call-start = ((), (), s32[]{:S(2)}) async-start(), calls=%async_computation.9 | async-start | bytes 11010048 | tf_op jit(solution)/shard_map/reduce_scatter | solution.py:47
  249.9 40.1 %copy-start.11 = (bf16[2048,1024]{1,0:T(8,128)(2,1)S(1)}, bf16[2048,1024]{1,0:T(8,128)(2,1)}, u32[]{:S(2)}) copy-start(bf16[2048,1024]{1,0:T(8,128)(2,1)} %param.18) | copy-start | bytes 12582916
  300.0 0.7 copy-start.10
  300.0 0.8 copy-start.8
  300.0 1.2 copy-start.7
  300.0 20.0 %copy-start.2 = (bf16[1792,512]{1,0:T(8,128)(2,1)S(1)}, bf16[1792,512]{1,0:T(8,128)(2,1)}, u32[]{:S(2)}) copy-start(bf16[1792,512]{1,0:T(8,128)(2,1)} %multiply_convert_fusion.1) | copy-start | bytes 5505028
  325.1 40.0 %copy-start.1 = (bf16[28,64,512]{2,1,0:T(8,128)(2,1)S(1)}, bf16[28,64,512]{2,1,0:T(8,128)(2,1)}, u32[]{:S(2)}) copy-start(bf16[28,64,512]{2,1,0:T(8,128)(2,1)} %param.10) | copy-start | bytes 5505028
  334.3 1.2 copy-start.5
Sparse Core Ops, SparseCore 0:
  97.8 18.9 all-gather.2
  199.3 16.0 reduce-scatter.2
  232.9 16.9 all-gather.4
  300.2 19.7 reduce-scatter.4
where the time goes:
time: 377 us; the launch traced here: 372 us
  waiting for transfers between devices  106 us (28%)
  matrix products  83.1 us (22%)
  local copies, waits for them, and re-layouts  72.5 us (19%)
  blocking collectives  37.6 us (10%)
  starting transfers between devices  30.6 us (8%)
  other arithmetic  27.4 us (7%)
  between operations  14.3 us (4%)
    all_to_all x1, waiting for transfers between devices, shards(): lax.all_to_all(outgoing, 'dp', split_axis=0, concat_axis=0, tiled=True)  50.7 us
    dot_general x1, matrix products, shards(): jnp.dot(normed_full, w_up, preferred_element_type=jnp.float32)  40.1 us
    reduce_scatter x2, waiting for transfers between devices, reduce_norm(): lax.psum_scatter(partial_sum, 'mp', scatter_dimension=1, tiled=True)  30.2 us
    all_to_all x1, blocking collectives, shards(): lax.all_to_all(sending, 'dp', split_axis=0, concat_axis=0, tiled=True)  23.8 us
    all_gather x1, waiting for transfers between devices, reduce_norm(): lax.all_gather(own_half, 'mp', axis=1, tiled=True)  17.1 us
    reshape x1, local copies, waits for them, and re-layouts, attend(): context.reshape(-1, width)  15.2 us
    reshape x1, local copies, waits for them, and re-layouts, attend(): qkv = qkv.reshape(row_count, seq_len, 3, head_local, HD)  14.5 us
    unnamed x31, local copies, waits for them, and re-layouts  13.1 us
  transfers between devices with their start and end apart: 7, of which 6 were waited for; matrix products, arithmetic and copies ran while one was open for 5% of the time, Pallas kernels for 0%

commit v1 on v0

v1 whole, which is shorter than its diff:
```python
import jax
import jax.numpy as jnp
from jax import lax
from jax.experimental import pallas as pl
from jax.experimental.pallas import tpu as pltpu
from jax.sharding import PartitionSpec as P

HD = 64
HEADS = 4
TILE = 512
SLOTS = 4
ERF = (
    0.797884941,
    0.0363330846,
    -3.25949759e-05,
    -5.53061935e-05,
    3.96474438e-06,
    -1.32263336e-07,
    1.75617062e-09,
)
SWAP = [(0, 1), (1, 0)]


def gelu(x):
    u = jnp.minimum(x * x, 30.25)
    poly = jnp.full_like(u, ERF[-1])
    for coef in ERF[-2::-1]:
        poly = poly * u + coef
    half = 0.5 * x
    return half + half * jnp.tanh(x * poly)


def norm(values, gain):
    mean = jnp.mean(values, -1, keepdims=True)
    centred = values - mean
    var = jnp.mean(centred * centred, -1, keepdims=True)
    return centred * lax.rsqrt(var + 1e-05) * gain


def pack_kernel(target, tokens, out, sems):
    rows = tokens.shape[0]
    copies = [
        pltpu.make_async_copy(tokens.at[r], out.at[target[r]], sems.at[r]) for r in range(rows)
    ]
    for copy in copies:
        copy.start()
    for copy in copies:
        copy.wait()


def pack(target, tokens, slots):
    rows, seq, width = tokens.shape
    return pl.pallas_call(
        pack_kernel,
        out_shape=jax.ShapeDtypeStruct((slots, seq, width), tokens.dtype),
        in_specs=[
            pl.BlockSpec(memory_space=pltpu.SMEM),
            pl.BlockSpec(memory_space=pl.ANY),
        ],
        out_specs=pl.BlockSpec(memory_space=pl.ANY),
        scratch_shapes=[pltpu.SemaphoreType.DMA((rows,))],
        name="pack_rows",
    )(target, tokens)


def unpack_kernel(source, received, out, sems):
    copies = [
        pltpu.make_async_copy(received.at[source[r]], out.at[r], sems.at[r])
        for r in range(out.shape[0])
    ]
    for copy in copies:
        copy.start()
    for copy in copies:
        copy.wait()


def unpack(source, received):
    rows = source.shape[0]
    _, seq, width = received.shape
    return pl.pallas_call(
        unpack_kernel,
        out_shape=jax.ShapeDtypeStruct((rows, seq, width), received.dtype),
        in_specs=[
            pl.BlockSpec(memory_space=pltpu.SMEM),
            pl.BlockSpec(memory_space=pl.ANY),
        ],
        out_specs=pl.BlockSpec(memory_space=pl.ANY),
        scratch_shapes=[pltpu.SemaphoreType.DMA((rows,))],
        name="unpack_rows",
    )(source, received)


def layer_kernel(
    info,
    received,
    x_other,
    wq_own,
    wq_oth,
    wo_own,
    wo_oth,
    wu_own,
    wu_oth,
    wd_own,
    wd_oth,
    gain_attn,
    gain_ffn,
    enc_own,
    enc_oth,
    emb_own,
    emb_oth,
    x_scr,
    qkv_scr,
    ctx_scr,
    normed_scr,
    acc_scr,
    emb_scr,
    wq,
    wo,
    wu,
    wd,
    row_sems,
    x_sem,
    q_sems,
    w_sems,
):
    rows = enc_own.shape[0] // 64
    seq = 64
    tokens = rows * seq
    half = enc_own.shape[1]
    model = 2 * half
    me = info[0]
    own_col = pl.multiple_of(me * half, half)
    oth_col = pl.multiple_of((1 - me) * half, half)
    row_copies = [
        pltpu.make_async_copy(
            received.at[info[8 + r]],
            x_scr.at[pl.ds(r * seq, seq), pl.ds(own_col, half)],
            row_sems.at[r],
        )
        for r in range(rows)
    ]
    x_copy = pltpu.make_async_copy(x_other, x_scr.at[:, pl.ds(oth_col, half)], x_sem)
    q_copies = [
        pltpu.make_async_copy(ref.at[i], wq.at[3 * h + i], q_sems.at[3 * h + i])
        for h, ref in enumerate((wq_own, wq_oth))
        for i in range(3)
    ]
    width_up = wu_own.shape[1]
    w_copies = [
        pltpu.make_async_copy(wo_own, wo.at[pl.ds(0, half)], w_sems.at[0]),
        pltpu.make_async_copy(wo_oth, wo.at[pl.ds(half, half)], w_sems.at[1]),
        pltpu.make_async_copy(wu_own, wu.at[0], w_sems.at[2]),
        pltpu.make_async_copy(wu_oth, wu.at[1], w_sems.at[3]),
        pltpu.make_async_copy(wd_own, wd.at[0], w_sems.at[4]),
        pltpu.make_async_copy(wd_oth, wd.at[1], w_sems.at[5]),
    ]
    for copy in row_copies:
        copy.start()
    x_copy.start()
    for copy in q_copies + w_copies:
        copy.start()
    for copy in row_copies:
        copy.wait()
    x_copy.wait()

    for n in range(6):
        q_copies[n].wait()
        qkv_scr[:, n * half : (n + 1) * half] = jnp.dot(
            x_scr[...], wq[n], preferred_element_type=jnp.float32
        ).astype(jnp.bfloat16)

    group = HEADS * HD
    block = (
        lax.broadcasted_iota(jnp.int32, (group, group), 0) // HD
        == lax.broadcasted_iota(jnp.int32, (group, group), 1) // HD
    )
    lane_head = lax.broadcasted_iota(jnp.int32, (seq, group), 1) // HD
    key_pos = lax.broadcasted_iota(jnp.int32, (seq, group), 0)
    query_pos = lax.broadcasted_iota(jnp.int32, (seq, group), 1) % HD

    def attend(r, carry):
        base = pl.multiple_of(r * seq, seq)
        bounds = [info[32 + 4 * r + i] for i in range(3)]
        key_seg = sum([(key_pos >= b).astype(jnp.int32) for b in bounds])
        query_seg = sum([(query_pos >= b).astype(jnp.int32) for b in bounds])
        same = key_seg == query_seg
        for g in range(model // group):
            at = (g * group // half) * 3 * half + (g * group) % half
            q = qkv_scr[pl.ds(base, seq), at : at + group]
            k = qkv_scr[pl.ds(base, seq), at + half : at + half + group]
            v = qkv_scr[pl.ds(base, seq), at + 2 * half : at + 2 * half + group]
            spread = jnp.where(block, jnp.concatenate([q] * HEADS, 0), jnp.zeros((), q.dtype))
            scores = lax.dot_general(
                k, spread, (((1,), (1,)), ((), ())), preferred_element_type=jnp.float32
            )
            scores = jnp.where(same, scores * (1.0 / 8.0), jnp.float32(-1e30))
            top = jnp.max(scores, 0, keepdims=True)
            weight = jnp.exp(scores - top)
            probs = (weight / jnp.sum(weight, 0, keepdims=True)).astype(jnp.bfloat16)
            mixed = lax.dot_general(
                probs, v, (((0,), (0,)), ((), ())), preferred_element_type=jnp.float32
            )
            context = jnp.where(lane_head == 0, mixed[:seq], 0.0)
            for h in range(1, HEADS):
                context = jnp.where(lane_head == h, mixed[h * seq : (h + 1) * seq], context)
            ctx_scr[pl.ds(base, seq), g * group : (g + 1) * group] = context.astype(jnp.bfloat16)
        return carry

    lax.fori_loop(0, rows, attend, 0)

    w_copies[0].wait()
    w_copies[1].wait()
    part = tokens // 4

    def mix(m, carry):
        at = pl.ds(pl.multiple_of(m * part, part), part)
        mixed = jnp.dot(ctx_scr[at, :], wo[...], preferred_element_type=jnp.float32)
        mixed = mixed + x_scr[at, :].astype(jnp.float32)
        normed_scr[at, :] = norm(mixed, gain_attn[...]).astype(jnp.bfloat16)
        return carry

    lax.fori_loop(0, 4, mix, 0)

    tiles = width_up // TILE
    for h in range(2):
        w_copies[2 + h].wait()
        w_copies[4 + h].wait()

        def feed(t, carry, h=h):
            at = pl.ds(pl.multiple_of(t * TILE, TILE), TILE)
            up = jnp.dot(normed_scr[...], wu[h, :, at], preferred_element_type=jnp.float32)
            hidden = gelu(up).astype(jnp.bfloat16)
            down = jnp.dot(hidden, wd[h, at, :], preferred_element_type=jnp.float32)
            acc_scr[...] += down
            return carry

        if h == 0:
            acc_scr[...] = normed_scr[...].astype(jnp.float32)
        lax.fori_loop(0, tiles, feed, 0)

    doc_iota = lax.broadcasted_iota(jnp.int32, (8, seq), 0)
    pos_iota = lax.broadcasted_iota(jnp.int32, (8, seq), 1)

    def finish(r, carry):
        at = pl.ds(pl.multiple_of(r * seq, seq), seq)
        out_at = pl.ds(pl.multiple_of(r * 8, 8), 8)
        encoded = norm(acc_scr[at, :], gain_ffn[...]).astype(jnp.bfloat16)
        x_scr[at, :] = encoded
        bounds = [info[32 + 4 * r + i] for i in range(3)]
        seg = sum([(pos_iota >= b).astype(jnp.int32) for b in bounds])
        member = (seg == doc_iota).astype(jnp.float32)
        count = jnp.sum(member, -1, keepdims=True)
        pooled = jnp.dot(member.astype(jnp.bfloat16), encoded, preferred_element_type=jnp.float32)
        pooled = pooled / jnp.maximum(count, 1.0)
        square = jnp.mean(pooled * pooled, -1, keepdims=True)
        emb_scr[out_at, :] = pooled * lax.rsqrt(square + 1e-06)
        return carry

    lax.fori_loop(0, rows, finish, 0)
    enc_own[...] = x_scr[:, pl.ds(own_col, half)]
    enc_oth[...] = x_scr[:, pl.ds(oth_col, half)]
    emb_own[...] = emb_scr[:, pl.ds(own_col, half)].astype(jnp.bfloat16)
    emb_oth[...] = emb_scr[:, pl.ds(oth_col, half)].astype(jnp.bfloat16)


def layer(info, received, x_other, weights, gain_attn, gain_ffn):
    tokens, half = x_other.shape
    rows = tokens // 64
    model = 2 * half
    wq, wo, wu, wd = weights[0], weights[2], weights[4], weights[6]
    flops = 2 * tokens * model * (3 * model + model + 4 * wu.shape[1])
    any_spec = pl.BlockSpec(memory_space=pl.ANY)
    vmem = pl.BlockSpec(memory_space=pltpu.VMEM)
    return pl.pallas_call(
        layer_kernel,
        out_shape=(
            jax.ShapeDtypeStruct((tokens, half), jnp.bfloat16),
            jax.ShapeDtypeStruct((tokens, half), jnp.bfloat16),
            jax.ShapeDtypeStruct((rows * 8, half), jnp.bfloat16),
            jax.ShapeDtypeStruct((rows * 8, half), jnp.bfloat16),
        ),
        in_specs=[pl.BlockSpec(memory_space=pltpu.SMEM)] + [any_spec] * 10 + [vmem] * 2,
        out_specs=(vmem,) * 4,
        scratch_shapes=[
            pltpu.VMEM((tokens, model), jnp.bfloat16),
            pltpu.VMEM((tokens, 3 * model), jnp.bfloat16),
            pltpu.VMEM((tokens, model), jnp.bfloat16),
            pltpu.VMEM((tokens, model), jnp.bfloat16),
            pltpu.VMEM((tokens, model), jnp.float32),
            pltpu.VMEM((rows * 8, model), jnp.float32),
            pltpu.VMEM((6, model, half), jnp.bfloat16),
            pltpu.VMEM((model, model), jnp.bfloat16),
            pltpu.VMEM((2,) + wu.shape, jnp.bfloat16),
            pltpu.VMEM((2,) + wd.shape, jnp.bfloat16),
            pltpu.SemaphoreType.DMA((rows,)),
            pltpu.SemaphoreType.DMA,
            pltpu.SemaphoreType.DMA((6,)),
            pltpu.SemaphoreType.DMA((6,)),
        ],
        compiler_params=pltpu.CompilerParams(vmem_limit_bytes=60 * 1024 * 1024),
        cost_estimate=pl.CostEstimate(
            flops=flops, bytes_accessed=28 * 1024 * 1024, transcendentals=0
        ),
        name="layer",
    )(info, received, x_other, *weights, gain_attn, gain_ffn)


def shards(tokens, doc_ids, dest, owner, w_qkv, w_out, gain_attn, w_up, w_down, gain_ffn):
    devices = lax.axis_size("dp")
    row_count, seq, half = tokens.shape
    docs = owner.shape[1]
    mine = row_count // 2
    me = lax.axis_index("mp")
    index = lax.axis_index("dp")

    qkv_own = jnp.moveaxis(w_qkv, 1, 0)
    weights = []
    for own in (qkv_own, w_out, w_up, w_down):
        weights += [own, lax.ppermute(own, "mp", SWAP)]

    bounds = jnp.stack([jnp.sum((doc_ids < k).astype(jnp.int32), -1) for k in range(1, docs)], -1)
    facts = lax.all_gather(jnp.concatenate([dest[:, None], bounds], -1), "dp", axis=0)
    slot = jnp.arange(row_count, dtype=jnp.int32)
    here = facts[:, :, 0] == (index * row_count + slot)[None, :]
    source = jnp.sum(jnp.where(here, jnp.arange(devices, dtype=jnp.int32)[:, None], 0), 0)
    new_bounds = jnp.sum(jnp.where(here[:, :, None], facts[:, :, 1:], 0), 0)

    received = lax.all_to_all(
        pack(dest // row_count, tokens, devices), "dp", split_axis=0, concat_axis=0, tiled=True
    )
    source_own = lax.dynamic_slice_in_dim(source, me * mine, mine)
    source_oth = lax.dynamic_slice_in_dim(source, (1 - me) * mine, mine)
    bounds_own = lax.dynamic_slice_in_dim(new_bounds, me * mine, mine)
    info = jnp.concatenate(
        [
            jnp.full((8,), me, jnp.int32),
            source_own,
            jnp.zeros((24 - mine,), jnp.int32),
            jnp.pad(bounds_own, ((0, 0), (0, 1))).reshape(-1),
        ]
    )
    x_other = lax.ppermute(unpack(source_oth, received), "mp", SWAP).reshape(-1, half)
    enc_own, enc_oth, emb_own, emb_oth = layer(
        info, received, x_other, weights, gain_attn[None], gain_ffn[None]
    )
    emb_recv = lax.ppermute(emb_oth, "mp", SWAP)
    enc_recv = lax.ppermute(enc_oth, "mp", SWAP)

    owners = owner.reshape(-1)
    position = jnp.arange(row_count * docs, dtype=jnp.int32)
    earlier = (owners[:, None] == owners[None, :]) & (position[None, :] < position[:, None])
    rank = jnp.sum(earlier.astype(jnp.int32), -1)
    target = jnp.pad(
        (owners * SLOTS + rank).reshape(2, mine, docs), ((0, 0), (0, 0), (0, 8 - docs)),
        constant_values=-1,
    ).reshape(2, mine * 8)
    out_slot = jnp.arange(devices * SLOTS, dtype=jnp.int32)[:, None]
    place_own = (lax.dynamic_index_in_dim(target, me, 0) == out_slot).astype(jnp.bfloat16)
    place_oth = (lax.dynamic_index_in_dim(target, 1 - me, 0) == out_slot).astype(jnp.bfloat16)
    sending = (
        jnp.dot(place_own, emb_own, preferred_element_type=jnp.float32)
        + jnp.dot(place_oth, emb_recv, preferred_element_type=jnp.float32)
    ).astype(jnp.bfloat16)
    got = lax.all_to_all(
        sending.reshape(devices, SLOTS, half), "dp", split_axis=0, concat_axis=0, tiled=True
    )
    index_part = got[:, : SLOTS - 1].astype(jnp.float32).reshape(1, devices * (SLOTS - 1), half)

    enc_own = enc_own.reshape(mine, seq, half)
    enc_recv = enc_recv.reshape(mine, seq, half)
    first = me == 0
    encoded = jnp.concatenate(
        [jnp.where(first, enc_own, enc_recv), jnp.where(first, enc_recv, enc_own)], 0
    )
    return (encoded, index_part)


def solution(mesh):
    return jax.shard_map(
        shards,
        mesh=mesh,
        in_specs=(
            P("dp", None, "mp"),
            P("dp", None),
            P("dp"),
            P("dp", None),
            P(None, None, "mp"),
            P("mp", None),
            P(),
            P(None, "mp"),
            P("mp", None),
            P(),
        ),
        out_specs=(P("dp", None, "mp"), P("dp", None, "mp")),
        check_vma=False,
    )
```

time: 377 us -> 411 us (1.090); the launches traced: 372 us -> 411 us
  blocking collectives: 37.6 us -> 214 us
  Pallas kernels: 0 us -> 156 us
  waiting for transfers between devices: 106 us -> 12.8 us
  matrix products: 83.1 us -> 1.32 us
  local copies, waits for them, and re-layouts: 72.5 us -> 3.52 us
  other arithmetic: 27.4 us -> 4.02 us
  between operations: 14.3 us -> 0.87 us
  starting transfers between devices: 30.6 us -> 18.6 us
    all_gather x0 -> x1, blocking collectives: none -> 214 us  [shards(): lax.all_gather(jnp.concatenate([dest[:, None], bounds], -1), 'dp', axis=0)]
    pallas_call x0 -> x3, Pallas kernels: none -> 156 us  [the longest x1 68.3 us: layer(): pl.pallas_call(layer_kernel, out_shape=(jax.ShapeDtypeStruct((tokens, hal...]
    dot_general x12 -> x2, matrix products: 83.1 us -> 1.32 us  [the longest x1 1.11 us: shards(): jnp.dot(place_own, emb_own, preferred_element_type=jnp.float32)]
    all_to_all x3 -> x2, waiting for transfers between devices: 58.8 us -> 11.2 us  [the longest x1 11.2 us: shards(): lax.all_to_all(sending.reshape(devices, SLOTS, half), 'dp', split_axis=0,...]
    reduce_scatter x2 -> x0, waiting for transfers between devices: 30.2 us -> none  [reduce_norm(): lax.psum_scatter(partial_sum, 'mp', scatter_dimension=1, tiled=True)]
    reshape x4, local copies, waits for them, and re-layouts: 29.9 us -> 1.89 us  [the longest x1 0.94 us: shards(): got[:, :SLOTS - 1].astype(jnp.float32)]
    all_to_all x1 -> x0, blocking collectives: 23.8 us -> none  [shards(): lax.all_to_all(sending, 'dp', split_axis=0, concat_axis=0, tiled=True)]
    all_gather x2 -> x0, waiting for transfers between devices: 17.1 us -> none  [the longest x1 17.1 us: reduce_norm(): lax.all_gather(own_half, 'mp', axis=1, tiled=True)]
  transfers between devices with their start and end apart: 7 -> 9, of which waited for: 6 -> 3; matrix products, arithmetic and copies ran while one was open for 5% -> 1% of each run, Pallas kernels for 0% -> 7%
where the time goes in v1:
time: 411 us
  blocking collectives  214 us (52%)
  Pallas kernels  156 us (38%)
  starting transfers between devices  18.6 us (5%)
  waiting for transfers between devices  12.8 us (3%)
    all_gather x1, blocking collectives, shards(): lax.all_gather(jnp.concatenate([dest[:, None], bounds], -1), 'dp', axis=0)  214 us
    pallas_call x1, Pallas kernels, layer(): pl.pallas_call(layer_kernel, out_shape=(jax.ShapeDtypeStruct((tokens, hal...  68.3 us
    pallas_call x1, Pallas kernels, pack(): pl.pallas_call(pack_kernel, out_shape=jax.ShapeDtypeStruct((slots, seq, w...  57.6 us
    pallas_call x1, Pallas kernels, unpack(): pl.pallas_call(unpack_kernel, out_shape=jax.ShapeDtypeStruct((rows, seq,...  29.7 us
    all_to_all x1, starting transfers between devices, shards(): lax.all_to_all(pack(dest // row_count, tokens, devices), 'dp', split_axis...  11.9 us
    all_to_all x1, waiting for transfers between devices, shards(): lax.all_to_all(sending.reshape(devices, SLOTS, half), 'dp', split_axis=0,...  11.2 us
  transfers between devices with their start and end apart: 9, of which 3 were waited for; matrix products, arithmetic and copies ran while one was open for 1% of the time, Pallas kernels for 7%

profile of v1, /device:TPU:0, one launch (start us, length us, event | category | flops | bytes accessed | tf_op | source)
XLA Modules:
  0.0 411.0 jit_solution(3447539348505358957)
XLA Ops:
  0.6 1.2 and_select_fusion.target
  1.8 57.6 %pack_rows.1 = bf16[64,64,512]{2,1,0:T(8,128)(2,1)} custom-call(s32[28]{0:T(128)} %and_select_fusion.target, bf16[28,64,512]{2,1,0:T(8,128)(2,1)} %tokens.1), custom_call_target="tpu_custom_call" | custom-call | tf_op jit(solution)/shard_map/pack_rows/pallas_call | solution.py:53
  59.4 0.0 copy-start.4
  59.4 0.0 copy-start.1
  59.5 0.0 copy-start.3
  59.5 11.9 %all-to-all-start = ((bf16[64,64,512]{2,1,0:T(8,128)(2,1)}), bf16[64,64,512]{2,1,0:T(8,128)(2,1)}, u32[]{:S(2)}, u32[]{:S(2)}) async-start(bf16[64,64,512]{2,1,0:T(8,128)(2,1)} %pack_rows.1), calls=%async_computation | async-start | bytes 8388608 | tf_op jit(solution)/shard_map/all_to_all | solution.py:328
  71.4 0.0 copy-start.2
  71.4 0.1 collective-permute-start.3
  71.5 0.5 collective-permute-start.4
  72.0 0.1 collective-permute-start.1
  72.1 0.4 collective-permute-start.2
  72.5 0.1 convert_reduce_fusion.3
  72.7 214.3 %all-gather.1 = s32[64,28,4]{1,2,0:T(4,128)S(1)} all-gather(s32[1,28,4]{1,2,0:T(4,128)S(1)} %add_bitcast_fusion), channel_id=2, replica_groups=mesh['dp'=64,'mp'=2] {'dp'}, dimensions={0}, use_global_device_ids=true | all-gather | bytes 29120 | tf_op jit(solution)/shard_map/all_gather | solution.py:322
  287.0 0.1 copy.31
  287.1 0.2 select_reduce_fusion
  287.2 0.6 fusion.8
  287.8 0.0 all-to-all-done.received
  287.8 29.7 %unpack_rows.1 = bf16[14,64,512]{2,1,0:T(8,128)(2,1)} custom-call(s32[14]{0:T(128)} %get-tuple-element.17.source, bf16[64,64,512]{2,1,0:T(8,128)(2,1)} %all-to-all-done.received), custom_call_target="tpu_custom_call" | custom-call | tf_op jit(solution)/shard_map/unpack_rows/pallas_call | solution.py:80
  317.5 0.3 collective-permute-start
  317.8 0.1 compare_bitcast_fusion
  317.9 0.1 copy.26
  318.0 0.1 fusion.1
  318.1 0.1 constant_dynamic-slice_fusion.2
  318.2 0.1 copy.32
  318.3 0.1 reshape.47
  318.4 0.1 copy.28
  318.5 0.1 eq.66
  318.6 0.6 pad_add_fusion.info
  319.2 0.0 collective-permute-done.2.wo_oth
  319.2 1.4 collective-permute-done
  320.6 68.3 %layer.1 = (bf16[896,512]{1,0:T(8,128)(2,1)}, bf16[896,512]{1,0:T(8,128)(2,1)}, bf16[112,512]{1,0:T(8,128)(2,1)}, bf16[112,512]{1,0:T(8,128)(2,1)}) custom-call(s32[88]{0:T(128)} %pad_add_fusion.info, bf16[64,64,512]{2,1,0:T(8,128)(2,1)} %all-to-all-done.received, bf16[896,512]{1,0:T(8,128)(2,1)} %bitcast.7.x_other, bf16[3,1024,512]{2,1,0:T(8,128)(2,1)} %bitcast.8.wq_own, ...), custom_call_target="tpu_custom_call" | custom-call | flops 22548578304 | bytes 29360128 | tf_op jit(solution)/shard_map/layer/pallas_call | solution.py:274
  388.9 0.3 collective-permute-start.6
  389.2 0.2 convert_reduce_fusion
  389.4 0.1 reduce_sum.62
  389.5 0.1 copy.29
  389.6 0.1 mul.25
  389.7 0.1 copy.33
  389.8 0.1 reshape.49
  389.9 0.4 collective-permute-start.5
  390.3 0.2 collective-permute-done.6
  390.5 0.2 fusion.2
  390.8 1.1 fusion
  391.9 0.8 reshape.50
  392.6 4.6 %all-to-all-start.1 = ((bf16[64,4,512]{2,1,0:T(4,128)(2,1)}), bf16[64,4,512]{2,1,0:T(4,128)(2,1)S(1)}, u32[]{:S(2)}, u32[]{:S(2)}) async-start(bf16[64,4,512]{2,1,0:T(4,128)(2,1)} %reshape.50), calls=%async_computation.1 | async-start | bytes 524288 | tf_op jit(solution)/shard_map/all_to_all | solution.py:364
  397.3 11.2 %all-to-all-done.1 = bf16[64,4,512]{2,1,0:T(4,128)(2,1)S(1)} async-done(((bf16[64,4,512]{2,1,0:T(4,128)(2,1)}), bf16[64,4,512]{2,1,0:T(4,128)(2,1)S(1)}, u32[]{:S(2)}, u32[]{:S(2)}) %all-to-all-start.1) | async-done | bytes 262176 | tf_op jit(solution)/shard_map/all_to_all | solution.py:364
  408.5 0.9 reshape.54
  409.5 0.1 broadcast_select_fusion.1
  409.6 1.4 pad_maximum_fusion
  (23 shorter events, 0.1 us)
Async XLA Ops:
  59.4 12.6 %copy-start.4 = (bf16[512,1024]{1,0:T(8,128)(2,1)S(1)}, bf16[512,1024]{1,0:T(8,128)(2,1)}, u32[]{:S(2)}) copy-start(bf16[512,1024]{1,0:T(8,128)(2,1)} %wo_own.1) | copy-start | bytes 3145732
  59.4 13.1 %copy-start.1 = (s32[28,64]{1,0:T(8,128)S(1)}, s32[28,64]{1,0:T(8,128)}, u32[]{:S(2)}) copy-start(s32[28,64]{1,0:T(8,128)} %param.11) | copy-start | bytes 21508
  59.5 13.2 %copy-start.3 = (s32[28]{0:T(128)S(1)}, s32[28]{0:T(128)}, u32[]{:S(2)}) copy-start(s32[28]{0:T(128)} %param.12) | copy-start | bytes 340
  59.5 228.4 %all-to-all-start = ((bf16[64,64,512]{2,1,0:T(8,128)(2,1)}), bf16[64,64,512]{2,1,0:T(8,128)(2,1)}, u32[]{:S(2)}, u32[]{:S(2)}) async-start(bf16[64,64,512]{2,1,0:T(8,128)(2,1)} %pack_rows.1), calls=%async_computation | async-start | bytes 8388608 | tf_op jit(solution)/shard_map/all_to_all | solution.py:328
  71.4 247.0 %copy-start.2 = (s32[28,4]{0,1:T(4,128)S(1)}, s32[28,4]{0,1:T(4,128)}, u32[]{:S(2)}) copy-start(s32[28,4]{0,1:T(4,128)} %param.13) | copy-start | bytes 1348
  71.4 247.8 %collective-permute-start.3 = (bf16[1024,2048]{1,0:T(8,128)(2,1)}, bf16[1024,2048]{1,0:T(8,128)(2,1)}, u32[]{:S(2)}, u32[]{:S(2)}) collective-permute-start(bf16[1024,2048]{1,0:T(8,128)(2,1)} %wu_own.1), channel_id=1, source_target_pairs={{0,1},{1,0},{2,3},{3,2},{4,5},{5,4},{6,7},{7,6},{8,9},{9,8},{10,11... | collective-permute-start | bytes 12582920 | tf_op jit(solution)/shard_map/ppermute | solution.py:319
  71.5 247.7 %collective-permute-start.4 = (bf16[2048,1024]{1,0:T(8,128)(2,1)}, bf16[2048,1024]{1,0:T(8,128)(2,1)}, u32[]{:S(2)}, u32[]{:S(2)}) collective-permute-start(bf16[2048,1024]{1,0:T(8,128)(2,1)} %wd_own.1), channel_id=1, source_target_pairs={{0,1},{1,0},{2,3},{3,2},{4,5},{5,4},{6,7},{7,6},{8,9},{9,8},{10,11... | collective-permute-start | bytes 12582920 | tf_op jit(solution)/shard_map/ppermute | solution.py:319
  72.0 247.2 %collective-permute-start.1 = (bf16[3,1024,512]{2,1,0:T(8,128)(2,1)}, bf16[3,1024,512]{2,1,0:T(8,128)(2,1)}, u32[]{:S(2)}, u32[]{:S(2)}) collective-permute-start(bf16[3,1024,512]{2,1,0:T(8,128)(2,1)} %bitcast.8.wq_own), channel_id=1, source_target_pairs={{0,1},{1,0},{2,3},{3,2},{4,5},{5,4},{6,7},{7,6},{8,9},{9,8},{10,11... | collective-permute-start | bytes 9437192 | tf_op jit(solution)/shard_map/ppermute | solution.py:319
  72.1 247.1 %collective-permute-start.2 = (bf16[512,1024]{1,0:T(8,128)(2,1)S(1)}, bf16[512,1024]{1,0:T(8,128)(2,1)S(1)}, u32[]{:S(2)}, u32[]{:S(2)}) collective-permute-start(bf16[512,1024]{1,0:T(8,128)(2,1)S(1)} %copy-done.4), channel_id=1, source_target_pairs={{0,1},{1,0},{2,3},{3,2},{4,5},{5,4},{6,7},{7,6},{8,9},{9,8},{10,11... | collective-permute-start | bytes 3145736 | tf_op jit(solution)/shard_map/ppermute | solution.py:319
  317.5 3.1 collective-permute-start
  319.2 1.4 copy-start.5
  388.9 20.5 %copy-start = (bf16[896,512]{1,0:T(8,128)(2,1)S(1)}, bf16[896,512]{1,0:T(8,128)(2,1)}, u32[]{:S(2)}) copy-start(bf16[896,512]{1,0:T(8,128)(2,1)} %get-tuple-element.6) | copy-start | bytes 2752516
  388.9 1.6 collective-permute-start.6
  389.9 19.6 %collective-permute-start.5 = (bf16[896,512]{1,0:T(8,128)(2,1)}, bf16[896,512]{1,0:T(8,128)(2,1)S(1)}, u32[]{:S(2)}, u32[]{:S(2)}) collective-permute-start(bf16[896,512]{1,0:T(8,128)(2,1)} %get-tuple-element.7), channel_id=1, source_target_pairs={{0,1},{1,0},{2,3},{3,2},{4,5},{5,4},{6,7},{7,6},{8,9},{9,8},{10,11... | collective-permute-start | bytes 2752520 | tf_op jit(solution)/shard_map/ppermute | solution.py:347
  392.6 15.8 %all-to-all-start.1 = ((bf16[64,4,512]{2,1,0:T(4,128)(2,1)}), bf16[64,4,512]{2,1,0:T(4,128)(2,1)S(1)}, u32[]{:S(2)}, u32[]{:S(2)}) async-start(bf16[64,4,512]{2,1,0:T(4,128)(2,1)} %reshape.50), calls=%async_computation.1 | async-start | bytes 524288 | tf_op jit(solution)/shard_map/all_to_all | solution.py:364

commit v2 on v1

--- a/solution.py
+++ b/solution.py
@@ -19,6 +19,8 @@
     1.75617062e-09,
 )
 SWAP = [(0, 1), (1, 0)]
+LANES = 128
+FACTS = 8
 
 
 def gelu(x):
@@ -37,10 +39,56 @@
     return centred * lax.rsqrt(var + 1e-05) * gain
 
 
-def pack_kernel(target, tokens, out, sems):
-    rows = tokens.shape[0]
+def pack_kernel(target, tokens, facts, out, staged, sems, fact_sem):
+    rows, seq, width = tokens.shape
+    body = seq * width // LANES
+    fact_copy = pltpu.make_async_copy(facts, out.at[:, pl.ds(body, FACTS)], fact_sem)
+    fact_copy.start()
+    copies = []
+    for r in range(rows):
+        for c in range(width // LANES):
+            staged[r, c * seq : (c + 1) * seq, :] = tokens[r, :, c * LANES : (c + 1) * LANES]
+        copies.append(
+            pltpu.make_async_copy(
+                staged.at[r], out.at[target[r], pl.ds(0, body)], sems.at[r]
+            )
+        )
+        copies[-1].start()
+    for copy in copies:
+        copy.wait()
+    fact_copy.wait()
+
+
+def pack(target, tokens, facts):
+    rows, seq, width = tokens.shape
+    slots = facts.shape[0]
+    body = seq * width // LANES
+    return pl.pallas_call(
+        pack_kernel,
+        out_shape=jax.ShapeDtypeStruct((slots, body + FACTS, LANES), tokens.dtype),
+        in_specs=[
+            pl.BlockSpec(memory_space=pltpu.SMEM),
+            pl.BlockSpec(memory_space=pltpu.VMEM),
+            pl.BlockSpec(memory_space=pltpu.VMEM),
+        ],
+        out_specs=pl.BlockSpec(memory_space=pl.ANY),
+        scratch_shapes=[
+            pltpu.VMEM((rows, body, LANES), tokens.dtype),
+            pltpu.SemaphoreType.DMA((rows,)),
+            pltpu.SemaphoreType.DMA,
+        ],
+        compiler_params=pltpu.CompilerParams(vmem_limit_bytes=16 * 1024 * 1024),
+        name="pack_rows",
+    )(target, tokens, facts)
+
+
+def unpack_kernel(source, received, out, sems):
+    rows, body, _ = out.shape
     copies = [
-        pltpu.make_async_copy(tokens.at[r], out.at[target[r]], sems.at[r]) for r in range(rows)
+        pltpu.make_async_copy(
+            received.at[source[r], pl.ds(0, body)], out.at[r], sems.at[r]
+        )
+        for r in range(rows)
     ]
     for copy in copies:
         copy.start()
@@ -48,44 +96,19 @@
         copy.wait()
 
 
-def pack(target, tokens, slots):
-    rows, seq, width = tokens.shape
+def unpack(source, received):
+    rows = source.shape[0]
+    body = received.shape[1] - FACTS
     return pl.pallas_call(
-        pack_kernel,
-        out_shape=jax.ShapeDtypeStruct((slots, seq, width), tokens.dtype),
+        unpack_kernel,
+        out_shape=jax.ShapeDtypeStruct((rows, body, LANES), received.dtype),
         in_specs=[
             pl.BlockSpec(memory_space=pltpu.SMEM),
             pl.BlockSpec(memory_space=pl.ANY),
         ],
-        out_specs=pl.BlockSpec(memory_space=pl.ANY),
+        out_specs=pl.BlockSpec(memory_space=pltpu.VMEM),
         scratch_shapes=[pltpu.SemaphoreType.DMA((rows,))],
-        name="pack_rows",
-    )(target, tokens)
-
-
-def unpack_kernel(source, received, out, sems):
-    copies = [
-        pltpu.make_async_copy(received.at[source[r]], out.at[r], sems.at[r])
-        for r in range(out.shape[0])
-    ]
-    for copy in copies:
-        copy.start()
-    for copy in copies:
-        copy.wait()
-
-
-def unpack(source, received):
-    rows = source.shape[0]
-    _, seq, width = received.shape
-    return pl.pallas_call(
-        unpack_kernel,
-        out_shape=jax.ShapeDtypeStruct((rows, seq, width), received.dtype),
-        in_specs=[
-            pl.BlockSpec(memory_space=pltpu.SMEM),
-            pl.BlockSpec(memory_space=pl.ANY),
-        ],
-        out_specs=pl.BlockSpec(memory_space=pl.ANY),
-        scratch_shapes=[pltpu.SemaphoreType.DMA((rows,))],
+        compiler_params=pltpu.CompilerParams(vmem_limit_bytes=16 * 1024 * 1024),
         name="unpack_rows",
     )(source, received)
 
@@ -119,7 +142,7 @@
     wu,
     wd,
     row_sems,
-    x_sem,
+    x_sems,
     q_sems,
     w_sems,
 ):
@@ -131,15 +154,25 @@
     me = info[0]
     own_col = pl.multiple_of(me * half, half)
     oth_col = pl.multiple_of((1 - me) * half, half)
-    row_copies = [
-        pltpu.make_async_copy(
-            received.at[info[8 + r]],
-            x_scr.at[pl.ds(r * seq, seq), pl.ds(own_col, half)],
-            row_sems.at[r],
-        )
-        for r in range(rows)
-    ]
-    x_copy = pltpu.make_async_copy(x_other, x_scr.at[:, pl.ds(oth_col, half)], x_sem)
+    row_copies = []
+    x_copies = []
+    for r in range(rows):
+        for c in range(half // LANES):
+            piece = pl.ds(c * seq, seq)
+            lanes = pl.ds(pl.multiple_of(own_col + c * LANES, LANES), LANES)
+            dst = x_scr.at[pl.ds(r * seq, seq), lanes]
+            row_copies.append(
+                pltpu.make_async_copy(received.at[info[8 + r], piece], dst, row_sems.at[r, c])
+            )
+    for c in range(half // LANES):
+        lanes = pl.ds(pl.multiple_of(oth_col + c * LANES, LANES), LANES)
+        for r in range(rows):
+            dst = x_scr.at[pl.ds(r * seq, seq), lanes]
+            x_copies.append(
+                pltpu.make_async_copy(
+                    x_other.at[r, pl.ds(c * seq, seq)], dst, x_sems.at[r, c]
+                )
+            )
     q_copies = [
         pltpu.make_async_copy(ref.at[i], wq.at[3 * h + i], q_sems.at[3 * h + i])
         for h, ref in enumerate((wq_own, wq_oth))
@@ -154,14 +187,10 @@
         pltpu.make_async_copy(wd_own, wd.at[0], w_sems.at[4]),
         pltpu.make_async_copy(wd_oth, wd.at[1], w_sems.at[5]),
     ]
-    for copy in row_copies:
+    for copy in row_copies + x_copies + q_copies + w_copies:
         copy.start()
-    x_copy.start()
-    for copy in q_copies + w_copies:
-        copy.start()
-    for copy in row_copies:
+    for copy in row_copies + x_copies:
         copy.wait()
-    x_copy.wait()
 
     for n in range(6):
         q_copies[n].wait()
@@ -264,8 +293,9 @@
 
 
 def layer(info, received, x_other, weights, gain_attn, gain_ffn):
-    tokens, half = x_other.shape
-    rows = tokens // 64
+    rows, body, _ = x_other.shape
+    half = body * LANES // 64
+    tokens = rows * 64
     model = 2 * half
     wq, wo, wu, wd = weights[0], weights[2], weights[4], weights[6]
     flops = 2 * tokens * model * (3 * model + model + 4 * wu.shape[1])
@@ -292,8 +322,8 @@
             pltpu.VMEM((model, model), jnp.bfloat16),
             pltpu.VMEM((2,) + wu.shape, jnp.bfloat16),
             pltpu.VMEM((2,) + wd.shape, jnp.bfloat16),
-            pltpu.SemaphoreType.DMA((rows,)),
-            pltpu.SemaphoreType.DMA,
+            pltpu.SemaphoreType.DMA((rows, half // LANES)),
+            pltpu.SemaphoreType.DMA((rows, half // LANES)),
             pltpu.SemaphoreType.DMA((6,)),
             pltpu.SemaphoreType.DMA((6,)),
         ],
@@ -311,23 +341,29 @@
     docs = owner.shape[1]
     mine = row_count // 2
     me = lax.axis_index("mp")
-    index = lax.axis_index("dp")
 
     qkv_own = jnp.moveaxis(w_qkv, 1, 0)
     weights = []
     for own in (qkv_own, w_out, w_up, w_down):
         weights += [own, lax.ppermute(own, "mp", SWAP)]
 
-    bounds = jnp.stack([jnp.sum((doc_ids < k).astype(jnp.int32), -1) for k in range(1, docs)], -1)
-    facts = lax.all_gather(jnp.concatenate([dest[:, None], bounds], -1), "dp", axis=0)
+    target = dest // row_count
+    sent = (jnp.arange(devices, dtype=jnp.int32)[:, None] == target[None, :]).astype(jnp.int32)
+    bounds = [jnp.sum((doc_ids < k).astype(jnp.int32), -1) for k in range(1, docs)]
+    fact_list = [dest % row_count + 1] + bounds
+    facts = jnp.stack([jnp.sum(sent * fact[None, :], -1) for fact in fact_list], -1)
+    facts = jnp.broadcast_to(
+        jnp.pad(facts, ((0, 0), (0, LANES - len(fact_list))))[:, None, :].astype(jnp.bfloat16),
+        (devices, FACTS, LANES),
+    )
+    received = lax.all_to_all(
+        pack(target, tokens, facts), "dp", split_axis=0, concat_axis=0, tiled=True
+    )
+    got_facts = received[:, -FACTS, : len(fact_list)].astype(jnp.int32)
     slot = jnp.arange(row_count, dtype=jnp.int32)
-    here = facts[:, :, 0] == (index * row_count + slot)[None, :]
+    here = got_facts[:, :1] == slot[None, :] + 1
     source = jnp.sum(jnp.where(here, jnp.arange(devices, dtype=jnp.int32)[:, None], 0), 0)
-    new_bounds = jnp.sum(jnp.where(here[:, :, None], facts[:, :, 1:], 0), 0)
-
-    received = lax.all_to_all(
-        pack(dest // row_count, tokens, devices), "dp", split_axis=0, concat_axis=0, tiled=True
-    )
+    new_bounds = jnp.sum(jnp.where(here[:, :, None], got_facts[:, None, 1:], 0), 0)
     source_own = lax.dynamic_slice_in_dim(source, me * mine, mine)
     source_oth = lax.dynamic_slice_in_dim(source, (1 - me) * mine, mine)
     bounds_own = lax.dynamic_slice_in_dim(new_bounds, me * mine, mine)
@@ -339,7 +375,7 @@
             jnp.pad(bounds_own, ((0, 0), (0, 1))).reshape(-1),
         ]
     )
-    x_other = lax.ppermute(unpack(source_oth, received), "mp", SWAP).reshape(-1, half)
+    x_other = lax.ppermute(unpack(source_oth, received), "mp", SWAP)
     enc_own, enc_oth, emb_own, emb_oth = layer(
         info, received, x_other, weights, gain_attn[None], gain_ffn[None]
     )

time: 411 us -> 179 us (0.44)
  blocking collectives: 214 us -> 0 us
  Pallas kernels: 156 us -> 73.1 us
  waiting for transfers between devices: 12.8 us -> 65.1 us
  starting transfers between devices: 18.6 us -> 25.7 us
    all_gather x1 -> x0, blocking collectives: 214 us -> none  [shards(): lax.all_gather(jnp.concatenate([dest[:, None], bounds], -1), 'dp', axis=0)]
    pallas_call x2, Pallas kernels: 87.3 us -> 5.52 us  [the longest x1 3.65 us: pack(): pl.pallas_call(pack_kernel, out_shape=jax.ShapeDtypeStruct((slots, body +...]
    all_to_all x1, waiting for transfers between devices: 0.01 us -> 52.9 us  [shards(): lax.all_to_all(pack(target, tokens, facts), 'dp', split_axis=0, concat_ax...]
    all_to_all x1, starting transfers between devices: 4.62 us -> 11.8 us  [shards(): lax.all_to_all(sending.reshape(devices, SLOTS, half), 'dp', split_axis=0,...]
  transfers between devices with their start and end apart: 9 -> 9, of which waited for: 3 -> 4; matrix products, arithmetic and copies ran while one was open for 1% -> 4% of each run, Pallas kernels for 7% -> 1%
where the time goes in v2:
time: 179 us; the launch traced here: 178 us
  Pallas kernels  73.1 us (41%)
  waiting for transfers between devices  65.1 us (36%)
  starting transfers between devices  25.7 us (14%)
  local copies, waits for them, and re-layouts  6.67 us (4%)
  other arithmetic  5.4 us (3%)
    pallas_call x1, Pallas kernels, layer(): pl.pallas_call(layer_kernel, out_shape=(jax.ShapeDtypeStruct((tokens, hal...  67.5 us
    all_to_all x1, waiting for transfers between devices, shards(): lax.all_to_all(pack(target, tokens, facts), 'dp', split_axis=0, concat_ax...  52.9 us
    all_to_all x1, starting transfers between devices, shards(): lax.all_to_all(pack(target, tokens, facts), 'dp', split_axis=0, concat_ax...  11.9 us
    all_to_all x1, starting transfers between devices, shards(): lax.all_to_all(sending.reshape(devices, SLOTS, half), 'dp', split_axis=0,...  11.8 us
    all_to_all x1, waiting for transfers between devices, shards(): lax.all_to_all(sending.reshape(devices, SLOTS, half), 'dp', split_axis=0,...  10.9 us
    unnamed x14, local copies, waits for them, and re-layouts  3.92 us
    pallas_call x1, Pallas kernels, pack(): pl.pallas_call(pack_kernel, out_shape=jax.ShapeDtypeStruct((slots, body +...  3.65 us
  transfers between devices with their start and end apart: 9, of which 4 were waited for; matrix products, arithmetic and copies ran while one was open for 4% of the time, Pallas kernels for 1%

profile of v2, /device:TPU:0, one launch (start us, length us, event | category | flops | bytes accessed | tf_op | source)
XLA Modules:
  0.0 178.1 jit_solution(6575411111749296400)
XLA Ops:
  0.6 0.9 convert_reduce_fusion.3
  1.5 0.7 fusion.7
  2.2 0.1 select_reduce_fusion.5
  2.3 0.1 copy.25
  2.5 1.5 copy-done.1
  4.0 3.7 %pack_rows.1 = bf16[64,264,128]{2,1,0:T(8,128)(2,1)S(1)} custom-call(s32[28]{0:T(128)S(1)} %get-tuple-element.24.target, bf16[28,64,512]{2,1,0:T(8,128)(2,1)S(1)} %copy-done.1, bf16[64,8,128]{2,1,0:T(8,128)(2,1)S(1)} %broadcast_in_dim.37.facts), custom_call_target="tpu_custom_call" | custom-call | tf_op jit(solution)/shard_map/pack_rows/pallas_call | solution.py:66
  7.7 2.0 %copy-done = bf16[64,264,128]{2,1,0:T(8,128)(2,1)} copy-done((bf16[64,264,128]{2,1,0:T(8,128)(2,1)}, bf16[64,264,128]{2,1,0:T(8,128)(2,1)S(1)}, u32[]{:S(2)}) %copy-start) | copy-done | bytes 4325400
  9.6 11.9 %all-to-all-start = ((bf16[64,264,128]{2,1,0:T(8,128)(2,1)}), bf16[64,264,128]{2,1,0:T(8,128)(2,1)}, u32[]{:S(2)}, u32[]{:S(2)}) async-start(bf16[64,264,128]{2,1,0:T(8,128)(2,1)} %copy-done), calls=%async_computation | async-start | bytes 8650752 | tf_op jit(solution)/shard_map/all_to_all | solution.py:359
  21.5 0.1 collective-permute-start.3
  21.6 0.5 collective-permute-start.4
  22.1 0.1 collective-permute-start.1
  22.2 0.4 collective-permute-start.2
  22.6 52.9 %all-to-all-done.received = bf16[64,264,128]{2,1,0:T(8,128)(2,1)} async-done(((bf16[64,264,128]{2,1,0:T(8,128)(2,1)}), bf16[64,264,128]{2,1,0:T(8,128)(2,1)}, u32[]{:S(2)}, u32[]{:S(2)}) %all-to-all-start) | async-done | bytes 4325408 | tf_op jit(solution)/shard_map/all_to_all | solution.py:359
  75.6 0.9 slice_convert_fusion.1
  76.5 0.1 slice_reduce_fusion
  76.6 0.2 select_reduce_fusion.1
  76.8 0.1 fusion.8
  76.9 1.9 %unpack_rows.1 = bf16[14,256,128]{2,1,0:T(8,128)(2,1)S(1)} custom-call(s32[14]{0:T(128)S(1)} %get-tuple-element.21.source, bf16[64,264,128]{2,1,0:T(8,128)(2,1)} %all-to-all-done.received), custom_call_target="tpu_custom_call" | custom-call | tf_op jit(solution)/shard_map/unpack_rows/pallas_call | solution.py:102
  78.7 0.3 collective-permute-start
  79.0 0.1 copy.22
  79.1 0.1 eq.93
  79.2 0.1 slice.18
  79.3 0.1 copy.20
  79.4 0.1 broadcast_compare_fusion
  79.5 0.2 select_reduce_fusion
  79.6 0.1 constant_dynamic-slice_fusion.2
  79.7 0.1 copy.26
  79.8 0.1 reshape.77
  79.9 0.7 pad_add_fusion.info
  80.6 1.0 collective-permute-done.x_other
  81.6 67.5 %layer.1 = (bf16[896,512]{1,0:T(8,128)(2,1)}, bf16[896,512]{1,0:T(8,128)(2,1)}, bf16[112,512]{1,0:T(8,128)(2,1)}, bf16[112,512]{1,0:T(8,128)(2,1)}) custom-call(s32[88]{0:T(128)} %pad_add_fusion.info, bf16[64,264,128]{2,1,0:T(8,128)(2,1)} %all-to-all-done.received, bf16[14,256,128]{2,1,0:T(8,128)(2,1)} %collective-permute-done.x_other, ...), custom_call_target="tpu_custom_call" | custom-call | flops 22548578304 | bytes 29360128 | tf_op jit(solution)/shard_map/layer/pallas_call | solution.py:304
  149.2 0.3 collective-permute-start.6
  149.5 0.2 convert_reduce_fusion
  149.7 0.1 reduce_sum.102
  149.8 0.1 copy.23
  149.9 0.1 mul.61
  150.0 0.1 copy.27
  150.1 0.1 reshape.78
  150.2 0.3 collective-permute-start.5
  150.5 0.2 collective-permute-done.6
  150.8 0.2 fusion.1
  151.0 1.1 fusion
  152.1 0.8 reshape.79
  152.9 11.8 %all-to-all-start.1 = ((bf16[64,4,512]{2,1,0:T(4,128)(2,1)}), bf16[64,4,512]{2,1,0:T(4,128)(2,1)S(1)}, u32[]{:S(2)}, u32[]{:S(2)}) async-start(bf16[64,4,512]{2,1,0:T(4,128)(2,1)} %reshape.79), calls=%async_computation.1 | async-start | bytes 524288 | tf_op jit(solution)/shard_map/all_to_all | solution.py:400
  164.7 10.9 %all-to-all-done.1 = bf16[64,4,512]{2,1,0:T(4,128)(2,1)S(1)} async-done(((bf16[64,4,512]{2,1,0:T(4,128)(2,1)}), bf16[64,4,512]{2,1,0:T(4,128)(2,1)S(1)}, u32[]{:S(2)}, u32[]{:S(2)}) %all-to-all-start.1) | async-done | bytes 262176 | tf_op jit(solution)/shard_map/all_to_all | solution.py:400
  175.6 0.9 reshape.84
  176.6 0.1 broadcast_select_fusion.1
  176.7 1.4 pad_maximum_fusion
  (27 shorter events, 0.2 us)
Async XLA Ops:
  2.5 1.5 copy-start.1
  7.6 2.0 %copy-start = (bf16[64,264,128]{2,1,0:T(8,128)(2,1)}, bf16[64,264,128]{2,1,0:T(8,128)(2,1)S(1)}, u32[]{:S(2)}) copy-start(bf16[64,264,128]{2,1,0:T(8,128)(2,1)S(1)} %pack_rows.1) | copy-start | bytes 12976132
  9.6 12.6 %copy-start.4 = (bf16[512,1024]{1,0:T(8,128)(2,1)S(1)}, bf16[512,1024]{1,0:T(8,128)(2,1)}, u32[]{:S(2)}) copy-start(bf16[512,1024]{1,0:T(8,128)(2,1)} %wo_own.1) | copy-start | bytes 3145732
  9.6 65.9 %all-to-all-start = ((bf16[64,264,128]{2,1,0:T(8,128)(2,1)}), bf16[64,264,128]{2,1,0:T(8,128)(2,1)}, u32[]{:S(2)}, u32[]{:S(2)}) async-start(bf16[64,264,128]{2,1,0:T(8,128)(2,1)} %copy-done), calls=%async_computation | async-start | bytes 8650752 | tf_op jit(solution)/shard_map/all_to_all | solution.py:359
  21.5 57.5 %copy-start.3 = (s32[28,4]{0,1:T(4,128)S(1)}, s32[28,4]{0,1:T(4,128)}, u32[]{:S(2)}) copy-start(s32[28,4]{0,1:T(4,128)} %param.13) | copy-start | bytes 1348
  21.5 59.1 %collective-permute-start.3 = (bf16[1024,2048]{1,0:T(8,128)(2,1)}, bf16[1024,2048]{1,0:T(8,128)(2,1)}, u32[]{:S(2)}, u32[]{:S(2)}) collective-permute-start(bf16[1024,2048]{1,0:T(8,128)(2,1)} %wu_own.1), channel_id=1, source_target_pairs={{0,1},{1,0},{2,3},{3,2},{4,5},{5,4},{6,7},{7,6},{8,9},{9,8},{10,11... | collective-permute-start | bytes 12582920 | tf_op jit(solution)/shard_map/ppermute | solution.py:348
  21.6 59.0 %collective-permute-start.4 = (bf16[2048,1024]{1,0:T(8,128)(2,1)}, bf16[2048,1024]{1,0:T(8,128)(2,1)}, u32[]{:S(2)}, u32[]{:S(2)}) collective-permute-start(bf16[2048,1024]{1,0:T(8,128)(2,1)} %wd_own.1), channel_id=1, source_target_pairs={{0,1},{1,0},{2,3},{3,2},{4,5},{5,4},{6,7},{7,6},{8,9},{9,8},{10,11... | collective-permute-start | bytes 12582920 | tf_op jit(solution)/shard_map/ppermute | solution.py:348
  22.1 58.5 %collective-permute-start.1 = (bf16[3,1024,512]{2,1,0:T(8,128)(2,1)}, bf16[3,1024,512]{2,1,0:T(8,128)(2,1)}, u32[]{:S(2)}, u32[]{:S(2)}) collective-permute-start(bf16[3,1024,512]{2,1,0:T(8,128)(2,1)} %bitcast.5.wq_own), channel_id=1, source_target_pairs={{0,1},{1,0},{2,3},{3,2},{4,5},{5,4},{6,7},{7,6},{8,9},{9,8},{10,11... | collective-permute-start | bytes 9437192 | tf_op jit(solution)/shard_map/ppermute | solution.py:348
  22.2 58.4 %collective-permute-start.2 = (bf16[512,1024]{1,0:T(8,128)(2,1)S(1)}, bf16[512,1024]{1,0:T(8,128)(2,1)}, u32[]{:S(2)}, u32[]{:S(2)}) collective-permute-start(bf16[512,1024]{1,0:T(8,128)(2,1)S(1)} %copy-done.4), channel_id=1, source_target_pairs={{0,1},{1,0},{2,3},{3,2},{4,5},{5,4},{6,7},{7,6},{8,9},{9,8},{10,11... | collective-permute-start | bytes 3145736 | tf_op jit(solution)/shard_map/ppermute | solution.py:348
  78.7 2.9 %collective-permute-start = (bf16[14,256,128]{2,1,0:T(8,128)(2,1)S(1)}, bf16[14,256,128]{2,1,0:T(8,128)(2,1)}, u32[]{:S(2)}, u32[]{:S(2)}) collective-permute-start(bf16[14,256,128]{2,1,0:T(8,128)(2,1)S(1)} %unpack_rows.1), channel_id=1, source_target_pairs={{0,1},{1,0},{2,3},{3,2},{4,5},{5,4},{6,7},{7,6},{8,9},{9,8},{10,11... | collective-permute-start | bytes 2752520 | tf_op jit(solution)/shard_map/ppermute | solution.py:378
  149.2 27.4 %copy-start.2 = (bf16[896,512]{1,0:T(8,128)(2,1)S(1)}, bf16[896,512]{1,0:T(8,128)(2,1)}, u32[]{:S(2)}) copy-start(bf16[896,512]{1,0:T(8,128)(2,1)} %get-tuple-element.6) | copy-start | bytes 2752516
  149.2 1.6 collective-permute-start.6
  150.2 26.4 %collective-permute-start.5 = (bf16[896,512]{1,0:T(8,128)(2,1)}, bf16[896,512]{1,0:T(8,128)(2,1)S(1)}, u32[]{:S(2)}, u32[]{:S(2)}) collective-permute-start(bf16[896,512]{1,0:T(8,128)(2,1)} %get-tuple-element.7), channel_id=1, source_target_pairs={{0,1},{1,0},{2,3},{3,2},{4,5},{5,4},{6,7},{7,6},{8,9},{9,8},{10,11... | collective-permute-start | bytes 2752520 | tf_op jit(solution)/shard_map/ppermute | solution.py:383
  152.9 22.7 %all-to-all-start.1 = ((bf16[64,4,512]{2,1,0:T(4,128)(2,1)}), bf16[64,4,512]{2,1,0:T(4,128)(2,1)S(1)}, u32[]{:S(2)}, u32[]{:S(2)}) async-start(bf16[64,4,512]{2,1,0:T(4,128)(2,1)} %reshape.79), calls=%async_computation.1 | async-start | bytes 524288 | tf_op jit(solution)/shard_map/all_to_all | solution.py:400

commit v3 on v2

v3 whole, which is shorter than its diff:
```python
import math

import jax
import jax.numpy as jnp
from jax import lax
from jax.experimental import pallas as pl
from jax.experimental.pallas import tpu as pltpu
from jax.sharding import PartitionSpec as P

HD = 64
TILE = 1024
PART = 448
SLOTS = 4
SWAP = [(0, 1), (1, 0)]
LANES = 128
FACTS = 8


def gelu(x):
    half = 0.5 * x
    return half + half * lax.erf(x * math.sqrt(0.5))


def norm(values, gain):
    mean = jnp.mean(values, -1, keepdims=True)
    centred = values - mean
    var = jnp.mean(centred * centred, -1, keepdims=True)
    return centred * lax.rsqrt(var + 1e-05) * gain


def pack_kernel(target, tokens, facts, out, staged, sems, fact_sem):
    rows, seq, width = tokens.shape
    body = seq * width // LANES
    fact_copy = pltpu.make_async_copy(facts, out.at[:, pl.ds(body, FACTS)], fact_sem)
    fact_copy.start()
    copies = []
    for r in range(rows):
        for c in range(width // LANES):
            staged[r, c * seq : (c + 1) * seq, :] = tokens[r, :, c * LANES : (c + 1) * LANES]
        copies.append(
            pltpu.make_async_copy(
                staged.at[r], out.at[target[r], pl.ds(0, body)], sems.at[r]
            )
        )
        copies[-1].start()
    for copy in copies:
        copy.wait()
    fact_copy.wait()


def pack(target, tokens, facts):
    rows, seq, width = tokens.shape
    slots = facts.shape[0]
    body = seq * width // LANES
    return pl.pallas_call(
        pack_kernel,
        out_shape=jax.ShapeDtypeStruct((slots, body + FACTS, LANES), tokens.dtype),
        in_specs=[
            pl.BlockSpec(memory_space=pltpu.SMEM),
            pl.BlockSpec(memory_space=pltpu.VMEM),
            pl.BlockSpec(memory_space=pltpu.VMEM),
        ],
        out_specs=pl.BlockSpec(memory_space=pl.ANY),
        scratch_shapes=[
            pltpu.VMEM((rows, body, LANES), tokens.dtype),
            pltpu.SemaphoreType.DMA((rows,)),
            pltpu.SemaphoreType.DMA,
        ],
        compiler_params=pltpu.CompilerParams(vmem_limit_bytes=16 * 1024 * 1024),
        name="pack_rows",
    )(target, tokens, facts)


def unpack_kernel(source, received, out, sems):
    rows, body, _ = out.shape
    copies = [
        pltpu.make_async_copy(
            received.at[source[r], pl.ds(0, body)], out.at[r], sems.at[r]
        )
        for r in range(rows)
    ]
    for copy in copies:
        copy.start()
    for copy in copies:
        copy.wait()


def unpack(source, received):
    rows = source.shape[0]
    body = received.shape[1] - FACTS
    return pl.pallas_call(
        unpack_kernel,
        out_shape=jax.ShapeDtypeStruct((rows, body, LANES), received.dtype),
        in_specs=[
            pl.BlockSpec(memory_space=pltpu.SMEM),
            pl.BlockSpec(memory_space=pl.ANY),
        ],
        out_specs=pl.BlockSpec(memory_space=pltpu.VMEM),
        scratch_shapes=[pltpu.SemaphoreType.DMA((rows,))],
        compiler_params=pltpu.CompilerParams(vmem_limit_bytes=16 * 1024 * 1024),
        name="unpack_rows",
    )(source, received)


def layer_kernel(
    info,
    received,
    x_other,
    wq_own,
    wq_oth,
    wo_own,
    wo_oth,
    wu_own,
    wu_oth,
    wd_own,
    wd_oth,
    gain_attn,
    gain_ffn,
    enc_own,
    enc_oth,
    emb,
    x_scr,
    qkv_scr,
    acc_scr,
    wu,
    wd,
    row_sems,
    x_sem,
    w_sems,
    out_sems,
):
    rows = x_scr.shape[0]
    seq = HD
    tokens, half = enc_own.shape
    model = 2 * half
    chunks = model // LANES
    body = half * seq // LANES
    me = info[0]
    own_at = pl.ds(pl.multiple_of(me * body, body), body)
    oth_at = pl.ds(pl.multiple_of((1 - me) * body, body), body)
    x_copies = [
        pltpu.make_async_copy(
            received.at[info[8 + r], pl.ds(0, body)], x_scr.at[r, own_at], row_sems.at[r]
        )
        for r in range(rows)
    ]
    x_copies.append(pltpu.make_async_copy(x_other, x_scr.at[:, oth_at], x_sem))
    w_copies = [
        pltpu.make_async_copy(src, dst.at[h], w_sems.at[i, h])
        for h, srcs in enumerate(((wu_own, wd_own), (wu_oth, wd_oth)))
        for i, (src, dst) in enumerate(zip(srcs, (wu, wd)))
    ]
    for copy in x_copies:
        copy.start()
    for copy in x_copies:
        copy.wait()
    for copy in w_copies:
        copy.start()

    def inputs(first, count):
        pieces = [
            x_scr[pl.ds(first, count), c * seq : (c + 1) * seq, :].reshape(count * seq, LANES)
            for c in range(chunks)
        ]
        return jnp.concatenate(pieces, 1)

    for h, wq in enumerate((wq_own, wq_oth)):
        for i in range(3):
            n = 3 * h + i
            qkv_scr[:, n * half : (n + 1) * half] = jnp.dot(
                inputs(0, rows), wq[i], preferred_element_type=jnp.float32
            ).astype(jnp.bfloat16)

    pair = 2 * HD
    block = (lax.broadcasted_iota(jnp.int32, (pair, pair), 0) < HD) == (
        lax.broadcasted_iota(jnp.int32, (pair, pair), 1) < HD
    )
    lane_low = lax.broadcasted_iota(jnp.int32, (seq, pair), 1) < HD
    key_pos = lax.broadcasted_iota(jnp.int32, (seq, pair), 0)
    query_pos = lax.broadcasted_iota(jnp.int32, (seq, pair), 1) % HD
    per_half = half // pair

    def attend(r, carry):
        here = pl.ds(pl.multiple_of(r * seq, seq), seq)
        bounds = [info[32 + 4 * r + i] for i in range(3)]
        key_seg = sum([(key_pos >= b).astype(jnp.int32) for b in bounds])
        query_seg = sum([(query_pos >= b).astype(jnp.int32) for b in bounds])
        same = key_seg == query_seg
        scores = []
        for p in range(2 * per_half):
            at = (p // per_half) * 3 * half + (p % per_half) * pair
            q = qkv_scr[here, at : at + pair]
            k = qkv_scr[here, at + half : at + half + pair]
            spread = jnp.where(block, jnp.concatenate([q, q], 0), jnp.zeros((), q.dtype))
            scores.append(
                lax.dot_general(
                    k, spread, (((1,), (1,)), ((), ())), preferred_element_type=jnp.float32
                )
            )
        probs = []
        for score in scores:
            score = jnp.where(same, score * (1.0 / math.sqrt(HD)), jnp.float32(-1e30))
            weight = jnp.exp(score - jnp.max(score, 0, keepdims=True))
            probs.append(
                (weight * (1.0 / jnp.sum(weight, 0, keepdims=True))).astype(jnp.bfloat16)
            )
        mixed = []
        for p in range(2 * per_half):
            at = (p // per_half) * 3 * half + 2 * half + (p % per_half) * pair
            mixed.append(
                lax.dot_general(
                    probs[p],
                    qkv_scr[here, at : at + pair],
                    (((0,), (0,)), ((), ())),
                    preferred_element_type=jnp.float32,
                )
            )
        for p in range(2 * per_half):
            at = (p // per_half) * 3 * half + (p % per_half) * pair
            qkv_scr[here, at : at + pair] = jnp.where(
                lane_low, mixed[p][:seq], mixed[p][seq:]
            ).astype(jnp.bfloat16)
        return carry

    lax.fori_loop(0, rows, attend, 0)

    count = 2
    for m in range(rows // count):
        at = slice(m * count * seq, (m + 1) * count * seq)
        mixed = jnp.dot(qkv_scr[at, :half], wo_own[...], preferred_element_type=jnp.float32)
        mixed += jnp.dot(
            qkv_scr[at, 3 * half : 4 * half], wo_oth[...], preferred_element_type=jnp.float32
        )
        mixed = mixed + inputs(m * count, count).astype(jnp.float32)
        normed = norm(mixed, gain_attn[...]).astype(jnp.bfloat16)
        qkv_scr[at, half : 3 * half] = normed
        acc_scr[at, :] = normed.astype(jnp.float32)

    for copy in w_copies:
        copy.wait()
    tiles = wu.shape[2] // TILE
    parts = tokens // PART

    def feed(t, carry):
        h = t // (tiles * parts)
        at = pl.ds(pl.multiple_of((t % tiles) * TILE, TILE), TILE)
        here = pl.ds(pl.multiple_of((t // tiles) % parts * PART, PART), PART)
        normed = qkv_scr[here, half : 3 * half]
        up = jnp.dot(normed, wu[h, :, at], preferred_element_type=jnp.float32)
        acc_scr[here, :] += jnp.dot(
            gelu(up).astype(jnp.bfloat16), wd[h, at, :], preferred_element_type=jnp.float32
        )
        return carry

    lax.fori_loop(0, 2 * tiles * parts, feed, 0)

    doc_iota = lax.broadcasted_iota(jnp.int32, (8, seq), 0)
    pos_iota = lax.broadcasted_iota(jnp.int32, (8, seq), 1)
    for r in range(rows):
        at = slice(r * seq, (r + 1) * seq)
        encoded = norm(acc_scr[at, :], gain_ffn[...]).astype(jnp.bfloat16)
        qkv_scr[at, : 2 * half] = encoded
        bounds = [info[32 + 4 * r + i] for i in range(3)]
        seg = sum([(pos_iota >= b).astype(jnp.int32) for b in bounds])
        member = (seg == doc_iota).astype(jnp.float32)
        total = jnp.sum(member, -1, keepdims=True)
        pooled = jnp.dot(member.astype(jnp.bfloat16), encoded, preferred_element_type=jnp.float32)
        pooled = pooled * (1.0 / jnp.maximum(total, 1.0))
        square = jnp.mean(pooled * pooled, -1, keepdims=True)
        embedded = pooled * lax.rsqrt(square + 1e-06)
        emb[me, r * 8 : (r + 1) * 8, :] = embedded[:, :half]
        emb[1 - me, r * 8 : (r + 1) * 8, :] = embedded[:, half:]
    own_col = pl.ds(pl.multiple_of(me * half, half), half)
    oth_col = pl.ds(pl.multiple_of((1 - me) * half, half), half)
    outs = [
        pltpu.make_async_copy(qkv_scr.at[:, own_col], enc_own, out_sems.at[0]),
        pltpu.make_async_copy(qkv_scr.at[:, oth_col], enc_oth, out_sems.at[1]),
    ]
    for copy in outs:
        copy.start()
    for copy in outs:
        copy.wait()


def layer(info, received, x_other, weights, gain_attn, gain_ffn):
    rows, body, _ = x_other.shape
    half = body * LANES // HD
    tokens = rows * HD
    model = 2 * half
    wu, wd = weights[4], weights[6]
    flops = 2 * tokens * model * (3 * model + model + 4 * wu.shape[1])
    any_spec = pl.BlockSpec(memory_space=pl.ANY)
    vmem = pl.BlockSpec(memory_space=pltpu.VMEM)
    return pl.pallas_call(
        layer_kernel,
        out_shape=(
            jax.ShapeDtypeStruct((tokens, half), jnp.bfloat16),
            jax.ShapeDtypeStruct((tokens, half), jnp.bfloat16),
            jax.ShapeDtypeStruct((2, rows * 8, half), jnp.float32),
        ),
        in_specs=[pl.BlockSpec(memory_space=pltpu.SMEM)]
        + [any_spec] * 2 + [vmem] * 4 + [any_spec] * 4 + [vmem] * 2,
        out_specs=(any_spec, any_spec, vmem),
        scratch_shapes=[
            pltpu.VMEM((rows, 2 * body, LANES), jnp.bfloat16),
            pltpu.VMEM((tokens, 3 * model), jnp.bfloat16),
            pltpu.VMEM((tokens, model), jnp.float32),
            pltpu.VMEM((2,) + wu.shape, jnp.bfloat16),
            pltpu.VMEM((2,) + wd.shape, jnp.bfloat16),
            pltpu.SemaphoreType.DMA((rows,)),
            pltpu.SemaphoreType.DMA,
            pltpu.SemaphoreType.DMA((2, 2)),
            pltpu.SemaphoreType.DMA((2,)),
        ],
        compiler_params=pltpu.CompilerParams(vmem_limit_bytes=46 * 1024 * 1024),
        cost_estimate=pl.CostEstimate(
            flops=flops, bytes_accessed=28 * 1024 * 1024, transcendentals=0
        ),
        name="layer",
    )(info, received, x_other, *weights, gain_attn, gain_ffn)


def shards(tokens, doc_ids, dest, owner, w_qkv, w_out, gain_attn, w_up, w_down, gain_ffn):
    devices = lax.axis_size("dp")
    row_count, seq, half = tokens.shape
    docs = owner.shape[1]
    mine = row_count // 2
    me = lax.axis_index("mp")

    qkv_own = jnp.moveaxis(w_qkv, 1, 0)
    weights = []
    for own in (qkv_own, w_out, w_up, w_down):
        weights += [own, lax.ppermute(own, "mp", SWAP)]

    target = dest // row_count
    sent = (jnp.arange(devices, dtype=jnp.int32)[:, None] == target[None, :]).astype(jnp.int32)
    bounds = [jnp.sum((doc_ids < k).astype(jnp.int32), -1) for k in range(1, docs)]
    fact_list = [dest % row_count + 1] + bounds
    facts = jnp.stack([jnp.sum(sent * fact[None, :], -1) for fact in fact_list], -1)
    facts = jnp.broadcast_to(
        jnp.pad(facts, ((0, 0), (0, LANES - len(fact_list))))[:, None, :].astype(jnp.bfloat16),
        (devices, FACTS, LANES),
    )
    received = lax.all_to_all(
        pack(target, tokens, facts), "dp", split_axis=0, concat_axis=0, tiled=True
    )
    got_facts = received[:, -FACTS, : len(fact_list)].astype(jnp.int32)
    slot = jnp.arange(row_count, dtype=jnp.int32)
    here = got_facts[:, :1] == slot[None, :] + 1
    source = jnp.sum(jnp.where(here, jnp.arange(devices, dtype=jnp.int32)[:, None], 0), 0)
    new_bounds = jnp.sum(jnp.where(here[:, :, None], got_facts[:, None, 1:], 0), 0)
    source_own = lax.dynamic_slice_in_dim(source, me * mine, mine)
    source_oth = lax.dynamic_slice_in_dim(source, (1 - me) * mine, mine)
    bounds_own = lax.dynamic_slice_in_dim(new_bounds, me * mine, mine)
    info = jnp.concatenate(
        [
            jnp.full((8,), me, jnp.int32),
            source_own,
            jnp.zeros((24 - mine,), jnp.int32),
            jnp.pad(bounds_own, ((0, 0), (0, 1))).reshape(-1),
        ]
    )
    x_other = lax.ppermute(unpack(source_oth, received), "mp", SWAP)
    enc_own, enc_oth, emb = layer(
        info, received, x_other, weights, gain_attn[None], gain_ffn[None]
    )
    emb = emb.astype(jnp.bfloat16)
    emb_recv = lax.ppermute(emb[1], "mp", SWAP)
    enc_recv = lax.ppermute(enc_oth, "mp", SWAP)

    owners = owner.reshape(-1)
    position = jnp.arange(row_count * docs, dtype=jnp.int32)
    earlier = (owners[:, None] == owners[None, :]) & (position[None, :] < position[:, None])
    rank = jnp.sum(earlier.astype(jnp.int32), -1)
    target = jnp.pad(
        (owners * SLOTS + rank).reshape(2, mine, docs), ((0, 0), (0, 0), (0, 8 - docs)),
        constant_values=-1,
    ).reshape(2, mine * 8)
    out_slot = jnp.arange(devices * SLOTS, dtype=jnp.int32)[:, None]
    place_own = (lax.dynamic_index_in_dim(target, me, 0) == out_slot).astype(jnp.bfloat16)
    place_oth = (lax.dynamic_index_in_dim(target, 1 - me, 0) == out_slot).astype(jnp.bfloat16)
    sending = (
        jnp.dot(place_own, emb[0], preferred_element_type=jnp.float32)
        + jnp.dot(place_oth, emb_recv, preferred_element_type=jnp.float32)
    ).astype(jnp.bfloat16)
    got = lax.all_to_all(
        sending.reshape(devices, SLOTS, half), "dp", split_axis=0, concat_axis=0, tiled=True
    )
    index_part = got[:, : SLOTS - 1].astype(jnp.float32).reshape(1, devices * (SLOTS - 1), half)

    enc_own = enc_own.reshape(mine, seq, half)
    enc_recv = enc_recv.reshape(mine, seq, half)
    first = me == 0
    encoded = jnp.concatenate(
        [jnp.where(first, enc_own, enc_recv), jnp.where(first, enc_recv, enc_own)], 0
    )
    return (encoded, index_part)


def solution(mesh):
    return jax.shard_map(
        shards,
        mesh=mesh,
        in_specs=(
            P("dp", None, "mp"),
            P("dp", None),
            P("dp"),
            P("dp", None),
            P(None, None, "mp"),
            P("mp", None),
            P(),
            P(None, "mp"),
            P("mp", None),
            P(),
        ),
        out_specs=(P("dp", None, "mp"), P("dp", None, "mp")),
        check_vma=False,
    )
```

time: 179 us -> 150 us (0.84)
  Pallas kernels: 73.1 us -> 45.9 us
    pallas_call x1, Pallas kernels: 67.5 us -> 40.4 us  [layer(): pl.pallas_call(layer_kernel, out_shape=(jax.ShapeDtypeStruct((tokens, hal...]
    unnamed x14 -> x16, local copies, waits for them, and re-layouts: 3.92 us -> 3.92 us
  transfers between devices with their start and end apart: 9 -> 9, of which waited for: 4 -> 4; matrix products, arithmetic and copies ran while one was open for 4% -> 3% of each run, Pallas kernels for 1% -> 1%
where the time goes in v3:
time: 150 us
  waiting for transfers between devices  65.3 us (44%)
  Pallas kernels  45.9 us (31%)
  starting transfers between devices  25.6 us (17%)
  local copies, waits for them, and re-layouts  6.68 us (4%)
  other arithmetic  4.97 us (3%)
    all_to_all x1, waiting for transfers between devices, shards(): lax.all_to_all(pack(target, tokens, facts), 'dp', split_axis=0, concat_ax...  52.7 us
    pallas_call x1, Pallas kernels, layer(): pl.pallas_call(layer_kernel, out_shape=(jax.ShapeDtypeStruct((tokens, hal...  40.4 us
    all_to_all x1, starting transfers between devices, shards(): lax.all_to_all(pack(target, tokens, facts), 'dp', split_axis=0, concat_ax...  11.9 us
    all_to_all x1, starting transfers between devices, shards(): lax.all_to_all(sending.reshape(devices, SLOTS, half), 'dp', split_axis=0,...  11.8 us
    all_to_all x1, waiting for transfers between devices, shards(): lax.all_to_all(sending.reshape(devices, SLOTS, half), 'dp', split_axis=0,...  10.9 us
    unnamed x16, local copies, waits for them, and re-layouts  3.92 us
    pallas_call x1, Pallas kernels, pack(): pl.pallas_call(pack_kernel, out_shape=jax.ShapeDtypeStruct((slots, body +...  3.65 us
  transfers between devices with their start and end apart: 9, of which 4 were waited for; matrix products, arithmetic and copies ran while one was open for 3% of the time, Pallas kernels for 1%

profile of v3, /device:TPU:0, one launch (start us, length us, event | category | flops | bytes accessed | tf_op | source)
XLA Modules:
  0.0 149.8 jit_solution(5682196623517966247)
XLA Ops:
  0.6 0.9 convert_reduce_fusion.3
  1.5 0.7 fusion.7
  2.2 0.1 select_reduce_fusion.5
  2.3 0.1 copy.25
  2.5 1.5 copy-done.1
  4.0 3.7 %pack_rows.1 = bf16[64,264,128]{2,1,0:T(8,128)(2,1)S(1)} custom-call(s32[28]{0:T(128)S(1)} %get-tuple-element.22.target, bf16[28,64,512]{2,1,0:T(8,128)(2,1)S(1)} %copy-done.1, bf16[64,8,128]{2,1,0:T(8,128)(2,1)S(1)} %broadcast_in_dim.37.facts), custom_call_target="tpu_custom_call" | custom-call | tf_op jit(solution)/shard_map/pack_rows/pallas_call | solution.py:55
  7.7 2.0 %copy-done = bf16[64,264,128]{2,1,0:T(8,128)(2,1)} copy-done((bf16[64,264,128]{2,1,0:T(8,128)(2,1)}, bf16[64,264,128]{2,1,0:T(8,128)(2,1)S(1)}, u32[]{:S(2)}) %copy-start) | copy-done | bytes 4325400
  9.7 11.9 %all-to-all-start = ((bf16[64,264,128]{2,1,0:T(8,128)(2,1)}), bf16[64,264,128]{2,1,0:T(8,128)(2,1)}, u32[]{:S(2)}, u32[]{:S(2)}) async-start(bf16[64,264,128]{2,1,0:T(8,128)(2,1)} %copy-done), calls=%async_computation | async-start | bytes 8650752 | tf_op jit(solution)/shard_map/all_to_all | solution.py:344
  21.5 0.1 collective-permute-start.3
  21.6 0.5 collective-permute-start.4
  22.1 0.1 collective-permute-start.1
  22.2 0.4 collective-permute-start.2
  22.6 0.1 copy.22
  22.7 0.1 eq.93
  22.9 52.7 %all-to-all-done.received = bf16[64,264,128]{2,1,0:T(8,128)(2,1)} async-done(((bf16[64,264,128]{2,1,0:T(8,128)(2,1)}), bf16[64,264,128]{2,1,0:T(8,128)(2,1)}, u32[]{:S(2)}, u32[]{:S(2)}) %all-to-all-start) | async-done | bytes 4325408 | tf_op jit(solution)/shard_map/all_to_all | solution.py:344
  75.6 0.9 slice_convert_fusion.1
  76.5 0.1 slice_reduce_fusion
  76.6 0.2 select_reduce_fusion.1
  76.8 0.1 fusion.8
  76.9 1.9 %unpack_rows.1 = bf16[14,256,128]{2,1,0:T(8,128)(2,1)S(1)} custom-call(s32[14]{0:T(128)S(1)} %get-tuple-element.19.source, bf16[64,264,128]{2,1,0:T(8,128)(2,1)} %all-to-all-done.received), custom_call_target="tpu_custom_call" | custom-call | tf_op jit(solution)/shard_map/unpack_rows/pallas_call | solution.py:91
  78.8 0.3 collective-permute-start
  79.0 0.2 convert_reduce_fusion
  79.2 0.1 reduce_sum.102
  79.3 0.1 copy.23
  79.4 0.1 mul.61
  79.5 0.1 copy.27
  79.6 0.1 reshape.78
  79.7 0.1 slice.26
  79.8 0.1 copy.20
  79.9 0.1 broadcast_compare_fusion
  80.0 0.2 select_reduce_fusion
  80.1 0.1 constant_dynamic-slice_fusion.2
  80.2 0.1 copy.26
  80.3 0.1 reshape.77
  80.4 0.1 pad_add_fusion.info
  80.5 1.1 collective-permute-done.x_other
  81.6 40.4 %layer.1 = (bf16[896,512]{1,0:T(8,128)(2,1)S(1)}, bf16[896,512]{1,0:T(8,128)(2,1)}, f32[2,112,512]{2,1,0:T(8,128)S(1)}) custom-call(s32[88]{0:T(128)S(1)} %pad_add_fusion.info, bf16[64,264,128]{2,1,0:T(8,128)(2,1)} %all-to-all-done.received, bf16[14,256,128]{2,1,0:T(8,128)(2,1)} %collective-permute-done.x_other, bf16[3,1024,512]{2,1,0:T(8,128)(2,1)} %bitcast.33, ...), custom_call_target="tpu_custom_call" | custom-call | flops 22548578304 | bytes 29360128 | tf_op jit(solution)/shard_map/layer/pallas_call | solution.py:294
  122.1 0.2 collective-permute-start.6
  122.3 0.4 collective-permute-start.5
  122.7 0.2 fusion.1
  122.9 0.6 collective-permute-done.6
  123.5 0.2 fusion
  123.7 0.8 reshape.79
  124.5 11.8 %all-to-all-start.1 = ((bf16[64,4,512]{2,1,0:T(4,128)(2,1)}), bf16[64,4,512]{2,1,0:T(4,128)(2,1)S(1)}, u32[]{:S(2)}, u32[]{:S(2)}) async-start(bf16[64,4,512]{2,1,0:T(4,128)(2,1)} %reshape.79), calls=%async_computation.1 | async-start | bytes 524288 | tf_op jit(solution)/shard_map/all_to_all | solution.py:386
  136.3 10.9 %all-to-all-done.1 = bf16[64,4,512]{2,1,0:T(4,128)(2,1)S(1)} async-done(((bf16[64,4,512]{2,1,0:T(4,128)(2,1)}), bf16[64,4,512]{2,1,0:T(4,128)(2,1)S(1)}, u32[]{:S(2)}, u32[]{:S(2)}) %all-to-all-start.1) | async-done | bytes 262176 | tf_op jit(solution)/shard_map/all_to_all | solution.py:386
  147.2 0.9 reshape.84
  148.1 0.2 broadcast_select_fusion.1
  148.4 1.4 pad_maximum_fusion
  (31 shorter events, 0.2 us)
Async XLA Ops:
  2.5 1.5 %copy-start.1 = (bf16[28,64,512]{2,1,0:T(8,128)(2,1)S(1)}, bf16[28,64,512]{2,1,0:T(8,128)(2,1)}, u32[]{:S(2)}) copy-start(bf16[28,64,512]{2,1,0:T(8,128)(2,1)} %tokens.1) | copy-start | bytes 5505028
  7.6 2.0 %copy-start = (bf16[64,264,128]{2,1,0:T(8,128)(2,1)}, bf16[64,264,128]{2,1,0:T(8,128)(2,1)S(1)}, u32[]{:S(2)}) copy-start(bf16[64,264,128]{2,1,0:T(8,128)(2,1)S(1)} %pack_rows.1) | copy-start | bytes 12976132
  9.6 12.6 %copy-start.2 = (bf16[512,1024]{1,0:T(8,128)(2,1)S(1)}, bf16[512,1024]{1,0:T(8,128)(2,1)}, u32[]{:S(2)}) copy-start(bf16[512,1024]{1,0:T(8,128)(2,1)} %wo_own.1) | copy-start | bytes 3145732
  9.6 13.0 %copy-start.5 = (s32[28,4]{0,1:T(4,128)S(1)}, s32[28,4]{0,1:T(4,128)}, u32[]{:S(2)}) copy-start(s32[28,4]{0,1:T(4,128)} %param.13) | copy-start | bytes 1348
  9.7 65.9 %all-to-all-start = ((bf16[64,264,128]{2,1,0:T(8,128)(2,1)}), bf16[64,264,128]{2,1,0:T(8,128)(2,1)}, u32[]{:S(2)}, u32[]{:S(2)}) async-start(bf16[64,264,128]{2,1,0:T(8,128)(2,1)} %copy-done), calls=%async_computation | async-start | bytes 8650752 | tf_op jit(solution)/shard_map/all_to_all | solution.py:344
  21.5 60.1 %copy-start.3 = (f32[1024]{0:T(1024)S(1)}, f32[1024]{0:T(1024)}, u32[]{:S(2)}) copy-start(f32[1024]{0:T(1024)} %param.16) | copy-start | bytes 12292
  21.5 60.1 %copy-start.4 = (f32[1024]{0:T(1024)S(1)}, f32[1024]{0:T(1024)}, u32[]{:S(2)}) copy-start(f32[1024]{0:T(1024)} %param.19) | copy-start | bytes 12292
  21.5 59.0 %collective-permute-start.3 = (bf16[1024,2048]{1,0:T(8,128)(2,1)}, bf16[1024,2048]{1,0:T(8,128)(2,1)}, u32[]{:S(2)}, u32[]{:S(2)}) collective-permute-start(bf16[1024,2048]{1,0:T(8,128)(2,1)} %wu_own.1), channel_id=1, source_target_pairs={{0,1},{1,0},{2,3},{3,2},{4,5},{5,4},{6,7},{7,6},{8,9},{9,8},{10,11... | collective-permute-start | bytes 12582920 | tf_op jit(solution)/shard_map/ppermute | solution.py:333
  21.6 58.9 %collective-permute-start.4 = (bf16[2048,1024]{1,0:T(8,128)(2,1)}, bf16[2048,1024]{1,0:T(8,128)(2,1)}, u32[]{:S(2)}, u32[]{:S(2)}) collective-permute-start(bf16[2048,1024]{1,0:T(8,128)(2,1)} %wd_own.1), channel_id=1, source_target_pairs={{0,1},{1,0},{2,3},{3,2},{4,5},{5,4},{6,7},{7,6},{8,9},{9,8},{10,11... | collective-permute-start | bytes 12582920 | tf_op jit(solution)/shard_map/ppermute | solution.py:333
  22.1 58.4 %collective-permute-start.1 = (bf16[3,1024,512]{2,1,0:T(8,128)(2,1)}, bf16[3,1024,512]{2,1,0:T(8,128)(2,1)}, u32[]{:S(2)}, u32[]{:S(2)}) collective-permute-start(bf16[3,1024,512]{2,1,0:T(8,128)(2,1)} %bitcast.32), channel_id=1, source_target_pairs={{0,1},{1,0},{2,3},{3,2},{4,5},{5,4},{6,7},{7,6},{8,9},{9,8},{10,11... | collective-permute-start | bytes 9437192 | tf_op jit(solution)/shard_map/ppermute | solution.py:333
  22.2 58.3 %collective-permute-start.2 = (bf16[512,1024]{1,0:T(8,128)(2,1)S(1)}, bf16[512,1024]{1,0:T(8,128)(2,1)S(1)}, u32[]{:S(2)}, u32[]{:S(2)}) collective-permute-start(bf16[512,1024]{1,0:T(8,128)(2,1)S(1)} %copy-done.2), channel_id=1, source_target_pairs={{0,1},{1,0},{2,3},{3,2},{4,5},{5,4},{6,7},{7,6},{8,9},{9,8},{10,11... | collective-permute-start | bytes 3145736 | tf_op jit(solution)/shard_map/ppermute | solution.py:333
  78.8 2.9 %collective-permute-start = (bf16[14,256,128]{2,1,0:T(8,128)(2,1)S(1)}, bf16[14,256,128]{2,1,0:T(8,128)(2,1)}, u32[]{:S(2)}, u32[]{:S(2)}) collective-permute-start(bf16[14,256,128]{2,1,0:T(8,128)(2,1)S(1)} %unpack_rows.1), channel_id=1, source_target_pairs={{0,1},{1,0},{2,3},{3,2},{4,5},{5,4},{6,7},{7,6},{8,9},{9,8},{10,11... | collective-permute-start | bytes 2752520 | tf_op jit(solution)/shard_map/ppermute | solution.py:363
  122.1 1.4 collective-permute-start.6
  122.3 25.9 %collective-permute-start.5 = (bf16[896,512]{1,0:T(8,128)(2,1)}, bf16[896,512]{1,0:T(8,128)(2,1)S(1)}, u32[]{:S(2)}, u32[]{:S(2)}) collective-permute-start(bf16[896,512]{1,0:T(8,128)(2,1)} %get-tuple-element.6), channel_id=1, source_target_pairs={{0,1},{1,0},{2,3},{3,2},{4,5},{5,4},{6,7},{7,6},{8,9},{9,8},{10,11... | collective-permute-start | bytes 2752520 | tf_op jit(solution)/shard_map/ppermute | solution.py:369
  124.5 22.7 %all-to-all-start.1 = ((bf16[64,4,512]{2,1,0:T(4,128)(2,1)}), bf16[64,4,512]{2,1,0:T(4,128)(2,1)S(1)}, u32[]{:S(2)}, u32[]{:S(2)}) async-start(bf16[64,4,512]{2,1,0:T(4,128)(2,1)} %reshape.79), calls=%async_computation.1 | async-start | bytes 524288 | tf_op jit(solution)/shard_map/all_to_all | solution.py:386

commit v4 on v3

--- a/solution.py
+++ b/solution.py
@@ -28,29 +28,44 @@
     return centred * lax.rsqrt(var + 1e-05) * gain
 
 
-def pack_kernel(target, tokens, facts, out, staged, sems, fact_sem):
+def pack_kernel(dest, doc_ids, tokens, out, raw, staged, empty, in_sems, out_sems, empty_sem):
     rows, seq, width = tokens.shape
     body = seq * width // LANES
-    fact_copy = pltpu.make_async_copy(facts, out.at[:, pl.ds(body, FACTS)], fact_sem)
-    fact_copy.start()
-    copies = []
+    loads = [pltpu.make_async_copy(tokens.at[r], raw.at[r], in_sems.at[r]) for r in range(rows)]
+    for copy in loads:
+        copy.start()
+    empty[...] = jnp.zeros_like(empty)
+    clear = pltpu.make_async_copy(empty, out.at[:, pl.ds(body, FACTS)], empty_sem)
+    clear.start()
+    lane = lax.broadcasted_iota(jnp.int32, (rows, LANES), 1)
+    facts = jnp.where(lane == 0, lax.broadcasted_iota(jnp.int32, (rows, LANES), 0) + 1, 0)
+    ids = doc_ids[...]
+    for k in range(1, 4):
+        bound = jnp.sum((ids < k).astype(jnp.float32), -1, keepdims=True).astype(jnp.int32)
+        facts = jnp.where(lane == k, bound, facts)
+    facts = facts.astype(jnp.float32)
+    stores = []
     for r in range(rows):
+        staged[r, body:, :] = jnp.broadcast_to(facts[r : r + 1, :], (FACTS, LANES)).astype(
+            jnp.bfloat16
+        )
+        loads[r].wait()
         for c in range(width // LANES):
-            staged[r, c * seq : (c + 1) * seq, :] = tokens[r, :, c * LANES : (c + 1) * LANES]
-        copies.append(
+            staged[r, c * seq : (c + 1) * seq, :] = raw[r, :, c * LANES : (c + 1) * LANES]
+        if r == 0:
+            clear.wait()
+        stores.append(
             pltpu.make_async_copy(
-                staged.at[r], out.at[target[r], pl.ds(0, body)], sems.at[r]
+                staged.at[r], out.at[lax.div(dest[r], rows)], out_sems.at[r]
             )
         )
-        copies[-1].start()
-    for copy in copies:
+        stores[-1].start()
+    for copy in stores:
         copy.wait()
-    fact_copy.wait()
-
-
-def pack(target, tokens, facts):
+
+
+def pack(dest, doc_ids, tokens, slots):
     rows, seq, width = tokens.shape
-    slots = facts.shape[0]
     body = seq * width // LANES
     return pl.pallas_call(
         pack_kernel,
@@ -58,24 +73,45 @@
         in_specs=[
             pl.BlockSpec(memory_space=pltpu.SMEM),
             pl.BlockSpec(memory_space=pltpu.VMEM),
-            pl.BlockSpec(memory_space=pltpu.VMEM),
+            pl.BlockSpec(memory_space=pltpu.HBM),
         ],
-        out_specs=pl.BlockSpec(memory_space=pl.ANY),
+        out_specs=pl.BlockSpec(memory_space=pltpu.HBM),
         scratch_shapes=[
-            pltpu.VMEM((rows, body, LANES), tokens.dtype),
+            pltpu.VMEM((rows, seq, width), tokens.dtype),
+            pltpu.VMEM((rows, body + FACTS, LANES), tokens.dtype),
+            pltpu.VMEM((slots, FACTS, LANES), tokens.dtype),
+            pltpu.SemaphoreType.DMA((rows,)),
             pltpu.SemaphoreType.DMA((rows,)),
             pltpu.SemaphoreType.DMA,
         ],
         compiler_params=pltpu.CompilerParams(vmem_limit_bytes=16 * 1024 * 1024),
         name="pack_rows",
-    )(target, tokens, facts)
-
-
-def unpack_kernel(source, received, out, sems):
+    )(dest, doc_ids, tokens)
+
+
+def unpack_kernel(core, received, out, info, facts, table, fact_sem, info_sem, sems):
     rows, body, _ = out.shape
+    slots = received.shape[0]
+    load = pltpu.make_async_copy(received.at[:, pl.ds(body, FACTS)], facts, fact_sem)
+    load.start()
+    load.wait()
+    values = facts[...].astype(jnp.float32)
+    shape = (slots, FACTS, LANES)
+    here = values[:, :, :1] == (lax.broadcasted_iota(jnp.int32, shape, 2) + 1).astype(jnp.float32)
+    source = lax.broadcasted_iota(jnp.int32, shape, 0).astype(jnp.float32)
+    result = jnp.sum(jnp.where(here, source, 0.0), 0)
+    kind = lax.broadcasted_iota(jnp.int32, (FACTS, LANES), 0)
+    for k in range(1, 4):
+        bound = jnp.sum(jnp.where(here, values[:, :, k : k + 1], 0.0), 0)
+        result = jnp.where(kind == k, bound, result)
+    table[...] = result.astype(jnp.int32)
+    keep = pltpu.make_async_copy(table, info, info_sem)
+    keep.start()
+    keep.wait()
+    first = (1 - core[0]) * rows
     copies = [
         pltpu.make_async_copy(
-            received.at[source[r], pl.ds(0, body)], out.at[r], sems.at[r]
+            received.at[info[0, first + r], pl.ds(0, body)], out.at[r], sems.at[r]
         )
         for r in range(rows)
     ]
@@ -85,24 +121,37 @@
         copy.wait()
 
 
-def unpack(source, received):
-    rows = source.shape[0]
+def unpack(core, received, rows):
+    slots = received.shape[0]
     body = received.shape[1] - FACTS
     return pl.pallas_call(
         unpack_kernel,
-        out_shape=jax.ShapeDtypeStruct((rows, body, LANES), received.dtype),
+        out_shape=(
+            jax.ShapeDtypeStruct((rows, body, LANES), received.dtype),
+            jax.ShapeDtypeStruct((FACTS, LANES), jnp.int32),
+        ),
         in_specs=[
             pl.BlockSpec(memory_space=pltpu.SMEM),
-            pl.BlockSpec(memory_space=pl.ANY),
+            pl.BlockSpec(memory_space=pltpu.HBM),
         ],
-        out_specs=pl.BlockSpec(memory_space=pltpu.VMEM),
-        scratch_shapes=[pltpu.SemaphoreType.DMA((rows,))],
+        out_specs=(
+            pl.BlockSpec(memory_space=pltpu.VMEM),
+            pl.BlockSpec(memory_space=pltpu.SMEM),
+        ),
+        scratch_shapes=[
+            pltpu.VMEM((slots, FACTS, LANES), received.dtype),
+            pltpu.VMEM((FACTS, LANES), jnp.int32),
+            pltpu.SemaphoreType.DMA,
+            pltpu.SemaphoreType.DMA,
+            pltpu.SemaphoreType.DMA((rows,)),
+        ],
         compiler_params=pltpu.CompilerParams(vmem_limit_bytes=16 * 1024 * 1024),
         name="unpack_rows",
-    )(source, received)
+    )(core, received)
 
 
 def layer_kernel(
+    core,
     info,
     received,
     x_other,
@@ -135,12 +184,13 @@
     model = 2 * half
     chunks = model // LANES
     body = half * seq // LANES
-    me = info[0]
+    me = core[0]
+    first_row = me * rows
     own_at = pl.ds(pl.multiple_of(me * body, body), body)
     oth_at = pl.ds(pl.multiple_of((1 - me) * body, body), body)
     x_copies = [
         pltpu.make_async_copy(
-            received.at[info[8 + r], pl.ds(0, body)], x_scr.at[r, own_at], row_sems.at[r]
+            received.at[info[0, first_row + r], pl.ds(0, body)], x_scr.at[r, own_at], row_sems.at[r]
         )
         for r in range(rows)
     ]
@@ -182,7 +232,7 @@
 
     def attend(r, carry):
         here = pl.ds(pl.multiple_of(r * seq, seq), seq)
-        bounds = [info[32 + 4 * r + i] for i in range(3)]
+        bounds = [info[k, first_row + r] for k in range(1, 4)]
         key_seg = sum([(key_pos >= b).astype(jnp.int32) for b in bounds])
         query_seg = sum([(query_pos >= b).astype(jnp.int32) for b in bounds])
         same = key_seg == query_seg
@@ -260,7 +310,7 @@
         at = slice(r * seq, (r + 1) * seq)
         encoded = norm(acc_scr[at, :], gain_ffn[...]).astype(jnp.bfloat16)
         qkv_scr[at, : 2 * half] = encoded
-        bounds = [info[32 + 4 * r + i] for i in range(3)]
+        bounds = [info[k, first_row + r] for k in range(1, 4)]
         seg = sum([(pos_iota >= b).astype(jnp.int32) for b in bounds])
         member = (seg == doc_iota).astype(jnp.float32)
         total = jnp.sum(member, -1, keepdims=True)
@@ -282,7 +332,7 @@
         copy.wait()
 
 
-def layer(info, received, x_other, weights, gain_attn, gain_ffn):
+def layer(core, info, received, x_other, weights, gain_attn, gain_ffn):
     rows, body, _ = x_other.shape
     half = body * LANES // HD
     tokens = rows * HD
@@ -298,7 +348,7 @@
             jax.ShapeDtypeStruct((tokens, half), jnp.bfloat16),
             jax.ShapeDtypeStruct((2, rows * 8, half), jnp.float32),
         ),
-        in_specs=[pl.BlockSpec(memory_space=pltpu.SMEM)]
+        in_specs=[pl.BlockSpec(memory_space=pltpu.SMEM)] * 2
         + [any_spec] * 2 + [vmem] * 4 + [any_spec] * 4 + [vmem] * 2,
         out_specs=(any_spec, any_spec, vmem),
         scratch_shapes=[
@@ -317,7 +367,7 @@
             flops=flops, bytes_accessed=28 * 1024 * 1024, transcendentals=0
         ),
         name="layer",
-    )(info, received, x_other, *weights, gain_attn, gain_ffn)
+    )(core, info, received, x_other, *weights, gain_attn, gain_ffn)
 
 
 def shards(tokens, doc_ids, dest, owner, w_qkv, w_out, gain_attn, w_up, w_down, gain_ffn):
@@ -332,37 +382,14 @@
     for own in (qkv_own, w_out, w_up, w_down):
         weights += [own, lax.ppermute(own, "mp", SWAP)]
 
-    target = dest // row_count
-    sent = (jnp.arange(devices, dtype=jnp.int32)[:, None] == target[None, :]).astype(jnp.int32)
-    bounds = [jnp.sum((doc_ids < k).astype(jnp.int32), -1) for k in range(1, docs)]
-    fact_list = [dest % row_count + 1] + bounds
-    facts = jnp.stack([jnp.sum(sent * fact[None, :], -1) for fact in fact_list], -1)
-    facts = jnp.broadcast_to(
-        jnp.pad(facts, ((0, 0), (0, LANES - len(fact_list))))[:, None, :].astype(jnp.bfloat16),
-        (devices, FACTS, LANES),
-    )
     received = lax.all_to_all(
-        pack(target, tokens, facts), "dp", split_axis=0, concat_axis=0, tiled=True
-    )
-    got_facts = received[:, -FACTS, : len(fact_list)].astype(jnp.int32)
-    slot = jnp.arange(row_count, dtype=jnp.int32)
-    here = got_facts[:, :1] == slot[None, :] + 1
-    source = jnp.sum(jnp.where(here, jnp.arange(devices, dtype=jnp.int32)[:, None], 0), 0)
-    new_bounds = jnp.sum(jnp.where(here[:, :, None], got_facts[:, None, 1:], 0), 0)
-    source_own = lax.dynamic_slice_in_dim(source, me * mine, mine)
-    source_oth = lax.dynamic_slice_in_dim(source, (1 - me) * mine, mine)
-    bounds_own = lax.dynamic_slice_in_dim(new_bounds, me * mine, mine)
-    info = jnp.concatenate(
-        [
-            jnp.full((8,), me, jnp.int32),
-            source_own,
-            jnp.zeros((24 - mine,), jnp.int32),
-            jnp.pad(bounds_own, ((0, 0), (0, 1))).reshape(-1),
-        ]
-    )
-    x_other = lax.ppermute(unpack(source_oth, received), "mp", SWAP)
+        pack(dest, doc_ids, tokens, devices), "dp", split_axis=0, concat_axis=0, tiled=True
+    )
+    core = me.astype(jnp.int32)[None]
+    x_send, info = unpack(core, received, mine)
+    x_other = lax.ppermute(x_send, "mp", SWAP)
     enc_own, enc_oth, emb = layer(
-        info, received, x_other, weights, gain_attn[None], gain_ffn[None]
+        core, info, received, x_other, weights, gain_attn[None], gain_ffn[None]
     )
     emb = emb.astype(jnp.bfloat16)
     emb_recv = lax.ppermute(emb[1], "mp", SWAP)

time: 150 us -> 157 us (1.047)
  Pallas kernels: 45.9 us -> 50.4 us
  other arithmetic: 4.97 us -> 1.87 us
  local copies, waits for them, and re-layouts: 6.68 us -> 9.46 us
  waiting for transfers between devices: 65.3 us -> 67.3 us
    unnamed x16 -> x22, local copies, waits for them, and re-layouts: 3.92 us -> 7.24 us
    pallas_call x1, Pallas kernels: 3.65 us -> 6.4 us  [pack(): pl.pallas_call(pack_kernel, out_shape=jax.ShapeDtypeStruct((slots, body +...]
    pallas_call x1, Pallas kernels: 1.87 us -> 4.04 us  [unpack(): pl.pallas_call(unpack_kernel, out_shape=(jax.ShapeDtypeStruct((rows, body...]
  transfers between devices with their start and end apart: 9 -> 9, of which waited for: 4 -> 4; matrix products, arithmetic and copies ran while one was open for 3% -> 2% of each run, Pallas kernels for 1% -> 3%
where the time goes in v4:
time: 157 us; the launch traced here: 156 us
  waiting for transfers between devices  67.3 us (43%)
  Pallas kernels  50.4 us (32%)
  starting transfers between devices  25.7 us (16%)
  local copies, waits for them, and re-layouts  9.46 us (6%)
  other arithmetic  1.87 us (1%)
    all_to_all x1, waiting for transfers between devices, shards(): lax.all_to_all(pack(dest, doc_ids, tokens, devices), 'dp', split_axis=0,...  52.9 us
    pallas_call x1, Pallas kernels, layer(): pl.pallas_call(layer_kernel, out_shape=(jax.ShapeDtypeStruct((tokens, hal...  40 us
    all_to_all x1, starting transfers between devices, shards(): lax.all_to_all(pack(dest, doc_ids, tokens, devices), 'dp', split_axis=0,...  11.9 us
    all_to_all x1, starting transfers between devices, shards(): lax.all_to_all(sending.reshape(devices, SLOTS, half), 'dp', split_axis=0,...  11.8 us
    all_to_all x1, waiting for transfers between devices, shards(): lax.all_to_all(sending.reshape(devices, SLOTS, half), 'dp', split_axis=0,...  10.8 us
    unnamed x22, local copies, waits for them, and re-layouts  7.24 us
    pallas_call x1, Pallas kernels, pack(): pl.pallas_call(pack_kernel, out_shape=jax.ShapeDtypeStruct((slots, body +...  6.4 us
    pallas_call x1, Pallas kernels, unpack(): pl.pallas_call(unpack_kernel, out_shape=(jax.ShapeDtypeStruct((rows, body...  4.04 us
  transfers between devices with their start and end apart: 9, of which 4 were waited for; matrix products, arithmetic and copies ran while one was open for 2% of the time, Pallas kernels for 3%

profile of v4, /device:TPU:0, one launch (start us, length us, event | category | flops | bytes accessed | tf_op | source)
XLA Modules:
  0.0 156.0 jit_solution(9053946507100343379)
XLA Ops:
  0.6 0.0 copy-start.1
  0.6 1.5 copy-done.1
  2.1 0.7 copy-done.2
  2.9 0.7 copy-done.3
  3.5 6.4 %pack_rows.1 = bf16[64,264,128]{2,1,0:T(8,128)(2,1)S(1)} custom-call(s32[28]{0:T(128)S(1)} %copy-done.3, s32[28,64]{1,0:T(8,128)S(1)} %copy-done.2, bf16[28,64,512]{2,1,0:T(8,128)(2,1)S(1)} %copy-done.1), custom_call_target="tpu_custom_call" | custom-call | tf_op jit(solution)/shard_map/pack_rows/pallas_call | solution.py:70
  9.9 2.0 %copy-done = bf16[64,264,128]{2,1,0:T(8,128)(2,1)} copy-done((bf16[64,264,128]{2,1,0:T(8,128)(2,1)}, bf16[64,264,128]{2,1,0:T(8,128)(2,1)S(1)}, u32[]{:S(2)}) %copy-start) | copy-done | bytes 4325400
  12.0 11.9 %all-to-all-start = ((bf16[64,264,128]{2,1,0:T(8,128)(2,1)}), bf16[64,264,128]{2,1,0:T(8,128)(2,1)}, u32[]{:S(2)}, u32[]{:S(2)}) async-start(bf16[64,264,128]{2,1,0:T(8,128)(2,1)} %copy-done), calls=%async_computation | async-start | bytes 8650752 | tf_op jit(solution)/shard_map/all_to_all | solution.py:385
  23.8 0.0 copy-start.9
  23.9 0.0 copy-start.7
  23.9 0.0 copy-start.8
  23.9 0.1 collective-permute-start.3
  24.0 0.5 collective-permute-start.4
  24.5 0.1 collective-permute-start.1
  24.6 0.0 copy-done.4
  24.6 0.4 collective-permute-start.2
  25.0 52.9 %all-to-all-done.received = bf16[64,264,128]{2,1,0:T(8,128)(2,1)} async-done(((bf16[64,264,128]{2,1,0:T(8,128)(2,1)}), bf16[64,264,128]{2,1,0:T(8,128)(2,1)}, u32[]{:S(2)}, u32[]{:S(2)}) %all-to-all-start) | async-done | bytes 4325408 | tf_op jit(solution)/shard_map/all_to_all | solution.py:385
  77.9 4.0 %unpack_rows.1 = (bf16[14,256,128]{2,1,0:T(8,128)(2,1)}, s32[8,128]{1,0:T(8,128)S(1)}) custom-call(s32[1]{0:T(128)} %bitcast.core, bf16[64,264,128]{2,1,0:T(8,128)(2,1)} %all-to-all-done.received), custom_call_target="tpu_custom_call" | custom-call | tf_op jit(solution)/shard_map/unpack_rows/pallas_call | solution.py:127
  81.9 0.3 collective-permute-start
  82.2 0.0 copy-done.9
  82.2 0.1 copy.17
  82.3 0.1 mul.12
  82.4 0.1 eq.49
  82.5 0.2 convert_reduce_fusion
  82.7 0.1 reduce_sum.12
  82.8 0.1 copy.18
  82.9 0.1 copy.20
  83.0 0.1 reshape.30
  83.1 0.0 collective-permute-done.2.wo_oth
  83.1 0.0 collective-permute-done.1.wq_oth
  83.1 0.0 collective-permute-done.3.wu_oth
  83.2 0.0 collective-permute-done.4.wd_oth
  83.2 1.7 %collective-permute-done.x_other = bf16[14,256,128]{2,1,0:T(8,128)(2,1)S(1)} collective-permute-done((bf16[14,256,128]{2,1,0:T(8,128)(2,1)}, bf16[14,256,128]{2,1,0:T(8,128)(2,1)S(1)}, u32[]{:S(2)}, u32[]{:S(2)}) %collective-permute-start) | collective-permute-done | bytes 917536 | tf_op jit(solution)/shard_map/ppermute | solution.py:390
  84.9 0.9 copy-done.5
  85.8 0.0 copy-done.8
  85.8 1.2 copy-done.6
  87.0 40.0 %layer.1 = (bf16[896,512]{1,0:T(8,128)(2,1)S(1)}, bf16[896,512]{1,0:T(8,128)(2,1)}, f32[2,112,512]{2,1,0:T(8,128)S(1)}) custom-call(s32[1]{0:T(128)} %bitcast.core, s32[8,128]{1,0:T(8,128)S(1)} %get-tuple-element.7.info, bf16[64,264,128]{2,1,0:T(8,128)(2,1)} %all-to-all-done.received, bf16[14,256,128]{2,1,0:T(8,128)(2,1)S(1)} %copy-done.6, ...), custom_call_target="tpu_custom_call" | custom-call | flops 22548578304 | bytes 29360128 | tf_op jit(solution)/shard_map/layer/pallas_call | solution.py:344
  127.0 0.2 collective-permute-start.5
  127.3 0.5 collective-permute-start.6
  127.7 0.2 fusion.1
  127.9 1.8 %collective-permute-done.6 = bf16[112,512]{1,0:T(8,128)(2,1)S(1)} collective-permute-done((bf16[112,512]{1,0:T(8,128)(2,1)S(1)}, bf16[112,512]{1,0:T(8,128)(2,1)S(1)}, u32[]{:S(2)}, u32[]{:S(2)}) %collective-permute-start.6) | collective-permute-done | bytes 114720 | tf_op jit(solution)/shard_map/ppermute | solution.py:395
  129.7 0.2 fusion
  129.9 0.8 reshape.31
  130.7 11.8 %all-to-all-start.1 = ((bf16[64,4,512]{2,1,0:T(4,128)(2,1)}), bf16[64,4,512]{2,1,0:T(4,128)(2,1)S(1)}, u32[]{:S(2)}, u32[]{:S(2)}) async-start(bf16[64,4,512]{2,1,0:T(4,128)(2,1)} %reshape.31), calls=%async_computation.1 | async-start | bytes 524288 | tf_op jit(solution)/shard_map/all_to_all | solution.py:413
  142.5 10.8 %all-to-all-done.1 = bf16[64,4,512]{2,1,0:T(4,128)(2,1)S(1)} async-done(((bf16[64,4,512]{2,1,0:T(4,128)(2,1)}), bf16[64,4,512]{2,1,0:T(4,128)(2,1)S(1)}, u32[]{:S(2)}, u32[]{:S(2)}) %all-to-all-start.1) | async-done | bytes 262176 | tf_op jit(solution)/shard_map/all_to_all | solution.py:413
  153.4 0.9 reshape.35
  154.4 0.0 collective-permute-done.5
  154.4 0.2 broadcast_select_fusion.1
  154.6 1.4 pad_maximum_fusion
  (14 shorter events, 0.1 us)
Async XLA Ops:
  0.6 1.5 copy-start.1
  2.1 0.7 copy-start.2
  2.8 0.7 copy-start.3
  9.9 2.1 %copy-start = (bf16[64,264,128]{2,1,0:T(8,128)(2,1)}, bf16[64,264,128]{2,1,0:T(8,128)(2,1)S(1)}, u32[]{:S(2)}) copy-start(bf16[64,264,128]{2,1,0:T(8,128)(2,1)S(1)} %pack_rows.1) | copy-start | bytes 12976132
  12.0 12.6 %copy-start.4 = (bf16[512,1024]{1,0:T(8,128)(2,1)S(1)}, bf16[512,1024]{1,0:T(8,128)(2,1)}, u32[]{:S(2)}) copy-start(bf16[512,1024]{1,0:T(8,128)(2,1)} %wo_own.1) | copy-start | bytes 3145732
  12.0 65.9 %all-to-all-start = ((bf16[64,264,128]{2,1,0:T(8,128)(2,1)}), bf16[64,264,128]{2,1,0:T(8,128)(2,1)}, u32[]{:S(2)}, u32[]{:S(2)}) async-start(bf16[64,264,128]{2,1,0:T(8,128)(2,1)} %copy-done), calls=%async_computation | async-start | bytes 8650752 | tf_op jit(solution)/shard_map/all_to_all | solution.py:385
  23.8 58.4 %copy-start.9 = (s32[28,4]{0,1:T(4,128)S(1)}, s32[28,4]{0,1:T(4,128)}, u32[]{:S(2)}) copy-start(s32[28,4]{0,1:T(4,128)} %param.13) | copy-start | bytes 1348
  23.9 61.9 %copy-start.7 = (f32[1024]{0:T(1024)S(1)}, f32[1024]{0:T(1024)}, u32[]{:S(2)}) copy-start(f32[1024]{0:T(1024)} %param.16) | copy-start | bytes 12292
  23.9 61.9 %copy-start.8 = (f32[1024]{0:T(1024)S(1)}, f32[1024]{0:T(1024)}, u32[]{:S(2)}) copy-start(f32[1024]{0:T(1024)} %param.19) | copy-start | bytes 12292
  23.9 59.3 %collective-permute-start.3 = (bf16[1024,2048]{1,0:T(8,128)(2,1)}, bf16[1024,2048]{1,0:T(8,128)(2,1)}, u32[]{:S(2)}, u32[]{:S(2)}) collective-permute-start(bf16[1024,2048]{1,0:T(8,128)(2,1)} %wu_own.1), channel_id=1, source_target_pairs={{0,1},{1,0},{2,3},{3,2},{4,5},{5,4},{6,7},{7,6},{8,9},{9,8},{10,11... | collective-permute-start | bytes 12582920 | tf_op jit(solution)/shard_map/ppermute | solution.py:383
  24.0 59.2 %collective-permute-start.4 = (bf16[2048,1024]{1,0:T(8,128)(2,1)}, bf16[2048,1024]{1,0:T(8,128)(2,1)}, u32[]{:S(2)}, u32[]{:S(2)}) collective-permute-start(bf16[2048,1024]{1,0:T(8,128)(2,1)} %wd_own.1), channel_id=1, source_target_pairs={{0,1},{1,0},{2,3},{3,2},{4,5},{5,4},{6,7},{7,6},{8,9},{9,8},{10,11... | collective-permute-start | bytes 12582920 | tf_op jit(solution)/shard_map/ppermute | solution.py:383
  24.5 58.7 %collective-permute-start.1 = (bf16[3,1024,512]{2,1,0:T(8,128)(2,1)}, bf16[3,1024,512]{2,1,0:T(8,128)(2,1)}, u32[]{:S(2)}, u32[]{:S(2)}) collective-permute-start(bf16[3,1024,512]{2,1,0:T(8,128)(2,1)} %bitcast.22), channel_id=1, source_target_pairs={{0,1},{1,0},{2,3},{3,2},{4,5},{5,4},{6,7},{7,6},{8,9},{9,8},{10,11... | collective-permute-start | bytes 9437192 | tf_op jit(solution)/shard_map/ppermute | solution.py:383
  24.6 58.6 %collective-permute-start.2 = (bf16[512,1024]{1,0:T(8,128)(2,1)S(1)}, bf16[512,1024]{1,0:T(8,128)(2,1)S(1)}, u32[]{:S(2)}, u32[]{:S(2)}) collective-permute-start(bf16[512,1024]{1,0:T(8,128)(2,1)S(1)} %copy-done.4), channel_id=1, source_target_pairs={{0,1},{1,0},{2,3},{3,2},{4,5},{5,4},{6,7},{7,6},{8,9},{9,8},{10,11... | collective-permute-start | bytes 3145736 | tf_op jit(solution)/shard_map/ppermute | solution.py:383
  81.9 2.9 %collective-permute-start = (bf16[14,256,128]{2,1,0:T(8,128)(2,1)}, bf16[14,256,128]{2,1,0:T(8,128)(2,1)S(1)}, u32[]{:S(2)}, u32[]{:S(2)}) collective-permute-start(bf16[14,256,128]{2,1,0:T(8,128)(2,1)} %get-tuple-element.8), channel_id=1, source_target_pairs={{0,1},{1,0},{2,3},{3,2},{4,5},{5,4},{6,7},{7,6},{8,9},{9,8},{10,11... | collective-permute-start | bytes 2752520 | tf_op jit(solution)/shard_map/ppermute | solution.py:390
  84.9 0.9 copy-start.5
  85.8 1.2 copy-start.6
  127.0 27.4 %collective-permute-start.5 = (bf16[896,512]{1,0:T(8,128)(2,1)}, bf16[896,512]{1,0:T(8,128)(2,1)S(1)}, u32[]{:S(2)}, u32[]{:S(2)}) collective-permute-start(bf16[896,512]{1,0:T(8,128)(2,1)} %get-tuple-element.10), channel_id=1, source_target_pairs={{0,1},{1,0},{2,3},{3,2},{4,5},{5,4},{6,7},{7,6},{8,9},{9,8},{10,11... | collective-permute-start | bytes 2752520 | tf_op jit(solution)/shard_map/ppermute | solution.py:396
  127.3 2.4 %collective-permute-start.6 = (bf16[112,512]{1,0:T(8,128)(2,1)S(1)}, bf16[112,512]{1,0:T(8,128)(2,1)S(1)}, u32[]{:S(2)}, u32[]{:S(2)}) collective-permute-start(bf16[112,512]{1,0:T(8,128)(2,1)S(1)} %slice_bitcast_fusion), channel_id=1, source_target_pairs={{0,1},{1,0},{2,3},{3,2},{4,5},{5,4},{6,7},{7,6},{8,9},{9,8},{10,11... | collective-permute-start | bytes 344072 | tf_op jit(solution)/shard_map/ppermute | solution.py:395
  130.7 22.7 %all-to-all-start.1 = ((bf16[64,4,512]{2,1,0:T(4,128)(2,1)}), bf16[64,4,512]{2,1,0:T(4,128)(2,1)S(1)}, u32[]{:S(2)}, u32[]{:S(2)}) async-start(bf16[64,4,512]{2,1,0:T(4,128)(2,1)} %reshape.31), calls=%async_computation.1 | async-start | bytes 524288 | tf_op jit(solution)/shard_map/all_to_all | solution.py:413

commit v5 on v4

--- a/solution.py
+++ b/solution.py
@@ -84,7 +84,7 @@
             pltpu.SemaphoreType.DMA((rows,)),
             pltpu.SemaphoreType.DMA,
         ],
-        compiler_params=pltpu.CompilerParams(vmem_limit_bytes=16 * 1024 * 1024),
+        compiler_params=pltpu.CompilerParams(vmem_limit_bytes=60 * 1024 * 1024),
         name="pack_rows",
     )(dest, doc_ids, tokens)
 
@@ -145,7 +145,7 @@
             pltpu.SemaphoreType.DMA,
             pltpu.SemaphoreType.DMA((rows,)),
         ],
-        compiler_params=pltpu.CompilerParams(vmem_limit_bytes=16 * 1024 * 1024),
+        compiler_params=pltpu.CompilerParams(vmem_limit_bytes=60 * 1024 * 1024),
         name="unpack_rows",
     )(core, received)
 
@@ -304,30 +304,43 @@
 
     lax.fori_loop(0, 2 * tiles * parts, feed, 0)
 
-    doc_iota = lax.broadcasted_iota(jnp.int32, (8, seq), 0)
-    pos_iota = lax.broadcasted_iota(jnp.int32, (8, seq), 1)
-    for r in range(rows):
-        at = slice(r * seq, (r + 1) * seq)
+    two = 2 * seq
+    doc = lax.broadcasted_iota(jnp.int32, (16, two), 0)
+    position = lax.broadcasted_iota(jnp.int32, (16, two), 1)
+    same_row = (doc < 8) == (position < seq)
+    doc = doc % 8
+    own_col = pl.ds(pl.multiple_of(me * half, half), half)
+    oth_col = pl.ds(pl.multiple_of((1 - me) * half, half), half)
+    outs = []
+    for m in range(rows // 2):
+        at = slice(m * two, (m + 1) * two)
         encoded = norm(acc_scr[at, :], gain_ffn[...]).astype(jnp.bfloat16)
         qkv_scr[at, : 2 * half] = encoded
-        bounds = [info[k, first_row + r] for k in range(1, 4)]
-        seg = sum([(pos_iota >= b).astype(jnp.int32) for b in bounds])
-        member = (seg == doc_iota).astype(jnp.float32)
+        for i, (col, out) in enumerate(((own_col, enc_own), (oth_col, enc_oth))):
+            outs.append(
+                pltpu.make_async_copy(
+                    qkv_scr.at[pl.ds(m * two, two), col],
+                    out.at[pl.ds(m * two, two)],
+                    out_sems.at[m, i],
+                )
+            )
+            outs[-1].start()
+        seg = jnp.zeros_like(position)
+        for k in range(1, 4):
+            bound = jnp.where(
+                position < seq,
+                info[k, first_row + 2 * m],
+                info[k, first_row + 2 * m + 1] + seq,
+            )
+            seg += (position >= bound).astype(jnp.int32)
+        member = ((seg == doc) & same_row).astype(jnp.float32)
         total = jnp.sum(member, -1, keepdims=True)
         pooled = jnp.dot(member.astype(jnp.bfloat16), encoded, preferred_element_type=jnp.float32)
         pooled = pooled * (1.0 / jnp.maximum(total, 1.0))
         square = jnp.mean(pooled * pooled, -1, keepdims=True)
-        embedded = pooled * lax.rsqrt(square + 1e-06)
-        emb[me, r * 8 : (r + 1) * 8, :] = embedded[:, :half]
-        emb[1 - me, r * 8 : (r + 1) * 8, :] = embedded[:, half:]
-    own_col = pl.ds(pl.multiple_of(me * half, half), half)
-    oth_col = pl.ds(pl.multiple_of((1 - me) * half, half), half)
-    outs = [
-        pltpu.make_async_copy(qkv_scr.at[:, own_col], enc_own, out_sems.at[0]),
-        pltpu.make_async_copy(qkv_scr.at[:, oth_col], enc_oth, out_sems.at[1]),
-    ]
-    for copy in outs:
-        copy.start()
+        embedded = (pooled * lax.rsqrt(square + 1e-06)).astype(jnp.bfloat16)
+        emb[me, m * 16 : (m + 1) * 16, :] = embedded[:, :half]
+        emb[1 - me, m * 16 : (m + 1) * 16, :] = embedded[:, half:]
     for copy in outs:
         copy.wait()
 
@@ -346,7 +359,7 @@
         out_shape=(
             jax.ShapeDtypeStruct((tokens, half), jnp.bfloat16),
             jax.ShapeDtypeStruct((tokens, half), jnp.bfloat16),
-            jax.ShapeDtypeStruct((2, rows * 8, half), jnp.float32),
+            jax.ShapeDtypeStruct((2, rows * 8, half), jnp.bfloat16),
         ),
         in_specs=[pl.BlockSpec(memory_space=pltpu.SMEM)] * 2
         + [any_spec] * 2 + [vmem] * 4 + [any_spec] * 4 + [vmem] * 2,
@@ -360,7 +373,7 @@
             pltpu.SemaphoreType.DMA((rows,)),
             pltpu.SemaphoreType.DMA,
             pltpu.SemaphoreType.DMA((2, 2)),
-            pltpu.SemaphoreType.DMA((2,)),
+            pltpu.SemaphoreType.DMA((rows // 2, 2)),
         ],
         compiler_params=pltpu.CompilerParams(vmem_limit_bytes=46 * 1024 * 1024),
         cost_estimate=pl.CostEstimate(
@@ -391,7 +404,6 @@
     enc_own, enc_oth, emb = layer(
         core, info, received, x_other, weights, gain_attn[None], gain_ffn[None]
     )
-    emb = emb.astype(jnp.bfloat16)
     emb_recv = lax.ppermute(emb[1], "mp", SWAP)
     enc_recv = lax.ppermute(enc_oth, "mp", SWAP)
 
@@ -413,14 +425,14 @@
     got = lax.all_to_all(
         sending.reshape(devices, SLOTS, half), "dp", split_axis=0, concat_axis=0, tiled=True
     )
-    index_part = got[:, : SLOTS - 1].astype(jnp.float32).reshape(1, devices * (SLOTS - 1), half)
-
     enc_own = enc_own.reshape(mine, seq, half)
     enc_recv = enc_recv.reshape(mine, seq, half)
     first = me == 0
     encoded = jnp.concatenate(
         [jnp.where(first, enc_own, enc_recv), jnp.where(first, enc_recv, enc_own)], 0
     )
+    got, encoded = lax.optimization_barrier((got, encoded))
+    index_part = got[:, : SLOTS - 1].astype(jnp.float32).reshape(1, devices * (SLOTS - 1), half)
     return (encoded, index_part)
 
 

time: 157 us -> 149 us (0.949)
  local copies, waits for them, and re-layouts: 9.46 us -> 6.24 us
  Pallas kernels: 50.4 us -> 47.2 us
    unnamed x22 -> x16, local copies, waits for them, and re-layouts: 7.24 us -> 4.03 us
    pallas_call x1, Pallas kernels: 6.4 us -> 3.53 us  [pack(): pl.pallas_call(pack_kernel, out_shape=jax.ShapeDtypeStruct((slots, body +...]
where the time goes in v5:
time: 149 us; the launch traced here: 148 us
  waiting for transfers between devices  66.1 us (44%)
  Pallas kernels  47.2 us (32%)
  starting transfers between devices  25.8 us (17%)
  local copies, waits for them, and re-layouts  6.24 us (4%)
  other arithmetic  1.73 us (1%)
    all_to_all x1, waiting for transfers between devices, shards(): lax.all_to_all(pack(dest, doc_ids, tokens, devices), 'dp', split_axis=0,...  52.9 us
    pallas_call x1, Pallas kernels, layer(): pl.pallas_call(layer_kernel, out_shape=(jax.ShapeDtypeStruct((tokens, hal...  39.7 us
    all_to_all x1, starting transfers between devices, shards(): lax.all_to_all(pack(dest, doc_ids, tokens, devices), 'dp', split_axis=0,...  12 us
    all_to_all x1, starting transfers between devices, shards(): lax.all_to_all(sending.reshape(devices, SLOTS, half), 'dp', split_axis=0,...  11.8 us
    all_to_all x1, waiting for transfers between devices, shards(): lax.all_to_all(sending.reshape(devices, SLOTS, half), 'dp', split_axis=0,...  9.32 us
    pallas_call x1, Pallas kernels, unpack(): pl.pallas_call(unpack_kernel, out_shape=(jax.ShapeDtypeStruct((rows, body...  4.04 us
    unnamed x16, local copies, waits for them, and re-layouts  4.03 us
    pallas_call x1, Pallas kernels, pack(): pl.pallas_call(pack_kernel, out_shape=jax.ShapeDtypeStruct((slots, body +...  3.53 us
  transfers between devices with their start and end apart: 9, of which 4 were waited for; matrix products, arithmetic and copies ran while one was open for 2% of the time, Pallas kernels for 3%

profile of v5, /device:TPU:0, one launch (start us, length us, event | category | flops | bytes accessed | tf_op | source)
XLA Modules:
  0.0 148.4 jit_solution(1978508136680269458)
XLA Ops:
  0.6 3.5 %pack_rows.1 = bf16[64,264,128]{2,1,0:T(8,128)(2,1)} custom-call(s32[28]{0:T(128)} %dest.1, s32[28,64]{1,0:T(8,128)} %doc_ids.1, bf16[28,64,512]{2,1,0:T(8,128)(2,1)} %tokens.1), custom_call_target="tpu_custom_call" | custom-call | tf_op jit(solution)/shard_map/pack_rows/pallas_call | solution.py:70
  4.2 0.0 copy-start
  4.2 12.0 %all-to-all-start = ((bf16[64,264,128]{2,1,0:T(8,128)(2,1)}), bf16[64,264,128]{2,1,0:T(8,128)(2,1)}, u32[]{:S(2)}, u32[]{:S(2)}) async-start(bf16[64,264,128]{2,1,0:T(8,128)(2,1)} %pack_rows.1), calls=%async_computation | async-start | bytes 8650752 | tf_op jit(solution)/shard_map/all_to_all | solution.py:398
  16.2 0.0 copy-start.6
  16.2 0.0 copy-start.3
  16.2 0.0 copy-start.4
  16.2 0.1 collective-permute-start.3
  16.3 0.5 collective-permute-start.4
  16.8 0.0 copy-done
  16.8 0.1 collective-permute-start.1
  16.9 0.4 collective-permute-start.2
  17.3 52.9 %all-to-all-done.received = bf16[64,264,128]{2,1,0:T(8,128)(2,1)} async-done(((bf16[64,264,128]{2,1,0:T(8,128)(2,1)}), bf16[64,264,128]{2,1,0:T(8,128)(2,1)}, u32[]{:S(2)}, u32[]{:S(2)}) %all-to-all-start) | async-done | bytes 4325408 | tf_op jit(solution)/shard_map/all_to_all | solution.py:398
  70.2 4.0 %unpack_rows.1 = (bf16[14,256,128]{2,1,0:T(8,128)(2,1)}, s32[8,128]{1,0:T(8,128)}) custom-call(s32[1]{0:T(128)} %bitcast.1.core, bf16[64,264,128]{2,1,0:T(8,128)(2,1)} %all-to-all-done.received), custom_call_target="tpu_custom_call" | custom-call | tf_op jit(solution)/shard_map/unpack_rows/pallas_call | solution.py:127
  74.3 0.3 collective-permute-start
  74.5 0.0 copy-done.6
  74.6 0.1 copy.17
  74.7 0.1 eq.48
  74.8 0.0 collective-permute-done.2.wo_oth
  74.8 0.0 collective-permute-done.1.wq_oth
  74.8 0.0 collective-permute-done.3.wu_oth
  74.8 0.0 collective-permute-done.4.wd_oth
  74.8 2.5 %collective-permute-done.x_other = bf16[14,256,128]{2,1,0:T(8,128)(2,1)} collective-permute-done((bf16[14,256,128]{2,1,0:T(8,128)(2,1)}, bf16[14,256,128]{2,1,0:T(8,128)(2,1)}, u32[]{:S(2)}, u32[]{:S(2)}) %collective-permute-start) | collective-permute-done | bytes 917536 | tf_op jit(solution)/shard_map/ppermute | solution.py:403
  77.3 0.0 copy-done.3
  77.3 0.0 copy-done.4
  77.3 0.0 copy-start.1
  77.4 1.9 %copy-done.1 = bf16[1024,3,512]{2,0,1:T(8,128)(2,1)S(1)} copy-done((bf16[1024,3,512]{2,0,1:T(8,128)(2,1)S(1)}, bf16[1024,3,512]{2,0,1:T(8,128)(2,1)}, u32[]{:S(2)}) %copy-start.1) | copy-done | bytes 3145752
  79.2 0.0 copy-start.2
  79.2 1.2 copy-done.2
  80.5 0.7 copy-done.5
  81.2 39.7 %layer.1 = (bf16[896,512]{1,0:T(8,128)(2,1)S(1)}, bf16[896,512]{1,0:T(8,128)(2,1)S(1)}, bf16[2,112,512]{2,1,0:T(8,128)(2,1)S(1)}) custom-call(s32[1]{0:T(128)} %bitcast.1.core, s32[8,128]{1,0:T(8,128)S(1)} %copy-done.5, bf16[64,264,128]{2,1,0:T(8,128)(2,1)} %all-to-all-done.received, bf16[14,256,128]{2,1,0:T(8,128)(2,1)} %collective-permute-done.x_other, ...), custom_call_target="tpu_custom_call" | custom-call | flops 22548578304 | bytes 29360128 | tf_op jit(solution)/shard_map/layer/pallas_call | solution.py:357
  120.8 0.2 collective-permute-start.6
  121.1 0.5 collective-permute-start.5
  121.5 0.2 convert_reduce_fusion
  121.7 0.1 reduce_sum.12
  121.8 0.1 copy.18
  121.9 0.1 mul.12
  122.0 0.1 copy.20
  122.1 0.1 reshape.30
  122.2 1.3 collective-permute-done.5
  123.6 0.2 fusion.1
  123.8 0.2 fusion
  124.0 0.8 reshape.31
  124.8 11.8 %all-to-all-start.1 = ((bf16[64,4,512]{2,1,0:T(4,128)(2,1)}), bf16[64,4,512]{2,1,0:T(4,128)(2,1)S(1)}, u32[]{:S(2)}, u32[]{:S(2)}) async-start(bf16[64,4,512]{2,1,0:T(4,128)(2,1)} %reshape.31), calls=%async_computation.1 | async-start | bytes 524288 | tf_op jit(solution)/shard_map/all_to_all | solution.py:425
  136.6 0.0 collective-permute-done.6
  136.6 0.1 broadcast_select_fusion.1
  136.7 1.4 pad_maximum_fusion
  138.1 9.3 %all-to-all-done.1 = bf16[64,4,512]{2,1,0:T(4,128)(2,1)S(1)} async-done(((bf16[64,4,512]{2,1,0:T(4,128)(2,1)}), bf16[64,4,512]{2,1,0:T(4,128)(2,1)S(1)}, u32[]{:S(2)}, u32[]{:S(2)}) %all-to-all-start.1) | async-done | bytes 262176 | tf_op jit(solution)/shard_map/all_to_all | solution.py:425
  147.5 0.9 reshape.35
  (7 shorter events, 0.1 us)
Async XLA Ops:
  4.2 12.6 %copy-start = (bf16[1024,3,512]{2,0,1:T(8,128)(2,1)S(1)}, bf16[1024,3,512]{2,0,1:T(8,128)(2,1)}, u32[]{:S(2)}) copy-start(bf16[1024,3,512]{2,0,1:T(8,128)(2,1)} %param.14) | copy-start | bytes 9437188
  4.2 66.0 %all-to-all-start = ((bf16[64,264,128]{2,1,0:T(8,128)(2,1)}), bf16[64,264,128]{2,1,0:T(8,128)(2,1)}, u32[]{:S(2)}, u32[]{:S(2)}) async-start(bf16[64,264,128]{2,1,0:T(8,128)(2,1)} %pack_rows.1), calls=%async_computation | async-start | bytes 8650752 | tf_op jit(solution)/shard_map/all_to_all | solution.py:398
  16.2 58.4 %copy-start.6 = (s32[28,4]{0,1:T(4,128)S(1)}, s32[28,4]{0,1:T(4,128)}, u32[]{:S(2)}) copy-start(s32[28,4]{0,1:T(4,128)} %param.13) | copy-start | bytes 1348
  16.2 61.2 %copy-start.3 = (f32[1024]{0:T(1024)S(1)}, f32[1024]{0:T(1024)}, u32[]{:S(2)}) copy-start(f32[1024]{0:T(1024)} %param.16) | copy-start | bytes 12292
  16.2 61.1 %copy-start.4 = (f32[1024]{0:T(1024)S(1)}, f32[1024]{0:T(1024)}, u32[]{:S(2)}) copy-start(f32[1024]{0:T(1024)} %param.19) | copy-start | bytes 12292
  16.2 58.6 %collective-permute-start.3 = (bf16[1024,2048]{1,0:T(8,128)(2,1)}, bf16[1024,2048]{1,0:T(8,128)(2,1)}, u32[]{:S(2)}, u32[]{:S(2)}) collective-permute-start(bf16[1024,2048]{1,0:T(8,128)(2,1)} %wu_own.1), channel_id=1, source_target_pairs={{0,1},{1,0},{2,3},{3,2},{4,5},{5,4},{6,7},{7,6},{8,9},{9,8},{10,11... | collective-permute-start | bytes 12582920 | tf_op jit(solution)/shard_map/ppermute | solution.py:396
  16.3 58.5 %collective-permute-start.4 = (bf16[2048,1024]{1,0:T(8,128)(2,1)}, bf16[2048,1024]{1,0:T(8,128)(2,1)}, u32[]{:S(2)}, u32[]{:S(2)}) collective-permute-start(bf16[2048,1024]{1,0:T(8,128)(2,1)} %wd_own.1), channel_id=1, source_target_pairs={{0,1},{1,0},{2,3},{3,2},{4,5},{5,4},{6,7},{7,6},{8,9},{9,8},{10,11... | collective-permute-start | bytes 12582920 | tf_op jit(solution)/shard_map/ppermute | solution.py:396
  16.8 58.0 %collective-permute-start.1 = (bf16[3,1024,512]{2,1,0:T(8,128)(2,1)S(1)}, bf16[3,1024,512]{2,1,0:T(8,128)(2,1)}, u32[]{:S(2)}, u32[]{:S(2)}) collective-permute-start(bf16[3,1024,512]{2,1,0:T(8,128)(2,1)S(1)} %bitcast.18), channel_id=1, source_target_pairs={{0,1},{1,0},{2,3},{3,2},{4,5},{5,4},{6,7},{7,6},{8,9},{9,8},{10,11... | collective-permute-start | bytes 9437192 | tf_op jit(solution)/shard_map/ppermute | solution.py:396
  16.9 57.9 %collective-permute-start.2 = (bf16[512,1024]{1,0:T(8,128)(2,1)}, bf16[512,1024]{1,0:T(8,128)(2,1)}, u32[]{:S(2)}, u32[]{:S(2)}) collective-permute-start(bf16[512,1024]{1,0:T(8,128)(2,1)} %wo_own.1), channel_id=1, source_target_pairs={{0,1},{1,0},{2,3},{3,2},{4,5},{5,4},{6,7},{7,6},{8,9},{9,8},{10,11... | collective-permute-start | bytes 3145736 | tf_op jit(solution)/shard_map/ppermute | solution.py:396
  74.3 3.1 %collective-permute-start = (bf16[14,256,128]{2,1,0:T(8,128)(2,1)}, bf16[14,256,128]{2,1,0:T(8,128)(2,1)}, u32[]{:S(2)}, u32[]{:S(2)}) collective-permute-start(bf16[14,256,128]{2,1,0:T(8,128)(2,1)} %get-tuple-element.10), channel_id=1, source_target_pairs={{0,1},{1,0},{2,3},{3,2},{4,5},{5,4},{6,7},{7,6},{8,9},{9,8},{10,11... | collective-permute-start | bytes 2752520 | tf_op jit(solution)/shard_map/ppermute | solution.py:403
  77.3 1.9 %copy-start.1 = (bf16[1024,3,512]{2,0,1:T(8,128)(2,1)S(1)}, bf16[1024,3,512]{2,0,1:T(8,128)(2,1)}, u32[]{:S(2)}) copy-start(bf16[1024,3,512]{2,0,1:T(8,128)(2,1)} %param.14) | copy-start | bytes 9437188
  79.2 1.2 copy-start.2
  80.5 0.7 copy-start.5
  120.8 15.8 %collective-permute-start.6 = (bf16[896,512]{1,0:T(8,128)(2,1)S(1)}, bf16[896,512]{1,0:T(8,128)(2,1)S(1)}, u32[]{:S(2)}, u32[]{:S(2)}) collective-permute-start(bf16[896,512]{1,0:T(8,128)(2,1)S(1)} %get-tuple-element.13), channel_id=1, source_target_pairs={{0,1},{1,0},{2,3},{3,2},{4,5},{5,4},{6,7},{7,6},{8,9},{9,8},{10,11... | collective-permute-start | bytes 2752520 | tf_op jit(solution)/shard_map/ppermute | solution.py:408
  121.1 2.5 %collective-permute-start.5 = (bf16[112,512]{1,0:T(8,128)(2,1)S(1)}, bf16[112,512]{1,0:T(8,128)(2,1)S(1)}, u32[]{:S(2)}, u32[]{:S(2)}) collective-permute-start(bf16[112,512]{1,0:T(8,128)(2,1)S(1)} %slice_bitcast_fusion), channel_id=1, source_target_pairs={{0,1},{1,0},{2,3},{3,2},{4,5},{5,4},{6,7},{7,6},{8,9},{9,8},{10,11... | collective-permute-start | bytes 344072 | tf_op jit(solution)/shard_map/ppermute | solution.py:407
  124.8 22.7 %all-to-all-start.1 = ((bf16[64,4,512]{2,1,0:T(4,128)(2,1)}), bf16[64,4,512]{2,1,0:T(4,128)(2,1)S(1)}, u32[]{:S(2)}, u32[]{:S(2)}) async-start(bf16[64,4,512]{2,1,0:T(4,128)(2,1)} %reshape.31), calls=%async_computation.1 | async-start | bytes 524288 | tf_op jit(solution)/shard_map/all_to_all | solution.py:425

commit v6 on v5

--- a/solution.py
+++ b/solution.py
@@ -9,7 +9,7 @@
 
 HD = 64
 TILE = 1024
-PART = 448
+PART = 896
 SLOTS = 4
 SWAP = [(0, 1), (1, 0)]
 LANES = 128
@@ -171,10 +171,13 @@
     x_scr,
     qkv_scr,
     acc_scr,
+    wq,
+    wo,
     wu,
     wd,
     row_sems,
     x_sem,
+    q_sems,
     w_sems,
     out_sems,
 ):
@@ -195,16 +198,21 @@
         for r in range(rows)
     ]
     x_copies.append(pltpu.make_async_copy(x_other, x_scr.at[:, oth_at], x_sem))
+    q_copies = [
+        pltpu.make_async_copy(src.at[i], wq.at[3 * h + i], q_sems.at[3 * h + i])
+        for h, src in enumerate((wq_own, wq_oth))
+        for i in range(3)
+    ]
     w_copies = [
         pltpu.make_async_copy(src, dst.at[h], w_sems.at[i, h])
-        for h, srcs in enumerate(((wu_own, wd_own), (wu_oth, wd_oth)))
-        for i, (src, dst) in enumerate(zip(srcs, (wu, wd)))
+        for i, (srcs, dst) in enumerate((((wo_own, wo_oth), wo), ((wu_own, wu_oth), wu), ((wd_own, wd_oth), wd)))
+        for h, src in enumerate(srcs)
     ]
-    for copy in x_copies:
+    for copy in x_copies + q_copies[:2]:
         copy.start()
     for copy in x_copies:
         copy.wait()
-    for copy in w_copies:
+    for copy in q_copies[2:]:
         copy.start()
 
     def inputs(first, count):
@@ -214,12 +222,12 @@
         ]
         return jnp.concatenate(pieces, 1)
 
-    for h, wq in enumerate((wq_own, wq_oth)):
-        for i in range(3):
-            n = 3 * h + i
-            qkv_scr[:, n * half : (n + 1) * half] = jnp.dot(
-                inputs(0, rows), wq[i], preferred_element_type=jnp.float32
-            ).astype(jnp.bfloat16)
+    for n in range(6):
+        q_copies[n].wait()
+        w_copies[n].start()
+        qkv_scr[:, n * half : (n + 1) * half] = jnp.dot(
+            inputs(0, rows), wq[n], preferred_element_type=jnp.float32
+        ).astype(jnp.bfloat16)
 
     pair = 2 * HD
     block = (lax.broadcasted_iota(jnp.int32, (pair, pair), 0) < HD) == (
@@ -274,19 +282,21 @@
 
     lax.fori_loop(0, rows, attend, 0)
 
+    for copy in w_copies[:2]:
+        copy.wait()
     count = 2
     for m in range(rows // count):
         at = slice(m * count * seq, (m + 1) * count * seq)
-        mixed = jnp.dot(qkv_scr[at, :half], wo_own[...], preferred_element_type=jnp.float32)
+        mixed = jnp.dot(qkv_scr[at, :half], wo[0], preferred_element_type=jnp.float32)
         mixed += jnp.dot(
-            qkv_scr[at, 3 * half : 4 * half], wo_oth[...], preferred_element_type=jnp.float32
+            qkv_scr[at, 3 * half : 4 * half], wo[1], preferred_element_type=jnp.float32
         )
         mixed = mixed + inputs(m * count, count).astype(jnp.float32)
         normed = norm(mixed, gain_attn[...]).astype(jnp.bfloat16)
         qkv_scr[at, half : 3 * half] = normed
         acc_scr[at, :] = normed.astype(jnp.float32)
 
-    for copy in w_copies:
+    for copy in w_copies[2:]:
         copy.wait()
     tiles = wu.shape[2] // TILE
     parts = tokens // PART
@@ -352,7 +362,7 @@
     model = 2 * half
     wu, wd = weights[4], weights[6]
     flops = 2 * tokens * model * (3 * model + model + 4 * wu.shape[1])
-    any_spec = pl.BlockSpec(memory_space=pl.ANY)
+    any_spec = pl.BlockSpec(memory_space=pltpu.HBM)
     vmem = pl.BlockSpec(memory_space=pltpu.VMEM)
     return pl.pallas_call(
         layer_kernel,
@@ -362,20 +372,24 @@
             jax.ShapeDtypeStruct((2, rows * 8, half), jnp.bfloat16),
         ),
         in_specs=[pl.BlockSpec(memory_space=pltpu.SMEM)] * 2
-        + [any_spec] * 2 + [vmem] * 4 + [any_spec] * 4 + [vmem] * 2,
+        + [any_spec] * 10
+        + [vmem] * 2,
         out_specs=(any_spec, any_spec, vmem),
         scratch_shapes=[
             pltpu.VMEM((rows, 2 * body, LANES), jnp.bfloat16),
             pltpu.VMEM((tokens, 3 * model), jnp.bfloat16),
             pltpu.VMEM((tokens, model), jnp.float32),
+            pltpu.VMEM((6, model, half), jnp.bfloat16),
+            pltpu.VMEM((2, half, model), jnp.bfloat16),
             pltpu.VMEM((2,) + wu.shape, jnp.bfloat16),
             pltpu.VMEM((2,) + wd.shape, jnp.bfloat16),
             pltpu.SemaphoreType.DMA((rows,)),
             pltpu.SemaphoreType.DMA,
-            pltpu.SemaphoreType.DMA((2, 2)),
+            pltpu.SemaphoreType.DMA((6,)),
+            pltpu.SemaphoreType.DMA((3, 2)),
             pltpu.SemaphoreType.DMA((rows // 2, 2)),
         ],
-        compiler_params=pltpu.CompilerParams(vmem_limit_bytes=46 * 1024 * 1024),
+        compiler_params=pltpu.CompilerParams(vmem_limit_bytes=60 * 1024 * 1024),
         cost_estimate=pl.CostEstimate(
             flops=flops, bytes_accessed=28 * 1024 * 1024, transcendentals=0
         ),
@@ -405,6 +419,7 @@
         core, info, received, x_other, weights, gain_attn[None], gain_ffn[None]
     )
     emb_recv = lax.ppermute(emb[1], "mp", SWAP)
+    enc_oth, emb_recv = lax.optimization_barrier((enc_oth, emb_recv))
     enc_recv = lax.ppermute(enc_oth, "mp", SWAP)
 
     owners = owner.reshape(-1)

time: 149 us -> 147 us (0.987)
  local copies, waits for them, and re-layouts: 6.24 us -> 4.34 us
    unnamed x16 -> x10, local copies, waits for them, and re-layouts: 4.03 us -> 1.14 us
  transfers between devices with their start and end apart: 9 -> 9, of which waited for: 4 -> 4; matrix products, arithmetic and copies ran while one was open for 2% -> 3% of each run, Pallas kernels for 3% -> 3%
where the time goes in v6:
time: 147 us; the launch traced here: 146 us
  waiting for transfers between devices  66.1 us (45%)
  Pallas kernels  46.3 us (31%)
  starting transfers between devices  25.4 us (17%)
  local copies, waits for them, and re-layouts  4.34 us (3%)
  other arithmetic  1.73 us (1%)
    all_to_all x1, waiting for transfers between devices, shards(): lax.all_to_all(pack(dest, doc_ids, tokens, devices), 'dp', split_axis=0,...  52.9 us
    pallas_call x1, Pallas kernels, layer(): pl.pallas_call(layer_kernel, out_shape=(jax.ShapeDtypeStruct((tokens, hal...  38.7 us
    all_to_all x1, starting transfers between devices, shards(): lax.all_to_all(pack(dest, doc_ids, tokens, devices), 'dp', split_axis=0,...  11.9 us
    all_to_all x1, starting transfers between devices, shards(): lax.all_to_all(sending.reshape(devices, SLOTS, half), 'dp', split_axis=0,...  11.8 us
    all_to_all x1, waiting for transfers between devices, shards(): lax.all_to_all(sending.reshape(devices, SLOTS, half), 'dp', split_axis=0,...  9.52 us
    pallas_call x1, Pallas kernels, unpack(): pl.pallas_call(unpack_kernel, out_shape=(jax.ShapeDtypeStruct((rows, body...  4.04 us
    pallas_call x1, Pallas kernels, pack(): pl.pallas_call(pack_kernel, out_shape=jax.ShapeDtypeStruct((slots, body +...  3.56 us
  transfers between devices with their start and end apart: 9, of which 4 were waited for; matrix products, arithmetic and copies ran while one was open for 3% of the time, Pallas kernels for 3%

profile of v6, /device:TPU:0, one launch (start us, length us, event | category | flops | bytes accessed | tf_op | source)
XLA Modules:
  0.0 146.0 jit_solution(12620916486769296923)
XLA Ops:
  0.6 3.6 %pack_rows.1 = bf16[64,264,128]{2,1,0:T(8,128)(2,1)} custom-call(s32[28]{0:T(128)} %dest.1, s32[28,64]{1,0:T(8,128)} %doc_ids.1, bf16[28,64,512]{2,1,0:T(8,128)(2,1)} %tokens.1), custom_call_target="tpu_custom_call" | custom-call | tf_op jit(solution)/shard_map/pack_rows/pallas_call | solution.py:70
  4.2 0.0 copy-start.2
  4.2 11.9 %all-to-all-start = ((bf16[64,264,128]{2,1,0:T(8,128)(2,1)}), bf16[64,264,128]{2,1,0:T(8,128)(2,1)}, u32[]{:S(2)}, u32[]{:S(2)}) async-start(bf16[64,264,128]{2,1,0:T(8,128)(2,1)} %pack_rows.1), calls=%async_computation | async-start | bytes 8650752 | tf_op jit(solution)/shard_map/all_to_all | solution.py:412
  16.1 0.1 collective-permute-start.3
  16.2 0.5 collective-permute-start.4
  16.7 0.0 copy-done.2
  16.7 0.1 collective-permute-start.1
  16.8 0.4 collective-permute-start.2
  17.2 52.9 %all-to-all-done.received = bf16[64,264,128]{2,1,0:T(8,128)(2,1)} async-done(((bf16[64,264,128]{2,1,0:T(8,128)(2,1)}), bf16[64,264,128]{2,1,0:T(8,128)(2,1)}, u32[]{:S(2)}, u32[]{:S(2)}) %all-to-all-start) | async-done | bytes 4325408 | tf_op jit(solution)/shard_map/all_to_all | solution.py:412
  70.2 4.0 %unpack_rows.1 = (bf16[14,256,128]{2,1,0:T(8,128)(2,1)}, s32[8,128]{1,0:T(8,128)}) custom-call(s32[1]{0:T(128)} %bitcast.1.core, bf16[64,264,128]{2,1,0:T(8,128)(2,1)} %all-to-all-done.received), custom_call_target="tpu_custom_call" | custom-call | tf_op jit(solution)/shard_map/unpack_rows/pallas_call | solution.py:127
  74.2 0.3 collective-permute-start
  74.5 0.0 collective-permute-done.2.wo_oth
  74.5 0.0 collective-permute-done.1.wq_oth
  74.5 0.0 collective-permute-done.3.wu_oth
  74.5 0.0 collective-permute-done.4.wd_oth
  74.5 2.6 %collective-permute-done.x_other = bf16[14,256,128]{2,1,0:T(8,128)(2,1)S(1)} collective-permute-done((bf16[14,256,128]{2,1,0:T(8,128)(2,1)}, bf16[14,256,128]{2,1,0:T(8,128)(2,1)S(1)}, u32[]{:S(2)}, u32[]{:S(2)}) %collective-permute-start) | collective-permute-done | bytes 917536 | tf_op jit(solution)/shard_map/ppermute | solution.py:417
  77.2 0.0 copy-start.3
  77.2 0.9 copy-done.3
  78.1 0.0 copy-start.1
  78.1 38.7 %layer.1 = (bf16[896,512]{1,0:T(8,128)(2,1)}, bf16[896,512]{1,0:T(8,128)(2,1)}, bf16[2,112,512]{2,1,0:T(8,128)(2,1)}) custom-call(s32[1]{0:T(128)} %bitcast.1.core, s32[8,128]{1,0:T(8,128)} %get-tuple-element.11.info, bf16[64,264,128]{2,1,0:T(8,128)(2,1)} %all-to-all-done.received, bf16[14,256,128]{2,1,0:T(8,128)(2,1)} %copy-done.3, ...), custom_call_target="tpu_custom_call" | custom-call | flops 22548578304 | bytes 29360128 | tf_op jit(solution)/shard_map/layer/pallas_call | solution.py:367
  116.8 0.0 copy-start
  116.9 1.0 slice_bitcast_fusion
  117.8 0.1 collective-permute-start.5
  118.0 0.0 copy-done.1
  118.0 0.1 copy.17
  118.1 0.1 eq.48
  118.2 1.0 collective-permute-done.5
  119.2 0.2 collective-permute-start.6
  119.3 0.2 convert_reduce_fusion
  119.5 0.1 reduce_sum.12
  119.6 0.1 copy.18
  119.7 0.1 mul.12
  119.8 0.1 copy.20
  119.9 0.1 reshape.30
  120.0 0.2 fusion.1
  120.2 1.1 fusion
  121.4 0.8 reshape.31
  122.1 11.8 %all-to-all-start.1 = ((bf16[64,4,512]{2,1,0:T(4,128)(2,1)}), bf16[64,4,512]{2,1,0:T(4,128)(2,1)S(1)}, u32[]{:S(2)}, u32[]{:S(2)}) async-start(bf16[64,4,512]{2,1,0:T(4,128)(2,1)} %reshape.31), calls=%async_computation.1 | async-start | bytes 524288 | tf_op jit(solution)/shard_map/all_to_all | solution.py:440
  134.0 0.0 collective-permute-done.6
  134.0 0.0 copy-done
  134.0 0.1 broadcast_select_fusion.1
  134.1 1.4 pad_maximum_fusion
  135.5 9.5 %all-to-all-done.1 = bf16[64,4,512]{2,1,0:T(4,128)(2,1)S(1)} async-done(((bf16[64,4,512]{2,1,0:T(4,128)(2,1)}), bf16[64,4,512]{2,1,0:T(4,128)(2,1)S(1)}, u32[]{:S(2)}, u32[]{:S(2)}) %all-to-all-start.1) | async-done | bytes 262176 | tf_op jit(solution)/shard_map/all_to_all | solution.py:440
  145.1 0.9 reshape.35
  (5 shorter events, 0.1 us)
Async XLA Ops:
  4.2 12.5 %copy-start.2 = (bf16[1024,3,512]{2,0,1:T(8,128)(2,1)S(1)}, bf16[1024,3,512]{2,0,1:T(8,128)(2,1)}, u32[]{:S(2)}) copy-start(bf16[1024,3,512]{2,0,1:T(8,128)(2,1)} %param.14) | copy-start | bytes 9437188
  4.2 66.0 %all-to-all-start = ((bf16[64,264,128]{2,1,0:T(8,128)(2,1)}), bf16[64,264,128]{2,1,0:T(8,128)(2,1)}, u32[]{:S(2)}, u32[]{:S(2)}) async-start(bf16[64,264,128]{2,1,0:T(8,128)(2,1)} %pack_rows.1), calls=%async_computation | async-start | bytes 8650752 | tf_op jit(solution)/shard_map/all_to_all | solution.py:412
  16.1 58.4 %collective-permute-start.3 = (bf16[1024,2048]{1,0:T(8,128)(2,1)}, bf16[1024,2048]{1,0:T(8,128)(2,1)}, u32[]{:S(2)}, u32[]{:S(2)}) collective-permute-start(bf16[1024,2048]{1,0:T(8,128)(2,1)} %wu_own.1), channel_id=1, source_target_pairs={{0,1},{1,0},{2,3},{3,2},{4,5},{5,4},{6,7},{7,6},{8,9},{9,8},{10,11... | collective-permute-start | bytes 12582920 | tf_op jit(solution)/shard_map/ppermute | solution.py:410
  16.2 58.3 %collective-permute-start.4 = (bf16[2048,1024]{1,0:T(8,128)(2,1)}, bf16[2048,1024]{1,0:T(8,128)(2,1)}, u32[]{:S(2)}, u32[]{:S(2)}) collective-permute-start(bf16[2048,1024]{1,0:T(8,128)(2,1)} %wd_own.1), channel_id=1, source_target_pairs={{0,1},{1,0},{2,3},{3,2},{4,5},{5,4},{6,7},{7,6},{8,9},{9,8},{10,11... | collective-permute-start | bytes 12582920 | tf_op jit(solution)/shard_map/ppermute | solution.py:410
  16.7 57.8 %collective-permute-start.1 = (bf16[3,1024,512]{2,1,0:T(8,128)(2,1)S(1)}, bf16[3,1024,512]{2,1,0:T(8,128)(2,1)}, u32[]{:S(2)}, u32[]{:S(2)}) collective-permute-start(bf16[3,1024,512]{2,1,0:T(8,128)(2,1)S(1)} %bitcast.21), channel_id=1, source_target_pairs={{0,1},{1,0},{2,3},{3,2},{4,5},{5,4},{6,7},{7,6},{8,9},{9,8},{10,11... | collective-permute-start | bytes 9437192 | tf_op jit(solution)/shard_map/ppermute | solution.py:410
  16.8 57.7 %collective-permute-start.2 = (bf16[512,1024]{1,0:T(8,128)(2,1)}, bf16[512,1024]{1,0:T(8,128)(2,1)}, u32[]{:S(2)}, u32[]{:S(2)}) collective-permute-start(bf16[512,1024]{1,0:T(8,128)(2,1)} %wo_own.1), channel_id=1, source_target_pairs={{0,1},{1,0},{2,3},{3,2},{4,5},{5,4},{6,7},{7,6},{8,9},{9,8},{10,11... | collective-permute-start | bytes 3145736 | tf_op jit(solution)/shard_map/ppermute | solution.py:410
  74.2 2.9 %collective-permute-start = (bf16[14,256,128]{2,1,0:T(8,128)(2,1)}, bf16[14,256,128]{2,1,0:T(8,128)(2,1)S(1)}, u32[]{:S(2)}, u32[]{:S(2)}) collective-permute-start(bf16[14,256,128]{2,1,0:T(8,128)(2,1)} %get-tuple-element.12), channel_id=1, source_target_pairs={{0,1},{1,0},{2,3},{3,2},{4,5},{5,4},{6,7},{7,6},{8,9},{9,8},{10,11... | collective-permute-start | bytes 2752520 | tf_op jit(solution)/shard_map/ppermute | solution.py:417
  77.2 0.9 copy-start.3
  78.1 39.9 %copy-start.1 = (s32[28,4]{0,1:T(4,128)S(1)}, s32[28,4]{0,1:T(4,128)}, u32[]{:S(2)}) copy-start(s32[28,4]{0,1:T(4,128)} %param.13) | copy-start | bytes 1348
  116.8 17.1 %copy-start = (bf16[896,512]{1,0:T(8,128)(2,1)S(1)}, bf16[896,512]{1,0:T(8,128)(2,1)}, u32[]{:S(2)}) copy-start(bf16[896,512]{1,0:T(8,128)(2,1)} %get-tuple-element.16) | copy-start | bytes 2752516
  117.8 1.3 collective-permute-start.5
  119.2 14.8 %collective-permute-start.6 = (bf16[896,512]{1,0:T(8,128)(2,1)}, bf16[896,512]{1,0:T(8,128)(2,1)S(1)}, u32[]{:S(2)}, u32[]{:S(2)}) collective-permute-start(bf16[896,512]{1,0:T(8,128)(2,1)} %get-tuple-element.17), channel_id=1, source_target_pairs={{0,1},{1,0},{2,3},{3,2},{4,5},{5,4},{6,7},{7,6},{8,9},{9,8},{10,11... | collective-permute-start | bytes 2752520 | tf_op jit(solution)/shard_map/ppermute | solution.py:423
  122.1 22.9 %all-to-all-start.1 = ((bf16[64,4,512]{2,1,0:T(4,128)(2,1)}), bf16[64,4,512]{2,1,0:T(4,128)(2,1)S(1)}, u32[]{:S(2)}, u32[]{:S(2)}) async-start(bf16[64,4,512]{2,1,0:T(4,128)(2,1)} %reshape.31), calls=%async_computation.1 | async-start | bytes 524288 | tf_op jit(solution)/shard_map/all_to_all | solution.py:440

commit v7 on v6

--- a/solution.py
+++ b/solution.py
@@ -89,7 +89,9 @@
     )(dest, doc_ids, tokens)
 
 
-def unpack_kernel(core, received, out, info, facts, table, fact_sem, info_sem, sems):
+def unpack_kernel(
+    core, received, out, info, facts, table, scalars, staged, fact_sem, info_sem, sems, out_sem
+):
     rows, body, _ = out.shape
     slots = received.shape[0]
     load = pltpu.make_async_copy(received.at[:, pl.ds(body, FACTS)], facts, fact_sem)
@@ -100,50 +102,55 @@
     here = values[:, :, :1] == (lax.broadcasted_iota(jnp.int32, shape, 2) + 1).astype(jnp.float32)
     source = lax.broadcasted_iota(jnp.int32, shape, 0).astype(jnp.float32)
     result = jnp.sum(jnp.where(here, source, 0.0), 0)
-    kind = lax.broadcasted_iota(jnp.int32, (FACTS, LANES), 0)
-    for k in range(1, 4):
-        bound = jnp.sum(jnp.where(here, values[:, :, k : k + 1], 0.0), 0)
-        result = jnp.where(kind == k, bound, result)
-    table[...] = result.astype(jnp.int32)
-    keep = pltpu.make_async_copy(table, info, info_sem)
+    table[0] = result.astype(jnp.int32)
+    keep = pltpu.make_async_copy(table.at[0], scalars, info_sem.at[0])
     keep.start()
     keep.wait()
     first = (1 - core[0]) * rows
     copies = [
         pltpu.make_async_copy(
-            received.at[info[0, first + r], pl.ds(0, body)], out.at[r], sems.at[r]
+            received.at[scalars[0, first + r], pl.ds(0, body)], staged.at[r], sems.at[r]
         )
         for r in range(rows)
     ]
     for copy in copies:
         copy.start()
+    kind = lax.broadcasted_iota(jnp.int32, (FACTS, LANES), 0)
+    for k in range(1, 4):
+        bound = jnp.sum(jnp.where(here, values[:, :, k : k + 1], 0.0), 0)
+        result = jnp.where(kind == k, bound, result)
+    table[1] = result.astype(jnp.int32)
+    keep = pltpu.make_async_copy(table.at[1], info, info_sem.at[1])
+    keep.start()
     for copy in copies:
         copy.wait()
+    store = pltpu.make_async_copy(staged, out, out_sem)
+    store.start()
+    store.wait()
+    keep.wait()
 
 
 def unpack(core, received, rows):
     slots = received.shape[0]
     body = received.shape[1] - FACTS
+    hbm = pl.BlockSpec(memory_space=pltpu.HBM)
     return pl.pallas_call(
         unpack_kernel,
         out_shape=(
             jax.ShapeDtypeStruct((rows, body, LANES), received.dtype),
             jax.ShapeDtypeStruct((FACTS, LANES), jnp.int32),
         ),
-        in_specs=[
-            pl.BlockSpec(memory_space=pltpu.SMEM),
-            pl.BlockSpec(memory_space=pltpu.HBM),
-        ],
-        out_specs=(
-            pl.BlockSpec(memory_space=pltpu.VMEM),
-            pl.BlockSpec(memory_space=pltpu.SMEM),
-        ),
+        in_specs=[pl.BlockSpec(memory_space=pltpu.SMEM), hbm],
+        out_specs=(hbm, hbm),
         scratch_shapes=[
             pltpu.VMEM((slots, FACTS, LANES), received.dtype),
-            pltpu.VMEM((FACTS, LANES), jnp.int32),
+            pltpu.VMEM((2, FACTS, LANES), jnp.int32),
+            pltpu.SMEM((FACTS, LANES), jnp.int32),
+            pltpu.VMEM((rows, body, LANES), received.dtype),
             pltpu.SemaphoreType.DMA,
+            pltpu.SemaphoreType.DMA((2,)),
+            pltpu.SemaphoreType.DMA((rows,)),
             pltpu.SemaphoreType.DMA,
-            pltpu.SemaphoreType.DMA((rows,)),
         ],
         compiler_params=pltpu.CompilerParams(vmem_limit_bytes=60 * 1024 * 1024),
         name="unpack_rows",
@@ -152,7 +159,7 @@
 
 def layer_kernel(
     core,
-    info,
+    table,
     received,
     x_other,
     wq_own,
@@ -167,9 +174,12 @@
     gain_ffn,
     enc_own,
     enc_oth,
-    emb,
+    emb_own,
+    emb_oth,
+    info,
     x_scr,
     qkv_scr,
+    emb_scr,
     acc_scr,
     wq,
     wo,
@@ -179,6 +189,7 @@
     x_sem,
     q_sems,
     w_sems,
+    info_sem,
     out_sems,
 ):
     rows = x_scr.shape[0]
@@ -189,28 +200,34 @@
     body = half * seq // LANES
     me = core[0]
     first_row = me * rows
+    facts = pltpu.make_async_copy(table, info, info_sem)
+    facts.start()
     own_at = pl.ds(pl.multiple_of(me * body, body), body)
     oth_at = pl.ds(pl.multiple_of((1 - me) * body, body), body)
-    x_copies = [
-        pltpu.make_async_copy(
-            received.at[info[0, first_row + r], pl.ds(0, body)], x_scr.at[r, own_at], row_sems.at[r]
-        )
-        for r in range(rows)
-    ]
-    x_copies.append(pltpu.make_async_copy(x_other, x_scr.at[:, oth_at], x_sem))
+    x_copies = [pltpu.make_async_copy(x_other, x_scr.at[:, oth_at], x_sem)]
     q_copies = [
         pltpu.make_async_copy(src.at[i], wq.at[3 * h + i], q_sems.at[3 * h + i])
         for h, src in enumerate((wq_own, wq_oth))
         for i in range(3)
     ]
-    w_copies = [
-        pltpu.make_async_copy(src, dst.at[h], w_sems.at[i, h])
-        for i, (srcs, dst) in enumerate((((wo_own, wo_oth), wo), ((wu_own, wu_oth), wu), ((wd_own, wd_oth), wd)))
-        for h, src in enumerate(srcs)
-    ]
     for copy in x_copies + q_copies[:2]:
         copy.start()
-    for copy in x_copies:
+    facts.wait()
+    row_copies = [
+        pltpu.make_async_copy(
+            received.at[info[0, first_row + r], pl.ds(0, body)], x_scr.at[r, own_at], row_sems.at[r]
+        )
+        for r in range(rows)
+    ]
+    w_pairs = ((wo_own, wo_oth, wo), (wu_own, wu_oth, wu), (wd_own, wd_oth, wd))
+    w_copies = [
+        pltpu.make_async_copy(pair[h], pair[2].at[h], w_sems.at[i, h])
+        for i, pair in enumerate(w_pairs)
+        for h in range(2)
+    ]
+    for copy in row_copies:
+        copy.start()
+    for copy in x_copies + row_copies:
         copy.wait()
     for copy in q_copies[2:]:
         copy.start()
@@ -349,13 +366,17 @@
         pooled = pooled * (1.0 / jnp.maximum(total, 1.0))
         square = jnp.mean(pooled * pooled, -1, keepdims=True)
         embedded = (pooled * lax.rsqrt(square + 1e-06)).astype(jnp.bfloat16)
-        emb[me, m * 16 : (m + 1) * 16, :] = embedded[:, :half]
-        emb[1 - me, m * 16 : (m + 1) * 16, :] = embedded[:, half:]
+        emb_scr[0, m * 16 : (m + 1) * 16, :] = embedded[:, :half]
+        emb_scr[1, m * 16 : (m + 1) * 16, :] = embedded[:, half:]
+    for i, out in enumerate((emb_own, emb_oth)):
+        which = me if i == 0 else 1 - me
+        outs.append(pltpu.make_async_copy(emb_scr.at[which], out, out_sems.at[rows // 2, i]))
+        outs[-1].start()
     for copy in outs:
         copy.wait()
 
 
-def layer(core, info, received, x_other, weights, gain_attn, gain_ffn):
+def layer(core, table, received, x_other, weights, gain_attn, gain_ffn):
     rows, body, _ = x_other.shape
     half = body * LANES // HD
     tokens = rows * HD
@@ -369,15 +390,18 @@
         out_shape=(
             jax.ShapeDtypeStruct((tokens, half), jnp.bfloat16),
             jax.ShapeDtypeStruct((tokens, half), jnp.bfloat16),
-            jax.ShapeDtypeStruct((2, rows * 8, half), jnp.bfloat16),
+            jax.ShapeDtypeStruct((rows * 8, half), jnp.bfloat16),
+            jax.ShapeDtypeStruct((rows * 8, half), jnp.bfloat16),
         ),
-        in_specs=[pl.BlockSpec(memory_space=pltpu.SMEM)] * 2
-        + [any_spec] * 10
+        in_specs=[pl.BlockSpec(memory_space=pltpu.SMEM)]
+        + [any_spec] * 11
         + [vmem] * 2,
-        out_specs=(any_spec, any_spec, vmem),
+        out_specs=(any_spec,) * 4,
         scratch_shapes=[
+            pltpu.SMEM(table.shape, jnp.int32),
             pltpu.VMEM((rows, 2 * body, LANES), jnp.bfloat16),
             pltpu.VMEM((tokens, 3 * model), jnp.bfloat16),
+            pltpu.VMEM((2, rows * 8, half), jnp.bfloat16),
             pltpu.VMEM((tokens, model), jnp.float32),
             pltpu.VMEM((6, model, half), jnp.bfloat16),
             pltpu.VMEM((2, half, model), jnp.bfloat16),
@@ -387,14 +411,15 @@
             pltpu.SemaphoreType.DMA,
             pltpu.SemaphoreType.DMA((6,)),
             pltpu.SemaphoreType.DMA((3, 2)),
-            pltpu.SemaphoreType.DMA((rows // 2, 2)),
+            pltpu.SemaphoreType.DMA,
+            pltpu.SemaphoreType.DMA((rows // 2 + 1, 2)),
         ],
         compiler_params=pltpu.CompilerParams(vmem_limit_bytes=60 * 1024 * 1024),
         cost_estimate=pl.CostEstimate(
             flops=flops, bytes_accessed=28 * 1024 * 1024, transcendentals=0
         ),
         name="layer",
-    )(core, info, received, x_other, *weights, gain_attn, gain_ffn)
+    )(core, table, received, x_other, *weights, gain_attn, gain_ffn)
 
 
 def shards(tokens, doc_ids, dest, owner, w_qkv, w_out, gain_attn, w_up, w_down, gain_ffn):
@@ -415,10 +440,10 @@
     core = me.astype(jnp.int32)[None]
     x_send, info = unpack(core, received, mine)
     x_other = lax.ppermute(x_send, "mp", SWAP)
-    enc_own, enc_oth, emb = layer(
+    enc_own, enc_oth, emb_own, emb_oth = layer(
         core, info, received, x_other, weights, gain_attn[None], gain_ffn[None]
     )
-    emb_recv = lax.ppermute(emb[1], "mp", SWAP)
+    emb_recv = lax.ppermute(emb_oth, "mp", SWAP)
     enc_oth, emb_recv = lax.optimization_barrier((enc_oth, emb_recv))
     enc_recv = lax.ppermute(enc_oth, "mp", SWAP)
 
@@ -434,7 +459,7 @@
     place_own = (lax.dynamic_index_in_dim(target, me, 0) == out_slot).astype(jnp.bfloat16)
     place_oth = (lax.dynamic_index_in_dim(target, 1 - me, 0) == out_slot).astype(jnp.bfloat16)
     sending = (
-        jnp.dot(place_own, emb[0], preferred_element_type=jnp.float32)
+        jnp.dot(place_own, emb_own, preferred_element_type=jnp.float32)
         + jnp.dot(place_oth, emb_recv, preferred_element_type=jnp.float32)
     ).astype(jnp.bfloat16)
     got = lax.all_to_all(

time: 147 us -> 145 us (0.986)
  no operation moved by 1% of the time
where the time goes in v7:
time: 145 us
  waiting for transfers between devices  66.3 us (46%)
  Pallas kernels  45.8 us (32%)
  starting transfers between devices  25.6 us (18%)
  local copies, waits for them, and re-layouts  3.35 us (2%)
  other arithmetic  1.73 us (1%)
    all_to_all x1, waiting for transfers between devices, shards(): lax.all_to_all(pack(dest, doc_ids, tokens, devices), 'dp', split_axis=0,...  52.9 us
    pallas_call x1, Pallas kernels, layer(): pl.pallas_call(layer_kernel, out_shape=(jax.ShapeDtypeStruct((tokens, hal...  38.4 us
    all_to_all x1, starting transfers between devices, shards(): lax.all_to_all(pack(dest, doc_ids, tokens, devices), 'dp', split_axis=0,...  12 us
    all_to_all x1, starting transfers between devices, shards(): lax.all_to_all(sending.reshape(devices, SLOTS, half), 'dp', split_axis=0,...  11.8 us
    all_to_all x1, waiting for transfers between devices, shards(): lax.all_to_all(sending.reshape(devices, SLOTS, half), 'dp', split_axis=0,...  9.52 us
    pallas_call x1, Pallas kernels, unpack(): pl.pallas_call(unpack_kernel, out_shape=(jax.ShapeDtypeStruct((rows, body...  3.93 us
    pallas_call x1, Pallas kernels, pack(): pl.pallas_call(pack_kernel, out_shape=jax.ShapeDtypeStruct((slots, body +...  3.5 us
  transfers between devices with their start and end apart: 9, of which 4 were waited for; matrix products, arithmetic and copies ran while one was open for 3% of the time, Pallas kernels for 3%

profile of v7, /device:TPU:0, one launch (start us, length us, event | category | flops | bytes accessed | tf_op | source)
XLA Modules:
  0.0 144.9 jit_solution(1967074766597879959)
XLA Ops:
  0.6 3.5 %pack_rows.1 = bf16[64,264,128]{2,1,0:T(8,128)(2,1)} custom-call(s32[28]{0:T(128)} %dest.1, s32[28,64]{1,0:T(8,128)} %doc_ids.1, bf16[28,64,512]{2,1,0:T(8,128)(2,1)} %tokens.1), custom_call_target="tpu_custom_call" | custom-call | tf_op jit(solution)/shard_map/pack_rows/pallas_call | solution.py:70
  4.1 0.0 copy-start.2
  4.2 12.0 %all-to-all-start = ((bf16[64,264,128]{2,1,0:T(8,128)(2,1)}), bf16[64,264,128]{2,1,0:T(8,128)(2,1)}, u32[]{:S(2)}, u32[]{:S(2)}) async-start(bf16[64,264,128]{2,1,0:T(8,128)(2,1)} %pack_rows.1), calls=%async_computation | async-start | bytes 8650752 | tf_op jit(solution)/shard_map/all_to_all | solution.py:437
  16.2 0.1 collective-permute-start.3
  16.2 0.5 collective-permute-start.4
  16.7 0.0 copy-done.2
  16.7 0.1 collective-permute-start.1
  16.8 0.4 collective-permute-start.2
  17.3 52.9 %all-to-all-done.received = bf16[64,264,128]{2,1,0:T(8,128)(2,1)} async-done(((bf16[64,264,128]{2,1,0:T(8,128)(2,1)}), bf16[64,264,128]{2,1,0:T(8,128)(2,1)}, u32[]{:S(2)}, u32[]{:S(2)}) %all-to-all-start) | async-done | bytes 4325408 | tf_op jit(solution)/shard_map/all_to_all | solution.py:437
  70.2 3.9 %unpack_rows.1 = (bf16[14,256,128]{2,1,0:T(8,128)(2,1)}, s32[8,128]{1,0:T(8,128)}) custom-call(s32[1]{0:T(128)} %bitcast.1.core, bf16[64,264,128]{2,1,0:T(8,128)(2,1)} %all-to-all-done.received), custom_call_target="tpu_custom_call" | custom-call | tf_op jit(solution)/shard_map/unpack_rows/pallas_call | solution.py:137
  74.1 0.3 collective-permute-start
  74.4 0.0 collective-permute-done.2.wo_oth
  74.4 0.0 collective-permute-done.1.wq_oth
  74.4 0.0 collective-permute-done.3.wu_oth
  74.4 0.0 collective-permute-done.4.wd_oth
  74.4 2.6 %collective-permute-done.x_other = bf16[14,256,128]{2,1,0:T(8,128)(2,1)S(1)} collective-permute-done((bf16[14,256,128]{2,1,0:T(8,128)(2,1)}, bf16[14,256,128]{2,1,0:T(8,128)(2,1)S(1)}, u32[]{:S(2)}, u32[]{:S(2)}) %collective-permute-start) | collective-permute-done | bytes 917536 | tf_op jit(solution)/shard_map/ppermute | solution.py:442
  77.1 0.0 copy-start.3
  77.1 0.9 copy-done.3
  78.0 0.0 copy-start.1
  78.0 38.4 %layer.1 = (bf16[896,512]{1,0:T(8,128)(2,1)}, bf16[896,512]{1,0:T(8,128)(2,1)}, bf16[112,512]{1,0:T(8,128)(2,1)}, bf16[112,512]{1,0:T(8,128)(2,1)}) custom-call(s32[1]{0:T(128)} %bitcast.1.core, s32[8,128]{1,0:T(8,128)} %get-tuple-element.12.table, bf16[64,264,128]{2,1,0:T(8,128)(2,1)} %all-to-all-done.received, bf16[14,256,128]{2,1,0:T(8,128)(2,1)} %copy-done.3, ...), custom_call_target="tpu_custom_call" | custom-call | flops 22548578304 | bytes 29360128 | tf_op jit(solution)/shard_map/layer/pallas_call | solution.py:388
  116.4 0.0 copy-start
  116.4 0.2 collective-permute-start.5
  116.6 0.0 copy-done.1
  116.7 0.1 copy.17
  116.8 0.1 eq.48
  116.9 1.2 collective-permute-done.5
  118.0 0.2 collective-permute-start.6
  118.2 0.2 convert_reduce_fusion
  118.4 0.1 reduce_sum.12
  118.5 0.1 copy.18
  118.6 0.1 mul.12
  118.7 0.1 copy.20
  118.8 0.1 reshape.30
  118.9 0.2 fusion.1
  119.1 1.1 fusion
  120.2 0.8 reshape.31
  121.0 11.8 %all-to-all-start.1 = ((bf16[64,4,512]{2,1,0:T(4,128)(2,1)}), bf16[64,4,512]{2,1,0:T(4,128)(2,1)S(1)}, u32[]{:S(2)}, u32[]{:S(2)}) async-start(bf16[64,4,512]{2,1,0:T(4,128)(2,1)} %reshape.31), calls=%async_computation.1 | async-start | bytes 524288 | tf_op jit(solution)/shard_map/all_to_all | solution.py:465
  132.8 0.0 collective-permute-done.6
  132.9 0.0 copy-done
  132.9 0.1 broadcast_select_fusion.1
  133.0 1.4 pad_maximum_fusion
  134.4 9.5 %all-to-all-done.1 = bf16[64,4,512]{2,1,0:T(4,128)(2,1)S(1)} async-done(((bf16[64,4,512]{2,1,0:T(4,128)(2,1)}), bf16[64,4,512]{2,1,0:T(4,128)(2,1)S(1)}, u32[]{:S(2)}, u32[]{:S(2)}) %all-to-all-start.1) | async-done | bytes 262176 | tf_op jit(solution)/shard_map/all_to_all | solution.py:465
  144.0 0.9 reshape.35
  (5 shorter events, 0.1 us)
Async XLA Ops:
  4.1 12.6 %copy-start.2 = (bf16[1024,3,512]{2,0,1:T(8,128)(2,1)S(1)}, bf16[1024,3,512]{2,0,1:T(8,128)(2,1)}, u32[]{:S(2)}) copy-start(bf16[1024,3,512]{2,0,1:T(8,128)(2,1)} %param.14) | copy-start | bytes 9437188
  4.2 66.0 %all-to-all-start = ((bf16[64,264,128]{2,1,0:T(8,128)(2,1)}), bf16[64,264,128]{2,1,0:T(8,128)(2,1)}, u32[]{:S(2)}, u32[]{:S(2)}) async-start(bf16[64,264,128]{2,1,0:T(8,128)(2,1)} %pack_rows.1), calls=%async_computation | async-start | bytes 8650752 | tf_op jit(solution)/shard_map/all_to_all | solution.py:437
  16.2 58.3 %collective-permute-start.3 = (bf16[1024,2048]{1,0:T(8,128)(2,1)}, bf16[1024,2048]{1,0:T(8,128)(2,1)}, u32[]{:S(2)}, u32[]{:S(2)}) collective-permute-start(bf16[1024,2048]{1,0:T(8,128)(2,1)} %wu_own.1), channel_id=1, source_target_pairs={{0,1},{1,0},{2,3},{3,2},{4,5},{5,4},{6,7},{7,6},{8,9},{9,8},{10,11... | collective-permute-start | bytes 12582920 | tf_op jit(solution)/shard_map/ppermute | solution.py:435
  16.2 58.2 %collective-permute-start.4 = (bf16[2048,1024]{1,0:T(8,128)(2,1)}, bf16[2048,1024]{1,0:T(8,128)(2,1)}, u32[]{:S(2)}, u32[]{:S(2)}) collective-permute-start(bf16[2048,1024]{1,0:T(8,128)(2,1)} %wd_own.1), channel_id=1, source_target_pairs={{0,1},{1,0},{2,3},{3,2},{4,5},{5,4},{6,7},{7,6},{8,9},{9,8},{10,11... | collective-permute-start | bytes 12582920 | tf_op jit(solution)/shard_map/ppermute | solution.py:435
  16.7 57.7 %collective-permute-start.1 = (bf16[3,1024,512]{2,1,0:T(8,128)(2,1)S(1)}, bf16[3,1024,512]{2,1,0:T(8,128)(2,1)}, u32[]{:S(2)}, u32[]{:S(2)}) collective-permute-start(bf16[3,1024,512]{2,1,0:T(8,128)(2,1)S(1)} %bitcast.17), channel_id=1, source_target_pairs={{0,1},{1,0},{2,3},{3,2},{4,5},{5,4},{6,7},{7,6},{8,9},{9,8},{10,11... | collective-permute-start | bytes 9437192 | tf_op jit(solution)/shard_map/ppermute | solution.py:435
  16.8 57.6 %collective-permute-start.2 = (bf16[512,1024]{1,0:T(8,128)(2,1)}, bf16[512,1024]{1,0:T(8,128)(2,1)}, u32[]{:S(2)}, u32[]{:S(2)}) collective-permute-start(bf16[512,1024]{1,0:T(8,128)(2,1)} %wo_own.1), channel_id=1, source_target_pairs={{0,1},{1,0},{2,3},{3,2},{4,5},{5,4},{6,7},{7,6},{8,9},{9,8},{10,11... | collective-permute-start | bytes 3145736 | tf_op jit(solution)/shard_map/ppermute | solution.py:435
  74.1 2.9 %collective-permute-start = (bf16[14,256,128]{2,1,0:T(8,128)(2,1)}, bf16[14,256,128]{2,1,0:T(8,128)(2,1)S(1)}, u32[]{:S(2)}, u32[]{:S(2)}) collective-permute-start(bf16[14,256,128]{2,1,0:T(8,128)(2,1)} %get-tuple-element.13), channel_id=1, source_target_pairs={{0,1},{1,0},{2,3},{3,2},{4,5},{5,4},{6,7},{7,6},{8,9},{9,8},{10,11... | collective-permute-start | bytes 2752520 | tf_op jit(solution)/shard_map/ppermute | solution.py:442
  77.1 0.9 copy-start.3
  78.0 38.7 %copy-start.1 = (s32[28,4]{0,1:T(4,128)S(1)}, s32[28,4]{0,1:T(4,128)}, u32[]{:S(2)}) copy-start(s32[28,4]{0,1:T(4,128)} %param.13) | copy-start | bytes 1348
  116.4 16.4 %copy-start = (bf16[896,512]{1,0:T(8,128)(2,1)S(1)}, bf16[896,512]{1,0:T(8,128)(2,1)}, u32[]{:S(2)}) copy-start(bf16[896,512]{1,0:T(8,128)(2,1)} %get-tuple-element.18) | copy-start | bytes 2752516
  116.4 1.6 %collective-permute-start.5 = (bf16[112,512]{1,0:T(8,128)(2,1)}, bf16[112,512]{1,0:T(8,128)(2,1)S(1)}, u32[]{:S(2)}, u32[]{:S(2)}) collective-permute-start(bf16[112,512]{1,0:T(8,128)(2,1)} %get-tuple-element.16), channel_id=1, source_target_pairs={{0,1},{1,0},{2,3},{3,2},{4,5},{5,4},{6,7},{7,6},{8,9},{9,8},{10,11... | collective-permute-start | bytes 344072 | tf_op jit(solution)/shard_map/ppermute | solution.py:446
  118.0 14.8 %collective-permute-start.6 = (bf16[896,512]{1,0:T(8,128)(2,1)}, bf16[896,512]{1,0:T(8,128)(2,1)S(1)}, u32[]{:S(2)}, u32[]{:S(2)}) collective-permute-start(bf16[896,512]{1,0:T(8,128)(2,1)} %get-tuple-element.19), channel_id=1, source_target_pairs={{0,1},{1,0},{2,3},{3,2},{4,5},{5,4},{6,7},{7,6},{8,9},{9,8},{10,11... | collective-permute-start | bytes 2752520 | tf_op jit(solution)/shard_map/ppermute | solution.py:448
  121.0 22.9 %all-to-all-start.1 = ((bf16[64,4,512]{2,1,0:T(4,128)(2,1)}), bf16[64,4,512]{2,1,0:T(4,128)(2,1)S(1)}, u32[]{:S(2)}, u32[]{:S(2)}) async-start(bf16[64,4,512]{2,1,0:T(4,128)(2,1)} %reshape.31), calls=%async_computation.1 | async-start | bytes 524288 | tf_op jit(solution)/shard_map/all_to_all | solution.py:465

commit v8 on v7

--- a/solution.py
+++ b/solution.py
@@ -437,16 +437,6 @@
     received = lax.all_to_all(
         pack(dest, doc_ids, tokens, devices), "dp", split_axis=0, concat_axis=0, tiled=True
     )
-    core = me.astype(jnp.int32)[None]
-    x_send, info = unpack(core, received, mine)
-    x_other = lax.ppermute(x_send, "mp", SWAP)
-    enc_own, enc_oth, emb_own, emb_oth = layer(
-        core, info, received, x_other, weights, gain_attn[None], gain_ffn[None]
-    )
-    emb_recv = lax.ppermute(emb_oth, "mp", SWAP)
-    enc_oth, emb_recv = lax.optimization_barrier((enc_oth, emb_recv))
-    enc_recv = lax.ppermute(enc_oth, "mp", SWAP)
-
     owners = owner.reshape(-1)
     position = jnp.arange(row_count * docs, dtype=jnp.int32)
     earlier = (owners[:, None] == owners[None, :]) & (position[None, :] < position[:, None])
@@ -458,10 +448,21 @@
     out_slot = jnp.arange(devices * SLOTS, dtype=jnp.int32)[:, None]
     place_own = (lax.dynamic_index_in_dim(target, me, 0) == out_slot).astype(jnp.bfloat16)
     place_oth = (lax.dynamic_index_in_dim(target, 1 - me, 0) == out_slot).astype(jnp.bfloat16)
-    sending = (
-        jnp.dot(place_own, emb_own, preferred_element_type=jnp.float32)
-        + jnp.dot(place_oth, emb_recv, preferred_element_type=jnp.float32)
-    ).astype(jnp.bfloat16)
+    core = me.astype(jnp.int32)[None]
+    core, place_own, place_oth = lax.optimization_barrier((core, place_own, place_oth))
+    x_send, info = unpack(core, received, mine)
+    x_other = lax.ppermute(x_send, "mp", SWAP)
+    enc_own, enc_oth, emb_own, emb_oth = layer(
+        core, info, received, x_other, weights, gain_attn[None], gain_ffn[None]
+    )
+    emb_recv = lax.ppermute(emb_oth, "mp", SWAP)
+    own_part = jnp.dot(place_own, emb_own, preferred_element_type=jnp.float32)
+    own_part, emb_recv = lax.optimization_barrier((own_part, emb_recv))
+    enc_oth, emb_recv = lax.optimization_barrier((enc_oth, emb_recv))
+    enc_recv = lax.ppermute(enc_oth, "mp", SWAP)
+
+    sending = jnp.dot(place_oth, emb_recv, preferred_element_type=jnp.float32)
+    sending = (sending + own_part).astype(jnp.bfloat16)
     got = lax.all_to_all(
         sending.reshape(devices, SLOTS, half), "dp", split_axis=0, concat_axis=0, tiled=True
     )

time: 145 us -> 143 us (0.986)
  waiting for transfers between devices: 66.3 us -> 64.5 us
where the time goes in v8:
time: 143 us; the launch traced here: 142 us
  waiting for transfers between devices  64.5 us (45%)
  Pallas kernels  45.9 us (32%)
  starting transfers between devices  25.6 us (18%)
  local copies, waits for them, and re-layouts  2.43 us (2%)
  other arithmetic  1.87 us (1%)
    all_to_all x1, waiting for transfers between devices, shards(): lax.all_to_all(pack(dest, doc_ids, tokens, devices), 'dp', split_axis=0,...  52 us
    pallas_call x1, Pallas kernels, layer(): pl.pallas_call(layer_kernel, out_shape=(jax.ShapeDtypeStruct((tokens, hal...  38.4 us
    all_to_all x1, starting transfers between devices, shards(): lax.all_to_all(pack(dest, doc_ids, tokens, devices), 'dp', split_axis=0,...  12 us
    all_to_all x1, starting transfers between devices, shards(): lax.all_to_all(sending.reshape(devices, SLOTS, half), 'dp', split_axis=0,...  11.8 us
    all_to_all x1, waiting for transfers between devices, shards(): lax.all_to_all(sending.reshape(devices, SLOTS, half), 'dp', split_axis=0,...  9.51 us
    pallas_call x1, Pallas kernels, unpack(): pl.pallas_call(unpack_kernel, out_shape=(jax.ShapeDtypeStruct((rows, body...  3.93 us
    pallas_call x1, Pallas kernels, pack(): pl.pallas_call(pack_kernel, out_shape=jax.ShapeDtypeStruct((slots, body +...  3.54 us
  transfers between devices with their start and end apart: 9, of which 4 were waited for; matrix products, arithmetic and copies ran while one was open for 3% of the time, Pallas kernels for 3%

profile of v8, /device:TPU:0, one launch (start us, length us, event | category | flops | bytes accessed | tf_op | source)
XLA Modules:
  0.0 142.4 jit_solution(11877659388206957729)
XLA Ops:
  0.6 3.5 %pack_rows.1 = bf16[64,264,128]{2,1,0:T(8,128)(2,1)} custom-call(s32[28]{0:T(128)} %dest.1, s32[28,64]{1,0:T(8,128)} %doc_ids.1, bf16[28,64,512]{2,1,0:T(8,128)(2,1)} %tokens.1), custom_call_target="tpu_custom_call" | custom-call | tf_op jit(solution)/shard_map/pack_rows/pallas_call | solution.py:70
  4.2 0.0 copy-start.2
  4.2 0.0 copy-start.1
  4.2 12.0 %all-to-all-start = ((bf16[64,264,128]{2,1,0:T(8,128)(2,1)}), bf16[64,264,128]{2,1,0:T(8,128)(2,1)}, u32[]{:S(2)}, u32[]{:S(2)}) async-start(bf16[64,264,128]{2,1,0:T(8,128)(2,1)} %pack_rows.1), calls=%async_computation | async-start | bytes 8650752 | tf_op jit(solution)/shard_map/all_to_all | solution.py:437
  16.2 0.1 collective-permute-start.3
  16.3 0.5 collective-permute-start.4
  16.8 0.0 copy-done.2
  16.8 0.1 collective-permute-start.1
  16.9 0.4 collective-permute-start.2
  17.3 0.0 copy-done.1
  17.3 0.1 copy.17
  17.4 0.1 eq.48
  17.5 0.2 convert_reduce_fusion
  17.7 0.1 reduce_sum.12
  17.8 0.1 copy.18
  17.9 0.1 mul.12
  18.0 0.1 copy.20
  18.1 0.1 reshape.30
  18.3 52.0 %all-to-all-done.received = bf16[64,264,128]{2,1,0:T(8,128)(2,1)} async-done(((bf16[64,264,128]{2,1,0:T(8,128)(2,1)}), bf16[64,264,128]{2,1,0:T(8,128)(2,1)}, u32[]{:S(2)}, u32[]{:S(2)}) %all-to-all-start) | async-done | bytes 4325408 | tf_op jit(solution)/shard_map/all_to_all | solution.py:437
  70.3 3.9 %unpack_rows.1 = (bf16[14,256,128]{2,1,0:T(8,128)(2,1)}, s32[8,128]{1,0:T(8,128)}) custom-call(s32[1]{0:T(128)} %bitcast.core, bf16[64,264,128]{2,1,0:T(8,128)(2,1)} %all-to-all-done.received), custom_call_target="tpu_custom_call" | custom-call | tf_op jit(solution)/shard_map/unpack_rows/pallas_call | solution.py:137
  74.2 0.3 collective-permute-start
  74.5 0.0 collective-permute-done.2.wo_oth
  74.5 0.0 collective-permute-done.1.wq_oth
  74.5 0.0 collective-permute-done.3.wu_oth
  74.5 0.0 collective-permute-done.4.wd_oth
  74.5 2.8 %collective-permute-done.x_other = bf16[14,256,128]{2,1,0:T(8,128)(2,1)} collective-permute-done((bf16[14,256,128]{2,1,0:T(8,128)(2,1)}, bf16[14,256,128]{2,1,0:T(8,128)(2,1)}, u32[]{:S(2)}, u32[]{:S(2)}) %collective-permute-start) | collective-permute-done | bytes 917536 | tf_op jit(solution)/shard_map/ppermute | solution.py:454
  77.3 38.4 %layer.1 = (bf16[896,512]{1,0:T(8,128)(2,1)}, bf16[896,512]{1,0:T(8,128)(2,1)}, bf16[112,512]{1,0:T(8,128)(2,1)}, bf16[112,512]{1,0:T(8,128)(2,1)}) custom-call(s32[1]{0:T(128)} %bitcast.core, s32[8,128]{1,0:T(8,128)} %get-tuple-element.19.table, bf16[64,264,128]{2,1,0:T(8,128)(2,1)} %all-to-all-done.received, ...), custom_call_target="tpu_custom_call" | custom-call | flops 22548578304 | bytes 29360128 | tf_op jit(solution)/shard_map/layer/pallas_call | solution.py:388
  115.7 0.0 copy-start
  115.7 0.2 collective-permute-start.5
  115.9 1.2 fusion.3
  117.1 0.2 collective-permute-done.5
  117.3 0.2 collective-permute-start.6
  117.5 0.2 fusion.4
  117.7 0.1 add_convert_fusion
  117.8 0.8 reshape.31
  118.6 11.8 %all-to-all-start.1 = ((bf16[64,4,512]{2,1,0:T(4,128)(2,1)}), bf16[64,4,512]{2,1,0:T(4,128)(2,1)S(1)}, u32[]{:S(2)}, u32[]{:S(2)}) async-start(bf16[64,4,512]{2,1,0:T(4,128)(2,1)} %reshape.31), calls=%async_computation.1 | async-start | bytes 524288 | tf_op jit(solution)/shard_map/all_to_all | solution.py:466
  130.4 0.0 collective-permute-done.6
  130.4 0.0 copy-done
  130.4 0.1 broadcast_select_fusion.1
  130.5 1.4 pad_maximum_fusion
  131.9 9.5 %all-to-all-done.1 = bf16[64,4,512]{2,1,0:T(4,128)(2,1)S(1)} async-done(((bf16[64,4,512]{2,1,0:T(4,128)(2,1)}), bf16[64,4,512]{2,1,0:T(4,128)(2,1)S(1)}, u32[]{:S(2)}, u32[]{:S(2)}) %all-to-all-start.1) | async-done | bytes 262176 | tf_op jit(solution)/shard_map/all_to_all | solution.py:466
  141.5 0.9 reshape.35
  (6 shorter events, 0.1 us)
Async XLA Ops:
  4.2 12.6 %copy-start.2 = (bf16[1024,3,512]{2,0,1:T(8,128)(2,1)S(1)}, bf16[1024,3,512]{2,0,1:T(8,128)(2,1)}, u32[]{:S(2)}) copy-start(bf16[1024,3,512]{2,0,1:T(8,128)(2,1)} %param.14) | copy-start | bytes 9437188
  4.2 13.1 %copy-start.1 = (s32[28,4]{0,1:T(4,128)S(1)}, s32[28,4]{0,1:T(4,128)}, u32[]{:S(2)}) copy-start(s32[28,4]{0,1:T(4,128)} %param.13) | copy-start | bytes 1348
  4.2 66.1 %all-to-all-start = ((bf16[64,264,128]{2,1,0:T(8,128)(2,1)}), bf16[64,264,128]{2,1,0:T(8,128)(2,1)}, u32[]{:S(2)}, u32[]{:S(2)}) async-start(bf16[64,264,128]{2,1,0:T(8,128)(2,1)} %pack_rows.1), calls=%async_computation | async-start | bytes 8650752 | tf_op jit(solution)/shard_map/all_to_all | solution.py:437
  16.2 58.3 %collective-permute-start.3 = (bf16[1024,2048]{1,0:T(8,128)(2,1)}, bf16[1024,2048]{1,0:T(8,128)(2,1)}, u32[]{:S(2)}, u32[]{:S(2)}) collective-permute-start(bf16[1024,2048]{1,0:T(8,128)(2,1)} %wu_own.1), channel_id=1, source_target_pairs={{0,1},{1,0},{2,3},{3,2},{4,5},{5,4},{6,7},{7,6},{8,9},{9,8},{10,11... | collective-permute-start | bytes 12582920 | tf_op jit(solution)/shard_map/ppermute | solution.py:435
  16.3 58.2 %collective-permute-start.4 = (bf16[2048,1024]{1,0:T(8,128)(2,1)}, bf16[2048,1024]{1,0:T(8,128)(2,1)}, u32[]{:S(2)}, u32[]{:S(2)}) collective-permute-start(bf16[2048,1024]{1,0:T(8,128)(2,1)} %wd_own.1), channel_id=1, source_target_pairs={{0,1},{1,0},{2,3},{3,2},{4,5},{5,4},{6,7},{7,6},{8,9},{9,8},{10,11... | collective-permute-start | bytes 12582920 | tf_op jit(solution)/shard_map/ppermute | solution.py:435
  16.8 57.7 %collective-permute-start.1 = (bf16[3,1024,512]{2,1,0:T(8,128)(2,1)S(1)}, bf16[3,1024,512]{2,1,0:T(8,128)(2,1)}, u32[]{:S(2)}, u32[]{:S(2)}) collective-permute-start(bf16[3,1024,512]{2,1,0:T(8,128)(2,1)S(1)} %bitcast.19), channel_id=1, source_target_pairs={{0,1},{1,0},{2,3},{3,2},{4,5},{5,4},{6,7},{7,6},{8,9},{9,8},{10,11... | collective-permute-start | bytes 9437192 | tf_op jit(solution)/shard_map/ppermute | solution.py:435
  16.9 57.6 %collective-permute-start.2 = (bf16[512,1024]{1,0:T(8,128)(2,1)}, bf16[512,1024]{1,0:T(8,128)(2,1)}, u32[]{:S(2)}, u32[]{:S(2)}) collective-permute-start(bf16[512,1024]{1,0:T(8,128)(2,1)} %wo_own.1), channel_id=1, source_target_pairs={{0,1},{1,0},{2,3},{3,2},{4,5},{5,4},{6,7},{7,6},{8,9},{9,8},{10,11... | collective-permute-start | bytes 3145736 | tf_op jit(solution)/shard_map/ppermute | solution.py:435
  74.2 3.1 %collective-permute-start = (bf16[14,256,128]{2,1,0:T(8,128)(2,1)}, bf16[14,256,128]{2,1,0:T(8,128)(2,1)}, u32[]{:S(2)}, u32[]{:S(2)}) collective-permute-start(bf16[14,256,128]{2,1,0:T(8,128)(2,1)} %get-tuple-element.20), channel_id=1, source_target_pairs={{0,1},{1,0},{2,3},{3,2},{4,5},{5,4},{6,7},{7,6},{8,9},{9,8},{10,11... | collective-permute-start | bytes 2752520 | tf_op jit(solution)/shard_map/ppermute | solution.py:454
  115.7 14.7 %copy-start = (bf16[896,512]{1,0:T(8,128)(2,1)S(1)}, bf16[896,512]{1,0:T(8,128)(2,1)}, u32[]{:S(2)}) copy-start(bf16[896,512]{1,0:T(8,128)(2,1)} %get-tuple-element.28) | copy-start | bytes 2752516
  115.7 1.6 %collective-permute-start.5 = (bf16[112,512]{1,0:T(8,128)(2,1)}, bf16[112,512]{1,0:T(8,128)(2,1)S(1)}, u32[]{:S(2)}, u32[]{:S(2)}) collective-permute-start(bf16[112,512]{1,0:T(8,128)(2,1)} %get-tuple-element.24), channel_id=1, source_target_pairs={{0,1},{1,0},{2,3},{3,2},{4,5},{5,4},{6,7},{7,6},{8,9},{9,8},{10,11... | collective-permute-start | bytes 344072 | tf_op jit(solution)/shard_map/ppermute | solution.py:458
  117.3 13.1 %collective-permute-start.6 = (bf16[896,512]{1,0:T(8,128)(2,1)}, bf16[896,512]{1,0:T(8,128)(2,1)S(1)}, u32[]{:S(2)}, u32[]{:S(2)}) collective-permute-start(bf16[896,512]{1,0:T(8,128)(2,1)} %get-tuple-element.29), channel_id=1, source_target_pairs={{0,1},{1,0},{2,3},{3,2},{4,5},{5,4},{6,7},{7,6},{8,9},{9,8},{10,11... | collective-permute-start | bytes 2752520 | tf_op jit(solution)/shard_map/ppermute | solution.py:462
  118.6 22.9 %all-to-all-start.1 = ((bf16[64,4,512]{2,1,0:T(4,128)(2,1)}), bf16[64,4,512]{2,1,0:T(4,128)(2,1)S(1)}, u32[]{:S(2)}, u32[]{:S(2)}) async-start(bf16[64,4,512]{2,1,0:T(4,128)(2,1)} %reshape.31), calls=%async_computation.1 | async-start | bytes 524288 | tf_op jit(solution)/shard_map/all_to_all | solution.py:466

commit v9 on v8

--- a/solution.py
+++ b/solution.py
@@ -84,13 +84,13 @@
             pltpu.SemaphoreType.DMA((rows,)),
             pltpu.SemaphoreType.DMA,
         ],
-        compiler_params=pltpu.CompilerParams(vmem_limit_bytes=60 * 1024 * 1024),
+        compiler_params=pltpu.CompilerParams(vmem_limit_bytes=62 * 1024 * 1024),
         name="pack_rows",
     )(dest, doc_ids, tokens)
 
 
 def unpack_kernel(
-    core, received, out, info, facts, table, scalars, staged, fact_sem, info_sem, sems, out_sem
+    core, received, out, info, facts, table, scalars, staged, fact_sem, info_sem, sems, out_sems
 ):
     rows, body, _ = out.shape
     slots = received.shape[0]
@@ -122,11 +122,13 @@
     table[1] = result.astype(jnp.int32)
     keep = pltpu.make_async_copy(table.at[1], info, info_sem.at[1])
     keep.start()
-    for copy in copies:
+    stores = []
+    for r in range(rows):
+        copies[r].wait()
+        stores.append(pltpu.make_async_copy(staged.at[r], out.at[r], out_sems.at[r]))
+        stores[-1].start()
+    for copy in stores:
         copy.wait()
-    store = pltpu.make_async_copy(staged, out, out_sem)
-    store.start()
-    store.wait()
     keep.wait()
 
 
@@ -150,9 +152,9 @@
             pltpu.SemaphoreType.DMA,
             pltpu.SemaphoreType.DMA((2,)),
             pltpu.SemaphoreType.DMA((rows,)),
-            pltpu.SemaphoreType.DMA,
+            pltpu.SemaphoreType.DMA((rows,)),
         ],
-        compiler_params=pltpu.CompilerParams(vmem_limit_bytes=60 * 1024 * 1024),
+        compiler_params=pltpu.CompilerParams(vmem_limit_bytes=62 * 1024 * 1024),
         name="unpack_rows",
     )(core, received)
 
@@ -336,6 +338,7 @@
     position = lax.broadcasted_iota(jnp.int32, (16, two), 1)
     same_row = (doc < 8) == (position < seq)
     doc = doc % 8
+    quarter = half // 2
     own_col = pl.ds(pl.multiple_of(me * half, half), half)
     oth_col = pl.ds(pl.multiple_of((1 - me) * half, half), half)
     outs = []
@@ -366,8 +369,9 @@
         pooled = pooled * (1.0 / jnp.maximum(total, 1.0))
         square = jnp.mean(pooled * pooled, -1, keepdims=True)
         embedded = (pooled * lax.rsqrt(square + 1e-06)).astype(jnp.bfloat16)
-        emb_scr[0, m * 16 : (m + 1) * 16, :] = embedded[:, :half]
-        emb_scr[1, m * 16 : (m + 1) * 16, :] = embedded[:, half:]
+        for i in range(2 * model // half):
+            at = slice((i % 2 * rows + 2 * m) * 8, (i % 2 * rows + 2 * m + 2) * 8)
+            emb_scr[i // 2, at, :] = embedded[:, i * quarter : (i + 1) * quarter]
     for i, out in enumerate((emb_own, emb_oth)):
         which = me if i == 0 else 1 - me
         outs.append(pltpu.make_async_copy(emb_scr.at[which], out, out_sems.at[rows // 2, i]))
@@ -390,8 +394,8 @@
         out_shape=(
             jax.ShapeDtypeStruct((tokens, half), jnp.bfloat16),
             jax.ShapeDtypeStruct((tokens, half), jnp.bfloat16),
-            jax.ShapeDtypeStruct((rows * 8, half), jnp.bfloat16),
-            jax.ShapeDtypeStruct((rows * 8, half), jnp.bfloat16),
+            jax.ShapeDtypeStruct((2 * rows * 8, half // 2), jnp.bfloat16),
+            jax.ShapeDtypeStruct((2 * rows * 8, half // 2), jnp.bfloat16),
         ),
         in_specs=[pl.BlockSpec(memory_space=pltpu.SMEM)]
         + [any_spec] * 11
@@ -401,7 +405,7 @@
             pltpu.SMEM(table.shape, jnp.int32),
             pltpu.VMEM((rows, 2 * body, LANES), jnp.bfloat16),
             pltpu.VMEM((tokens, 3 * model), jnp.bfloat16),
-            pltpu.VMEM((2, rows * 8, half), jnp.bfloat16),
+            pltpu.VMEM((2, 2 * rows * 8, half // 2), jnp.bfloat16),
             pltpu.VMEM((tokens, model), jnp.float32),
             pltpu.VMEM((6, model, half), jnp.bfloat16),
             pltpu.VMEM((2, half, model), jnp.bfloat16),
@@ -414,7 +418,7 @@
             pltpu.SemaphoreType.DMA,
             pltpu.SemaphoreType.DMA((rows // 2 + 1, 2)),
         ],
-        compiler_params=pltpu.CompilerParams(vmem_limit_bytes=60 * 1024 * 1024),
+        compiler_params=pltpu.CompilerParams(vmem_limit_bytes=62 * 1024 * 1024),
         cost_estimate=pl.CostEstimate(
             flops=flops, bytes_accessed=28 * 1024 * 1024, transcendentals=0
         ),
@@ -441,11 +445,12 @@
     position = jnp.arange(row_count * docs, dtype=jnp.int32)
     earlier = (owners[:, None] == owners[None, :]) & (position[None, :] < position[:, None])
     rank = jnp.sum(earlier.astype(jnp.int32), -1)
+    target = (owners * 2 * SLOTS + rank).reshape(2, 1, mine, docs)
+    target = target + jnp.array([0, SLOTS], jnp.int32).reshape(1, 2, 1, 1)
     target = jnp.pad(
-        (owners * SLOTS + rank).reshape(2, mine, docs), ((0, 0), (0, 0), (0, 8 - docs)),
-        constant_values=-1,
-    ).reshape(2, mine * 8)
-    out_slot = jnp.arange(devices * SLOTS, dtype=jnp.int32)[:, None]
+        target, ((0, 0), (0, 0), (0, 0), (0, 8 - docs)), constant_values=-1
+    ).reshape(2, 2 * mine * 8)
+    out_slot = jnp.arange(devices * 2 * SLOTS, dtype=jnp.int32)[:, None]
     place_own = (lax.dynamic_index_in_dim(target, me, 0) == out_slot).astype(jnp.bfloat16)
     place_oth = (lax.dynamic_index_in_dim(target, 1 - me, 0) == out_slot).astype(jnp.bfloat16)
     core = me.astype(jnp.int32)[None]
@@ -464,7 +469,7 @@
     sending = jnp.dot(place_oth, emb_recv, preferred_element_type=jnp.float32)
     sending = (sending + own_part).astype(jnp.bfloat16)
     got = lax.all_to_all(
-        sending.reshape(devices, SLOTS, half), "dp", split_axis=0, concat_axis=0, tiled=True
+        sending.reshape(devices, 2 * SLOTS, half // 2), "dp", split_axis=0, concat_axis=0, tiled=True
     )
     enc_own = enc_own.reshape(mine, seq, half)
     enc_recv = enc_recv.reshape(mine, seq, half)
@@ -473,7 +478,8 @@
         [jnp.where(first, enc_own, enc_recv), jnp.where(first, enc_recv, enc_own)], 0
     )
     got, encoded = lax.optimization_barrier((got, encoded))
-    index_part = got[:, : SLOTS - 1].astype(jnp.float32).reshape(1, devices * (SLOTS - 1), half)
+    got = jnp.concatenate([got[:, : SLOTS - 1], got[:, SLOTS:-1]], -1)
+    index_part = got.astype(jnp.float32).reshape(1, devices * (SLOTS - 1), half)
     return (encoded, index_part)
 
 

time: 143 us -> 143 us (level)
  other arithmetic: 1.87 us -> 3.49 us
  local copies, waits for them, and re-layouts: 2.43 us -> 0.97 us
    reshape x3 -> x1, local copies, waits for them, and re-layouts: 1.8 us -> 0.09 us  [shards(): target = jnp.pad(target, ((0, 0), (0, 0), (0, 0), (0, 8 - docs)), constan...]
where the time goes in v9:
time: 143 us; the launch traced here: 142 us
  waiting for transfers between devices  64.3 us (45%)
  Pallas kernels  45.7 us (32%)
  starting transfers between devices  25.4 us (18%)
  other arithmetic  3.49 us (2%)
    all_to_all x1, waiting for transfers between devices, shards(): lax.all_to_all(pack(dest, doc_ids, tokens, devices), 'dp', split_axis=0,...  51.8 us
    pallas_call x1, Pallas kernels, layer(): pl.pallas_call(layer_kernel, out_shape=(jax.ShapeDtypeStruct((tokens, hal...  38.4 us
    all_to_all x1, starting transfers between devices, shards(): lax.all_to_all(pack(dest, doc_ids, tokens, devices), 'dp', split_axis=0,...  11.8 us
    all_to_all x1, starting transfers between devices, shards(): lax.all_to_all(sending.reshape(devices, 2 * SLOTS, half // 2), 'dp', spli...  11.8 us
    all_to_all x1, waiting for transfers between devices, shards(): lax.all_to_all(sending.reshape(devices, 2 * SLOTS, half // 2), 'dp', spli...  9.51 us
    pallas_call x1, Pallas kernels, unpack(): pl.pallas_call(unpack_kernel, out_shape=(jax.ShapeDtypeStruct((rows, body...  3.75 us
    pallas_call x1, Pallas kernels, pack(): pl.pallas_call(pack_kernel, out_shape=jax.ShapeDtypeStruct((slots, body +...  3.5 us
  transfers between devices with their start and end apart: 9, of which 4 were waited for; matrix products, arithmetic and copies ran while one was open for 3% of the time, Pallas kernels for 3%

profile of v9, /device:TPU:0, one launch (start us, length us, event | category | flops | bytes accessed | tf_op | source)
XLA Modules:
  0.0 142.0 jit_solution(12294389422311284428)
XLA Ops:
  0.6 3.5 %pack_rows.1 = bf16[64,264,128]{2,1,0:T(8,128)(2,1)} custom-call(s32[28]{0:T(128)} %dest.1, s32[28,64]{1,0:T(8,128)} %doc_ids.1, bf16[28,64,512]{2,1,0:T(8,128)(2,1)} %tokens.1), custom_call_target="tpu_custom_call" | custom-call | tf_op jit(solution)/shard_map/pack_rows/pallas_call | solution.py:70
  4.1 0.0 copy-start.2
  4.1 0.0 copy-start.1
  4.2 11.8 %all-to-all-start = ((bf16[64,264,128]{2,1,0:T(8,128)(2,1)}), bf16[64,264,128]{2,1,0:T(8,128)(2,1)}, u32[]{:S(2)}, u32[]{:S(2)}) async-start(bf16[64,264,128]{2,1,0:T(8,128)(2,1)} %pack_rows.1), calls=%async_computation | async-start | bytes 8650752 | tf_op jit(solution)/shard_map/all_to_all | solution.py:441
  16.0 0.1 collective-permute-start.3
  16.1 0.5 collective-permute-start.4
  16.6 0.1 collective-permute-start.1
  16.7 0.0 copy-done.2
  16.7 0.4 collective-permute-start.2
  17.1 0.0 copy-done.1
  17.1 0.1 copy.22
  17.2 0.1 eq.48
  17.3 0.2 convert_reduce_fusion
  17.5 0.1 reduce_sum.12
  17.6 0.1 copy.24
  17.7 0.1 mul.17
  17.8 0.1 copy.25
  17.9 0.1 broadcast_add_fusion
  18.0 0.1 reshape.64
  18.1 0.2 fusion
  18.3 51.8 %all-to-all-done.received = bf16[64,264,128]{2,1,0:T(8,128)(2,1)} async-done(((bf16[64,264,128]{2,1,0:T(8,128)(2,1)}), bf16[64,264,128]{2,1,0:T(8,128)(2,1)}, u32[]{:S(2)}, u32[]{:S(2)}) %all-to-all-start) | async-done | bytes 4325408 | tf_op jit(solution)/shard_map/all_to_all | solution.py:441
  70.1 3.8 %unpack_rows.1 = (bf16[14,256,128]{2,1,0:T(8,128)(2,1)}, s32[8,128]{1,0:T(8,128)}) custom-call(s32[1]{0:T(128)} %bitcast.core, bf16[64,264,128]{2,1,0:T(8,128)(2,1)} %all-to-all-done.received), custom_call_target="tpu_custom_call" | custom-call | tf_op jit(solution)/shard_map/unpack_rows/pallas_call | solution.py:139
  73.8 0.3 collective-permute-start
  74.1 0.0 collective-permute-done.2.wo_oth
  74.1 0.0 collective-permute-done.1.wq_oth
  74.1 0.0 collective-permute-done.3.wu_oth
  74.1 0.0 collective-permute-done.4.wd_oth
  74.1 2.8 %collective-permute-done.x_other = bf16[14,256,128]{2,1,0:T(8,128)(2,1)} collective-permute-done((bf16[14,256,128]{2,1,0:T(8,128)(2,1)}, bf16[14,256,128]{2,1,0:T(8,128)(2,1)}, u32[]{:S(2)}, u32[]{:S(2)}) %collective-permute-start) | collective-permute-done | bytes 917536 | tf_op jit(solution)/shard_map/ppermute | solution.py:459
  76.9 38.4 %layer.1 = (bf16[896,512]{1,0:T(8,128)(2,1)}, bf16[896,512]{1,0:T(8,128)(2,1)}, bf16[224,256]{1,0:T(8,128)(2,1)}, bf16[224,256]{1,0:T(8,128)(2,1)}) custom-call(s32[1]{0:T(128)} %bitcast.core, s32[8,128]{1,0:T(8,128)} %get-tuple-element.19.table, bf16[64,264,128]{2,1,0:T(8,128)(2,1)} %all-to-all-done.received, ...), custom_call_target="tpu_custom_call" | custom-call | flops 22548578304 | bytes 29360128 | tf_op jit(solution)/shard_map/layer/pallas_call | solution.py:392
  115.3 0.0 copy-start
  115.3 0.2 collective-permute-start.5
  115.5 1.2 fusion.5
  116.7 0.2 collective-permute-done.5
  116.9 0.2 collective-permute-start.6
  117.1 0.2 fusion.6
  117.4 0.8 fusion.2
  118.1 11.8 %all-to-all-start.1 = ((bf16[64,8,256]{2,1,0:T(8,128)(2,1)}), bf16[64,8,256]{2,1,0:T(8,128)(2,1)S(1)}, u32[]{:S(2)}, u32[]{:S(2)}) async-start(bf16[64,8,256]{2,1,0:T(8,128)(2,1)} %fusion.2), calls=%async_computation.1 | async-start | bytes 524288 | tf_op jit(solution)/shard_map/all_to_all | solution.py:471
  129.9 0.0 collective-permute-done.6
  129.9 0.0 copy-done
  130.0 0.1 broadcast_select_fusion.1
  130.1 1.4 pad_maximum_fusion
  131.5 9.5 %all-to-all-done.1 = bf16[64,8,256]{2,1,0:T(8,128)(2,1)S(1)} async-done(((bf16[64,8,256]{2,1,0:T(8,128)(2,1)}), bf16[64,8,256]{2,1,0:T(8,128)(2,1)S(1)}, u32[]{:S(2)}, u32[]{:S(2)}) %all-to-all-start.1) | async-done | bytes 262176 | tf_op jit(solution)/shard_map/all_to_all | solution.py:471
  141.0 0.1 fusion.4
  141.1 0.1 concatenate.18
  141.2 0.1 concatenate.19
  141.3 0.8 maximum_convert_fusion
  (5 shorter events, 0.0 us)
Async XLA Ops:
  4.1 12.6 %copy-start.2 = (bf16[512,1024]{1,0:T(8,128)(2,1)S(1)}, bf16[512,1024]{1,0:T(8,128)(2,1)}, u32[]{:S(2)}) copy-start(bf16[512,1024]{1,0:T(8,128)(2,1)} %wo_own.1) | copy-start | bytes 3145732
  4.1 13.0 %copy-start.1 = (s32[28,4]{0,1:T(4,128)S(1)}, s32[28,4]{0,1:T(4,128)}, u32[]{:S(2)}) copy-start(s32[28,4]{0,1:T(4,128)} %param.14) | copy-start | bytes 1348
  4.2 65.9 %all-to-all-start = ((bf16[64,264,128]{2,1,0:T(8,128)(2,1)}), bf16[64,264,128]{2,1,0:T(8,128)(2,1)}, u32[]{:S(2)}, u32[]{:S(2)}) async-start(bf16[64,264,128]{2,1,0:T(8,128)(2,1)} %pack_rows.1), calls=%async_computation | async-start | bytes 8650752 | tf_op jit(solution)/shard_map/all_to_all | solution.py:441
  16.0 58.1 %collective-permute-start.3 = (bf16[1024,2048]{1,0:T(8,128)(2,1)}, bf16[1024,2048]{1,0:T(8,128)(2,1)}, u32[]{:S(2)}, u32[]{:S(2)}) collective-permute-start(bf16[1024,2048]{1,0:T(8,128)(2,1)} %wu_own.1), channel_id=1, source_target_pairs={{0,1},{1,0},{2,3},{3,2},{4,5},{5,4},{6,7},{7,6},{8,9},{9,8},{10,11... | collective-permute-start | bytes 12582920 | tf_op jit(solution)/shard_map/ppermute | solution.py:439
  16.1 58.0 %collective-permute-start.4 = (bf16[2048,1024]{1,0:T(8,128)(2,1)}, bf16[2048,1024]{1,0:T(8,128)(2,1)}, u32[]{:S(2)}, u32[]{:S(2)}) collective-permute-start(bf16[2048,1024]{1,0:T(8,128)(2,1)} %wd_own.1), channel_id=1, source_target_pairs={{0,1},{1,0},{2,3},{3,2},{4,5},{5,4},{6,7},{7,6},{8,9},{9,8},{10,11... | collective-permute-start | bytes 12582920 | tf_op jit(solution)/shard_map/ppermute | solution.py:439
  16.6 57.5 %collective-permute-start.1 = (bf16[3,1024,512]{2,1,0:T(8,128)(2,1)}, bf16[3,1024,512]{2,1,0:T(8,128)(2,1)}, u32[]{:S(2)}, u32[]{:S(2)}) collective-permute-start(bf16[3,1024,512]{2,1,0:T(8,128)(2,1)} %bitcast.3.wq_own), channel_id=1, source_target_pairs={{0,1},{1,0},{2,3},{3,2},{4,5},{5,4},{6,7},{7,6},{8,9},{9,8},{10,11... | collective-permute-start | bytes 9437192 | tf_op jit(solution)/shard_map/ppermute | solution.py:439
  16.7 57.4 %collective-permute-start.2 = (bf16[512,1024]{1,0:T(8,128)(2,1)S(1)}, bf16[512,1024]{1,0:T(8,128)(2,1)}, u32[]{:S(2)}, u32[]{:S(2)}) collective-permute-start(bf16[512,1024]{1,0:T(8,128)(2,1)S(1)} %copy-done.2), channel_id=1, source_target_pairs={{0,1},{1,0},{2,3},{3,2},{4,5},{5,4},{6,7},{7,6},{8,9},{9,8},{10,11... | collective-permute-start | bytes 3145736 | tf_op jit(solution)/shard_map/ppermute | solution.py:439
  73.8 3.1 %collective-permute-start = (bf16[14,256,128]{2,1,0:T(8,128)(2,1)}, bf16[14,256,128]{2,1,0:T(8,128)(2,1)}, u32[]{:S(2)}, u32[]{:S(2)}) collective-permute-start(bf16[14,256,128]{2,1,0:T(8,128)(2,1)} %get-tuple-element.20), channel_id=1, source_target_pairs={{0,1},{1,0},{2,3},{3,2},{4,5},{5,4},{6,7},{7,6},{8,9},{9,8},{10,11... | collective-permute-start | bytes 2752520 | tf_op jit(solution)/shard_map/ppermute | solution.py:459
  115.3 14.6 %copy-start = (bf16[896,512]{1,0:T(8,128)(2,1)S(1)}, bf16[896,512]{1,0:T(8,128)(2,1)}, u32[]{:S(2)}) copy-start(bf16[896,512]{1,0:T(8,128)(2,1)} %get-tuple-element.28) | copy-start | bytes 2752516
  115.3 1.6 %collective-permute-start.5 = (bf16[224,256]{1,0:T(8,128)(2,1)}, bf16[224,256]{1,0:T(8,128)(2,1)S(1)}, u32[]{:S(2)}, u32[]{:S(2)}) collective-permute-start(bf16[224,256]{1,0:T(8,128)(2,1)} %get-tuple-element.24), channel_id=1, source_target_pairs={{0,1},{1,0},{2,3},{3,2},{4,5},{5,4},{6,7},{7,6},{8,9},{9,8},{10,11... | collective-permute-start | bytes 344072 | tf_op jit(solution)/shard_map/ppermute | solution.py:463
  116.9 13.0 %collective-permute-start.6 = (bf16[896,512]{1,0:T(8,128)(2,1)}, bf16[896,512]{1,0:T(8,128)(2,1)S(1)}, u32[]{:S(2)}, u32[]{:S(2)}) collective-permute-start(bf16[896,512]{1,0:T(8,128)(2,1)} %get-tuple-element.29), channel_id=1, source_target_pairs={{0,1},{1,0},{2,3},{3,2},{4,5},{5,4},{6,7},{7,6},{8,9},{9,8},{10,11... | collective-permute-start | bytes 2752520 | tf_op jit(solution)/shard_map/ppermute | solution.py:467
  118.1 22.9 %all-to-all-start.1 = ((bf16[64,8,256]{2,1,0:T(8,128)(2,1)}), bf16[64,8,256]{2,1,0:T(8,128)(2,1)S(1)}, u32[]{:S(2)}, u32[]{:S(2)}) async-start(bf16[64,8,256]{2,1,0:T(8,128)(2,1)} %fusion.2), calls=%async_computation.1 | async-start | bytes 524288 | tf_op jit(solution)/shard_map/all_to_all | solution.py:471

commit v10 on v9

--- a/solution.py
+++ b/solution.py
@@ -13,7 +13,7 @@
 SLOTS = 4
 SWAP = [(0, 1), (1, 0)]
 LANES = 128
-FACTS = 8
+FACTS = 16
 
 
 def gelu(x):

time: 143 us -> 145 us (1.014)
  no operation moved by 1% of the time
where the time goes in v10:
time: 145 us; the launch traced here: 144 us
  waiting for transfers between devices  65.6 us (45%)
  Pallas kernels  45.9 us (32%)
  starting transfers between devices  25.8 us (18%)
  other arithmetic  3.49 us (2%)
    all_to_all x1, waiting for transfers between devices, shards(): lax.all_to_all(pack(dest, doc_ids, tokens, devices), 'dp', split_axis=0,...  53.1 us
    pallas_call x1, Pallas kernels, layer(): pl.pallas_call(layer_kernel, out_shape=(jax.ShapeDtypeStruct((tokens, hal...  38.4 us
    all_to_all x1, starting transfers between devices, shards(): lax.all_to_all(sending.reshape(devices, 2 * SLOTS, half // 2), 'dp', spli...  12.2 us
    all_to_all x1, starting transfers between devices, shards(): lax.all_to_all(pack(dest, doc_ids, tokens, devices), 'dp', split_axis=0,...  11.8 us
    all_to_all x1, waiting for transfers between devices, shards(): lax.all_to_all(sending.reshape(devices, 2 * SLOTS, half // 2), 'dp', spli...  9.51 us
    pallas_call x1, Pallas kernels, unpack(): pl.pallas_call(unpack_kernel, out_shape=(jax.ShapeDtypeStruct((rows, body...  3.89 us
    pallas_call x1, Pallas kernels, pack(): pl.pallas_call(pack_kernel, out_shape=jax.ShapeDtypeStruct((slots, body +...  3.55 us
  transfers between devices with their start and end apart: 9, of which 4 were waited for; matrix products, arithmetic and copies ran while one was open for 3% of the time, Pallas kernels for 3%

profile of v10, /device:TPU:0, one launch (start us, length us, event | category | flops | bytes accessed | tf_op | source)
XLA Modules:
  0.0 143.9 jit_solution(13680465700018976907)
XLA Ops:
  0.6 3.6 %pack_rows.1 = bf16[64,272,128]{2,1,0:T(8,128)(2,1)} custom-call(s32[28]{0:T(128)} %dest.1, s32[28,64]{1,0:T(8,128)} %doc_ids.1, bf16[28,64,512]{2,1,0:T(8,128)(2,1)} %tokens.1), custom_call_target="tpu_custom_call" | custom-call | tf_op jit(solution)/shard_map/pack_rows/pallas_call | solution.py:70
  4.2 0.0 copy-start.2
  4.2 0.0 copy-start.1
  4.2 11.8 %all-to-all-start = ((bf16[64,272,128]{2,1,0:T(8,128)(2,1)}), bf16[64,272,128]{2,1,0:T(8,128)(2,1)}, u32[]{:S(2)}, u32[]{:S(2)}) async-start(bf16[64,272,128]{2,1,0:T(8,128)(2,1)} %pack_rows.1), calls=%async_computation | async-start | bytes 8912896 | tf_op jit(solution)/shard_map/all_to_all | solution.py:441
  16.1 0.1 collective-permute-start.3
  16.2 0.5 collective-permute-start.4
  16.7 0.1 collective-permute-start.1
  16.7 0.0 copy-done.2
  16.8 0.4 collective-permute-start.2
  17.2 0.0 copy-done.1
  17.2 0.1 copy.22
  17.3 0.1 eq.48
  17.4 0.2 convert_reduce_fusion
  17.6 0.1 reduce_sum.12
  17.7 0.1 copy.24
  17.8 0.1 mul.17
  17.9 0.1 copy.25
  18.0 0.1 broadcast_add_fusion
  18.1 0.1 reshape.64
  18.2 0.2 fusion
  18.3 53.1 %all-to-all-done.received = bf16[64,272,128]{2,1,0:T(8,128)(2,1)} async-done(((bf16[64,272,128]{2,1,0:T(8,128)(2,1)}), bf16[64,272,128]{2,1,0:T(8,128)(2,1)}, u32[]{:S(2)}, u32[]{:S(2)}) %all-to-all-start) | async-done | bytes 4456480 | tf_op jit(solution)/shard_map/all_to_all | solution.py:441
  71.4 3.9 %unpack_rows.1 = (bf16[14,256,128]{2,1,0:T(8,128)(2,1)}, s32[16,128]{1,0:T(8,128)}) custom-call(s32[1]{0:T(128)} %bitcast.core, bf16[64,272,128]{2,1,0:T(8,128)(2,1)} %all-to-all-done.received), custom_call_target="tpu_custom_call" | custom-call | tf_op jit(solution)/shard_map/unpack_rows/pallas_call | solution.py:139
  75.3 0.3 collective-permute-start
  75.6 0.0 collective-permute-done.2.wo_oth
  75.6 0.0 collective-permute-done.1.wq_oth
  75.6 0.0 collective-permute-done.3.wu_oth
  75.6 0.0 collective-permute-done.4.wd_oth
  75.6 2.8 %collective-permute-done.x_other = bf16[14,256,128]{2,1,0:T(8,128)(2,1)} collective-permute-done((bf16[14,256,128]{2,1,0:T(8,128)(2,1)}, bf16[14,256,128]{2,1,0:T(8,128)(2,1)}, u32[]{:S(2)}, u32[]{:S(2)}) %collective-permute-start) | collective-permute-done | bytes 917536 | tf_op jit(solution)/shard_map/ppermute | solution.py:459
  78.4 38.4 %layer.1 = (bf16[896,512]{1,0:T(8,128)(2,1)}, bf16[896,512]{1,0:T(8,128)(2,1)}, bf16[224,256]{1,0:T(8,128)(2,1)}, bf16[224,256]{1,0:T(8,128)(2,1)}) custom-call(s32[1]{0:T(128)} %bitcast.core, s32[16,128]{1,0:T(8,128)} %get-tuple-element.19.table, bf16[64,272,128]{2,1,0:T(8,128)(2,1)} %all-to-all-done.received, ...), custom_call_target="tpu_custom_call" | custom-call | flops 22548578304 | bytes 29360128 | tf_op jit(solution)/shard_map/layer/pallas_call | solution.py:392
  116.8 0.0 copy-start
  116.8 0.2 collective-permute-start.5
  117.1 1.2 fusion.5
  118.2 0.2 collective-permute-done.5
  118.4 0.2 collective-permute-start.6
  118.6 0.2 fusion.6
  118.9 0.8 fusion.2
  119.6 12.2 %all-to-all-start.1 = ((bf16[64,8,256]{2,1,0:T(8,128)(2,1)}), bf16[64,8,256]{2,1,0:T(8,128)(2,1)S(1)}, u32[]{:S(2)}, u32[]{:S(2)}) async-start(bf16[64,8,256]{2,1,0:T(8,128)(2,1)} %fusion.2), calls=%async_computation.1 | async-start | bytes 524288 | tf_op jit(solution)/shard_map/all_to_all | solution.py:471
  131.8 0.0 collective-permute-done.6
  131.9 0.0 copy-done
  131.9 0.1 broadcast_select_fusion.1
  132.0 1.4 pad_maximum_fusion
  133.4 9.5 %all-to-all-done.1 = bf16[64,8,256]{2,1,0:T(8,128)(2,1)S(1)} async-done(((bf16[64,8,256]{2,1,0:T(8,128)(2,1)}), bf16[64,8,256]{2,1,0:T(8,128)(2,1)S(1)}, u32[]{:S(2)}, u32[]{:S(2)}) %all-to-all-start.1) | async-done | bytes 262176 | tf_op jit(solution)/shard_map/all_to_all | solution.py:471
  142.9 0.1 fusion.4
  143.0 0.1 concatenate.18
  143.1 0.1 concatenate.19
  143.2 0.8 maximum_convert_fusion
  (5 shorter events, 0.0 us)
Async XLA Ops:
  4.2 12.6 %copy-start.2 = (bf16[512,1024]{1,0:T(8,128)(2,1)S(1)}, bf16[512,1024]{1,0:T(8,128)(2,1)}, u32[]{:S(2)}) copy-start(bf16[512,1024]{1,0:T(8,128)(2,1)} %wo_own.1) | copy-start | bytes 3145732
  4.2 13.0 %copy-start.1 = (s32[28,4]{0,1:T(4,128)S(1)}, s32[28,4]{0,1:T(4,128)}, u32[]{:S(2)}) copy-start(s32[28,4]{0,1:T(4,128)} %param.14) | copy-start | bytes 1348
  4.2 67.2 %all-to-all-start = ((bf16[64,272,128]{2,1,0:T(8,128)(2,1)}), bf16[64,272,128]{2,1,0:T(8,128)(2,1)}, u32[]{:S(2)}, u32[]{:S(2)}) async-start(bf16[64,272,128]{2,1,0:T(8,128)(2,1)} %pack_rows.1), calls=%async_computation | async-start | bytes 8912896 | tf_op jit(solution)/shard_map/all_to_all | solution.py:441
  16.1 59.6 %collective-permute-start.3 = (bf16[1024,2048]{1,0:T(8,128)(2,1)}, bf16[1024,2048]{1,0:T(8,128)(2,1)}, u32[]{:S(2)}, u32[]{:S(2)}) collective-permute-start(bf16[1024,2048]{1,0:T(8,128)(2,1)} %wu_own.1), channel_id=1, source_target_pairs={{0,1},{1,0},{2,3},{3,2},{4,5},{5,4},{6,7},{7,6},{8,9},{9,8},{10,11... | collective-permute-start | bytes 12582920 | tf_op jit(solution)/shard_map/ppermute | solution.py:439
  16.2 59.5 %collective-permute-start.4 = (bf16[2048,1024]{1,0:T(8,128)(2,1)}, bf16[2048,1024]{1,0:T(8,128)(2,1)}, u32[]{:S(2)}, u32[]{:S(2)}) collective-permute-start(bf16[2048,1024]{1,0:T(8,128)(2,1)} %wd_own.1), channel_id=1, source_target_pairs={{0,1},{1,0},{2,3},{3,2},{4,5},{5,4},{6,7},{7,6},{8,9},{9,8},{10,11... | collective-permute-start | bytes 12582920 | tf_op jit(solution)/shard_map/ppermute | solution.py:439
  16.7 59.0 %collective-permute-start.1 = (bf16[3,1024,512]{2,1,0:T(8,128)(2,1)}, bf16[3,1024,512]{2,1,0:T(8,128)(2,1)}, u32[]{:S(2)}, u32[]{:S(2)}) collective-permute-start(bf16[3,1024,512]{2,1,0:T(8,128)(2,1)} %bitcast.3.wq_own), channel_id=1, source_target_pairs={{0,1},{1,0},{2,3},{3,2},{4,5},{5,4},{6,7},{7,6},{8,9},{9,8},{10,11... | collective-permute-start | bytes 9437192 | tf_op jit(solution)/shard_map/ppermute | solution.py:439
  16.8 58.8 %collective-permute-start.2 = (bf16[512,1024]{1,0:T(8,128)(2,1)S(1)}, bf16[512,1024]{1,0:T(8,128)(2,1)}, u32[]{:S(2)}, u32[]{:S(2)}) collective-permute-start(bf16[512,1024]{1,0:T(8,128)(2,1)S(1)} %copy-done.2), channel_id=1, source_target_pairs={{0,1},{1,0},{2,3},{3,2},{4,5},{5,4},{6,7},{7,6},{8,9},{9,8},{10,11... | collective-permute-start | bytes 3145736 | tf_op jit(solution)/shard_map/ppermute | solution.py:439
  75.3 3.1 %collective-permute-start = (bf16[14,256,128]{2,1,0:T(8,128)(2,1)}, bf16[14,256,128]{2,1,0:T(8,128)(2,1)}, u32[]{:S(2)}, u32[]{:S(2)}) collective-permute-start(bf16[14,256,128]{2,1,0:T(8,128)(2,1)} %get-tuple-element.20), channel_id=1, source_target_pairs={{0,1},{1,0},{2,3},{3,2},{4,5},{5,4},{6,7},{7,6},{8,9},{9,8},{10,11... | collective-permute-start | bytes 2752520 | tf_op jit(solution)/shard_map/ppermute | solution.py:459
  116.8 15.0 %copy-start = (bf16[896,512]{1,0:T(8,128)(2,1)S(1)}, bf16[896,512]{1,0:T(8,128)(2,1)}, u32[]{:S(2)}) copy-start(bf16[896,512]{1,0:T(8,128)(2,1)} %get-tuple-element.28) | copy-start | bytes 2752516
  116.8 1.6 %collective-permute-start.5 = (bf16[224,256]{1,0:T(8,128)(2,1)}, bf16[224,256]{1,0:T(8,128)(2,1)S(1)}, u32[]{:S(2)}, u32[]{:S(2)}) collective-permute-start(bf16[224,256]{1,0:T(8,128)(2,1)} %get-tuple-element.24), channel_id=1, source_target_pairs={{0,1},{1,0},{2,3},{3,2},{4,5},{5,4},{6,7},{7,6},{8,9},{9,8},{10,11... | collective-permute-start | bytes 344072 | tf_op jit(solution)/shard_map/ppermute | solution.py:463
  118.4 13.4 %collective-permute-start.6 = (bf16[896,512]{1,0:T(8,128)(2,1)}, bf16[896,512]{1,0:T(8,128)(2,1)S(1)}, u32[]{:S(2)}, u32[]{:S(2)}) collective-permute-start(bf16[896,512]{1,0:T(8,128)(2,1)} %get-tuple-element.29), channel_id=1, source_target_pairs={{0,1},{1,0},{2,3},{3,2},{4,5},{5,4},{6,7},{7,6},{8,9},{9,8},{10,11... | collective-permute-start | bytes 2752520 | tf_op jit(solution)/shard_map/ppermute | solution.py:467
  119.6 23.3 %all-to-all-start.1 = ((bf16[64,8,256]{2,1,0:T(8,128)(2,1)}), bf16[64,8,256]{2,1,0:T(8,128)(2,1)S(1)}, u32[]{:S(2)}, u32[]{:S(2)}) async-start(bf16[64,8,256]{2,1,0:T(8,128)(2,1)} %fusion.2), calls=%async_computation.1 | async-start | bytes 524288 | tf_op jit(solution)/shard_map/all_to_all | solution.py:471
